TPU v7x, 32 devices: a whole 2x2x4 slice. The times are simulated.
32 devices in a mesh: lat: 4 (over y, core), lev: 8 (over z, x).
Axes of the slice: x: 2, y: 2, z: 4, core: 2. Of those that a mesh axis runs over, the one named last changes fastest.
Arguments:
- fields: float32 [4, 128, 32, 1152], P(None, 'lev', 'lat'), may hold values from -6 to 6
- winds: float32 [2, 128, 32, 1152], P(None, 'lev', 'lat'), may hold values from -0.3 to 0.3
- remap_weight: bfloat16 [128, 128], replicated, may hold values from -0.5 to 0.5
- w_first: bfloat16 [512, 512], replicated, may hold values from -0.25 to 0.25
- w_second: bfloat16 [512, 512], replicated, may hold values from -0.25 to 0.25
- w_third: bfloat16 [512, 512], replicated, may hold values from -0.25 to 0.25
- lon_counts: int32 [4, 8], P('lat'), may hold values from 1 to 384, 1152 in all within a row
- group_list: int32 [4, 6], replicated, may hold values from 0 to 31, as said below
Outputs:
- columns_out: bfloat16 [4, 128, 32, 3072], P(None, None, 'lat', 'lev')
Inputs may be any that keep to these rules, and one draw needn't show every extreme that they name: `lon_counts`: each row sums to 1152, and its largest entry is exactly 384. `group_list`: row p lists in ascending order the 6 latitude rows whose columns owner p (index p of lat) processes; no row appears twice; every row j with j // 8 equal to 2 appears; at most 2 rows of one owner's list have the same j // 8, and some owner has exactly 2 such rows.
All inputs are finite; a program needn't handle non-finite values.
Results may differ from a plain program's by a relative error of at most 0.0053.
Values may be sent and summed in bfloat16 or wider, within the bound.
No kernel may reach another device: no remote copies, remote signals or barrier semaphores. Data moves between devices by JAX's collectives and lax.ppermute only.
A program may use at most 128 MiB of HBM per device.

v0:
```python
import jax
import jax.numpy as jnp
from jax import lax
from jax.sharding import PartitionSpec as P

DIFFUSION = 0.15


def padded(x, sides, width):
    for axis, dim in sides:
        size, length = (lax.axis_size(axis), x.shape[dim])
        up = [(i, (i + 1) % size) for i in range(size - 1)]
        down = [(j, i) for i, j in up]
        last = lax.slice_in_dim(x, length - width, length, axis=dim)
        first = lax.slice_in_dim(x, 0, width, axis=dim)
        before = lax.ppermute(last, axis, up)
        after = lax.ppermute(first, axis, down)
        x = jnp.concatenate([before, x, after], axis=dim)
    return x


def flux_divergence(values, east_wind, north_wind, first_row, total_rows):
    inner_count = values.shape[-2] - 2
    face_flux = (
        0.25
        * (north_wind[..., :-1, :] + north_wind[..., 1:, :])
        * (values[..., :-1, :] + values[..., 1:, :])
    )
    face_flux = face_flux - DIFFUSION * (values[..., 1:, :] - values[..., :-1, :])
    faces = first_row + jnp.arange(inner_count + 1, dtype=jnp.int32)
    keep_face = ((faces >= 1) & (faces <= total_rows - 1)).astype(jnp.float32)[:, None]
    face_flux = face_flux * keep_face
    inner = values[..., 1:-1, :]
    inner_wind = east_wind[..., 1:-1, :]
    west_values = jnp.roll(inner, 1, axis=-1)
    west_wind = jnp.roll(inner_wind, 1, axis=-1)
    side_flux = 0.25 * (west_wind + inner_wind) * (west_values + inner) - DIFFUSION * (
        inner - west_values
    )
    return -(face_flux[..., 1:, :] - face_flux[..., :-1, :]) - (
        jnp.roll(side_flux, -1, axis=-1) - side_flux
    )


def convect(columns, w_first, w_second, w_third):
    pattern = (((0,), (0,)), ((), ()))
    hidden_one = jax.nn.silu(
        lax.dot_general(w_first, columns, pattern, preferred_element_type=jnp.float32)
    ).astype(jnp.bfloat16)
    hidden_two = jax.nn.silu(
        lax.dot_general(w_second, hidden_one, pattern, preferred_element_type=jnp.float32)
    ).astype(jnp.bfloat16)
    return lax.dot_general(w_third, hidden_two, pattern, preferred_element_type=jnp.float32).astype(
        jnp.bfloat16
    )


def shards(fields, winds, remap_weight, w_first, w_second, w_third, lon_counts, group_list):
    field_count, level_count, lat_rows, lon_total = fields.shape
    band_count = lax.axis_size("lat")
    band_index = lax.axis_index("lat")
    owner_count = lax.axis_size("lev")
    first_row = band_index * lat_rows
    total_rows = band_count * lat_rows
    stacked = jnp.concatenate([fields, winds], axis=0)
    extended = padded(stacked, (("lat", 2),), 1)
    east_wind = extended[field_count]
    north_wind = extended[field_count + 1]
    predicted = fields + flux_divergence(
        extended[:field_count], east_wind, north_wind, first_row, total_rows
    )
    widened = padded(predicted, (("lat", 2),), 1)
    second = flux_divergence(widened, east_wind, north_wind, first_row, total_rows)
    advected = 0.5 * (fields + predicted + second)
    lon_split = lon_counts[0]
    lon_start = jnp.cumsum(lon_split) - lon_split
    slot_width = 128 * ((2 * lon_total // owner_count + 127) // 128)
    offsets = jnp.arange(slot_width, dtype=jnp.int32)
    lon_index = (lon_start[:, None] + offsets[None, :]).reshape(-1)
    in_range = (offsets[None, :] < lon_split[:, None]).reshape(-1)
    selector = (
        (jnp.arange(lon_total, dtype=jnp.int32)[:, None] == lon_index[None, :]) & in_range[None, :]
    ).astype(jnp.bfloat16)
    packed = jnp.dot(
        advected.astype(jnp.bfloat16).reshape(-1, lon_total),
        selector,
        preferred_element_type=jnp.float32,
    )
    packed = packed.astype(jnp.bfloat16).reshape(
        field_count, level_count, lat_rows, owner_count * slot_width
    )
    block = lax.all_to_all(packed, "lev", split_axis=3, concat_axis=1, tiled=True)
    count_f, count_m, count_r, count_c = block.shape
    mixed = jnp.stack(
        [
            jnp.dot(
                remap_weight,
                block[index].reshape(count_m, count_r * count_c),
                preferred_element_type=jnp.float32,
            )
            for index in range(count_f)
        ]
    )
    remapped = block.astype(jnp.float32) + mixed.reshape(count_f, count_m, count_r, count_c)
    features = remapped.astype(jnp.bfloat16).reshape(-1, lat_rows, slot_width)
    feature_count = features.shape[0]
    local_hits = jnp.any(
        group_list[:, :, None]
        == (first_row + jnp.arange(lat_rows, dtype=jnp.int32))[None, None, :],
        axis=(0, 1),
    )
    tendency = convect(
        features.reshape(feature_count, lat_rows * slot_width), w_first, w_second, w_third
    ).reshape(feature_count, lat_rows, slot_width)
    tendency = jnp.where(local_hits[None, :, None], tendency, jnp.zeros_like(tendency))
    columns_out = remapped + tendency.reshape(field_count, -1, lat_rows, slot_width).astype(
        jnp.float32
    )
    return columns_out.astype(jnp.bfloat16)


def solution(mesh):
    in_specs = (
        P(None, "lev", "lat", None),
        P(None, "lev", "lat", None),
        P(),
        P(),
        P(),
        P(),
        P("lat", None),
        P(),
    )
    out_specs = P(None, None, "lat", "lev")
    return jax.shard_map(shards, mesh=mesh, in_specs=in_specs, out_specs=out_specs, check_vma=False)
```

profile of v0, /device:TPU:0, one launch (start us, length us, event | category | flops | bytes accessed | tf_op | source)
XLA Modules:
  0.0 292.0 jit_solution(14317542531573282640)
XLA Ops:
  0.0 1.9 constant_dynamic-update-slice_fusion.1
  5.3 3.1 %collective-permute-start = (f32[6,16,1,1152]{3,1,2,0:T(8,128)}, f32[6,16,1,1152]{3,1,2,0:T(8,128)}, u32[]{:S(2)}, u32[]{:S(2)}) collective-permute-start(f32[6,16,1,1152]{3,1,2,0:T(8,128)} %copy.64), channel_id=1, source_target_pairs={{0,8},{8,16},{16,24},{1,9},{9,17},{17,25},{2,10},{10,18},{18,26},{... | collective-permute-start | bytes 1327112 | tf_op jit(solution)/shard_map/ppermute | solution.py:16
  12.5 2.1 collective-permute-done.1
  23.8 8.3 %collective-permute-start.2 = (f32[4,16,1,1152]{3,1,2,0:T(8,128)S(1)}, f32[4,16,1,1152]{3,1,2,0:T(8,128)S(1)}, u32[]{:S(2)}, u32[]{:S(2)}) collective-permute-start(f32[4,16,1,1152]{3,1,2,0:T(8,128)S(1)} %copy.70), channel_id=1, source_target_pairs={{0,8},{8,16},{16,24},{1,9},{9,17},{17,25},{2,10},{10,18},{18,26},{... | collective-permute-start | bytes 884744 | tf_op jit(solution)/shard_map/ppermute | solution.py:16
  38.6 5.8 %fusion.19 = bf16[512,3072]{1,0:T(8,128)(2,1)} fusion(bf16[512,1152]{1,0:T(8,128)(2,1)S(1)} %bitcast.116, s32[3072]{0:T(1024)S(1)} %add.103, pred[3072]{0:T(1024)(128)(4,1)S(1)} %lt.20), kind=kOutput, calls=%fused_computation.30 | convolution fusion | flops 3632529408 | bytes 4340736 | tf_op jit(solution)/shard_map/dot_general | solution.py:84
  44.4 22.6 %copy.74 = bf16[4,16,8,3072]{1,2,0,3:T(8,128)(2,1)} copy(bf16[4,16,8,3072]{3,2,1,0:T(8,128)(2,1)} %bitcast.107) | data formatting | bytes 6291456 | tf_op jit(solution)/shard_map/reshape | solution.py:89
  66.9 28.7 %reshape.118 = bf16[8,2,98304]{2,1,0:T(2,128)(2,1)} reshape(bf16[3072,4,8,16]{3,2,1,0:T(8,128)(2,1)} %bitcast.93) | data formatting | bytes 6291456
  95.6 6.0 %all-to-all-start = ((bf16[8,2,98304]{2,1,0:T(2,128)(2,1)}), bf16[8,2,98304]{2,1,0:T(2,128)(2,1)}, u32[]{:S(2)}, u32[]{:S(2)}) async-start(bf16[8,2,98304]{2,1,0:T(2,128)(2,1)} %reshape.118), calls=%async_computation | async-start | bytes 6291456 | tf_op jit(solution)/shard_map/all_to_all | solution.py:92
  101.7 69.1 %all-to-all-done = bf16[8,2,98304]{2,1,0:T(2,128)(2,1)} async-done(((bf16[8,2,98304]{2,1,0:T(2,128)(2,1)}), bf16[8,2,98304]{2,1,0:T(2,128)(2,1)}, u32[]{:S(2)}, u32[]{:S(2)}) %all-to-all-start) | async-done | bytes 3145760 | tf_op jit(solution)/shard_map/all_to_all | solution.py:92
  170.9 20.2 %reshape.119 = bf16[3072,4,8,16]{3,2,1,0:T(8,128)(2,1)} reshape(bf16[8,2,98304]{2,1,0:T(2,128)(2,1)} %all-to-all-done) | data formatting | bytes 6291456
  191.0 25.1 %copy.75 = bf16[4,16,8,8,384]{4,2,1,3,0:T(8,128)(2,1)} copy(bf16[4,16,8,8,384]{1,2,0,4,3:T(8,128)(2,1)} %bitcast.94) | data formatting | bytes 6291456 | tf_op jit(solution)/shard_map/all_to_all | solution.py:92
  216.1 5.5 %bitcast_convert_fusion = f32[4,8,16,8,384]{4,3,2,1,0:T(8,128)} fusion(bf16[4,16,8,8,384]{4,2,1,3,0:T(8,128)(2,1)} %copy.75), kind=kLoop, calls=%fused_computation.67 | loop fusion | flops 1572864 | bytes 9437184 | tf_op jit(solution)/shard_map/convert_element_type | solution.py:104
  225.6 2.0 copy.78
  227.6 2.7 fusion.43
  230.3 3.1 %copy.76 = f32[1,128,8,384]{3,2,1,0:T(8,128)} copy(f32[1,128,8,384]{1,3,2,0:T(8,128)} %bitcast.104) | data formatting | bytes 3145728 | tf_op jit(solution)/shard_map/stack | solution.py:94
  236.2 3.2 %copy.77 = f32[1,128,8,384]{3,2,1,0:T(8,128)} copy(f32[1,128,8,384]{1,3,2,0:T(8,128)} %bitcast.105) | data formatting | bytes 3145728 | tf_op jit(solution)/shard_map/stack | solution.py:94
  241.1 3.1 %copy.79 = f32[1,128,8,384]{3,2,1,0:T(8,128)} copy(f32[1,128,8,384]{1,3,2,0:T(8,128)} %bitcast.106) | data formatting | bytes 3145728 | tf_op jit(solution)/shard_map/stack | solution.py:94
  244.2 7.0 %copy.86 = f32[64,8,8,384]{3,1,2,0:T(8,128)} copy(f32[64,8,8,384]{3,2,1,0:T(8,128)} %bitcast.97) | data formatting | bytes 12582912
  251.9 4.0 %copy.87 = f32[64,8,8,384]{3,1,2,0:T(8,128)} copy(f32[64,8,8,384]{3,2,1,0:T(8,128)S(1)} %bitcast.100) | data formatting | bytes 12582912
  255.9 11.6 %fusion.25 = f32[3072,512]{1,0:T(8,128)} fusion(bf16[512,512]{1,0:T(8,128)(2,1)S(1)} %copy-done, bf16[512,512]{1,0:T(8,128)(2,1)S(1)} %copy-done.12, f32[512,3072]{1,0:T(8,128)} %bitcast.101, f32[512,3072]{1,0:T(8,128)} %bitcast.102), kind=kOutput, calls=%fused_computation.34 | convolution fusion | flops 3232235520 | bytes 19922944 | tf_op jit(solution)/shard_map/dot_general | solution.py:51
  267.5 6.4 %fusion.22 = bf16[512,3072]{0,1:T(8,128)(2,1)} fusion(bf16[512,512]{1,0:T(8,128)(2,1)S(1)} %copy-done.13, f32[3072,512]{1,0:T(8,128)} %fusion.25), kind=kOutput, calls=%fused_computation.32 | convolution fusion | flops 1620049920 | bytes 9961472 | tf_op jit(solution)/shard_map/dot_general | solution.py:53
  273.9 5.5 %reshape.115 = bf16[4,128,8,384]{1,0,3,2:T(4,128)(2,1)} reshape(bf16[512,3072]{0,1:T(8,128)(2,1)} %fusion.22) | data formatting | bytes 6291456 | tf_op jit(solution)/shard_map/reshape | solution.py:114
  279.4 5.3 %copy.81 = bf16[4,128,8,384]{3,2,1,0:T(8,128)(2,1)} copy(bf16[4,128,8,384]{1,0,3,2:T(4,128)(2,1)} %reshape.115) | data formatting | bytes 6291456 | tf_op jit(solution)/shard_map/reshape | solution.py:114
  284.7 7.3 %add_convert_fusion = bf16[4,128,8,384]{3,2,1,0:T(8,128)(2,1)} fusion(f32[4,128,8,384]{3,2,1,0:T(8,128)} %bitcast.98, bf16[4,128,8,384]{3,2,1,0:T(8,128)(2,1)} %copy.81, pred[8]{0:T(512)(128)(4,1)S(1)} %compare_reduce_fusion, f32[1,128,8,384]{3,2,1,0:T(8,128)} %copy.79, f32[1,128,8,384]{3,2,1,0:T(8,128)S(1)} %copy.78, f32[1,128,8,384]{3,2,1,0:T(8,128)} %copy.77, ...), kind=kLoop, calls=%fused_computation.16 | loop fusion | flops 12582912 | bytes 18874376 | tf_op jit(solution)/shard_map/convert_element_type | solution.py:119
  (80 shorter events, 32.3 us)
Async XLA Ops:
  0.0 255.9 %copy-start = (bf16[512,512]{1,0:T(8,128)(2,1)S(1)}, bf16[512,512]{1,0:T(8,128)(2,1)}, u32[]{:S(2)}) copy-start(bf16[512,512]{1,0:T(8,128)(2,1)} %param.12) | copy-start | bytes 1572868
  0.0 2.0 copy-start.8
  2.0 8.4 %copy-start.11 = (s32[1,8]{1,0:T(1,128)S(1)}, s32[1,8]{1,0:T(1,128)}, u32[]{:S(2)}) copy-start(s32[1,8]{1,0:T(1,128)} %param.14) | copy-start | bytes 100
  2.0 8.7 %copy-start.1 = (f32[4,16,8,1152]{3,2,1,0:T(8,128)S(1)}, f32[4,16,8,1152]{3,2,1,0:T(8,128)}, u32[]{:S(2)}) copy-start(f32[4,16,8,1152]{3,2,1,0:T(8,128)} %param.8) | copy-start | bytes 7077892
  2.1 1.8 copy-start.2
  5.3 5.7 %collective-permute-start = (f32[6,16,1,1152]{3,1,2,0:T(8,128)}, f32[6,16,1,1152]{3,1,2,0:T(8,128)}, u32[]{:S(2)}, u32[]{:S(2)}) collective-permute-start(f32[6,16,1,1152]{3,1,2,0:T(8,128)} %copy.64), channel_id=1, source_target_pairs={{0,8},{8,16},{16,24},{1,9},{9,17},{17,25},{2,10},{10,18},{18,26},{... | collective-permute-start | bytes 1327112 | tf_op jit(solution)/shard_map/ppermute | solution.py:16
  9.2 5.4 %collective-permute-start.1 = (f32[6,16,1,1152]{3,1,2,0:T(8,128)}, f32[6,16,1,1152]{3,1,2,0:T(8,128)}, u32[]{:S(2)}, u32[]{:S(2)}) collective-permute-start(f32[6,16,1,1152]{3,1,2,0:T(8,128)} %copy.65), channel_id=1, source_target_pairs={{8,0},{16,8},{24,16},{9,1},{17,9},{25,17},{10,2},{18,10},{26,18},{... | collective-permute-start | bytes 1327112 | tf_op jit(solution)/shard_map/ppermute | solution.py:17
  18.8 2.0 copy-start.3
  23.8 11.2 %collective-permute-start.2 = (f32[4,16,1,1152]{3,1,2,0:T(8,128)S(1)}, f32[4,16,1,1152]{3,1,2,0:T(8,128)S(1)}, u32[]{:S(2)}, u32[]{:S(2)}) collective-permute-start(f32[4,16,1,1152]{3,1,2,0:T(8,128)S(1)} %copy.70), channel_id=1, source_target_pairs={{0,8},{8,16},{16,24},{1,9},{9,17},{17,25},{2,10},{10,18},{18,26},{... | collective-permute-start | bytes 884744 | tf_op jit(solution)/shard_map/ppermute | solution.py:16
  32.2 3.5 %collective-permute-start.3 = (f32[4,16,1,1152]{3,1,2,0:T(8,128)S(1)}, f32[4,16,1,1152]{3,1,2,0:T(8,128)S(1)}, u32[]{:S(2)}, u32[]{:S(2)}) collective-permute-start(f32[4,16,1,1152]{3,1,2,0:T(8,128)S(1)} %copy.72), channel_id=1, source_target_pairs={{8,0},{16,8},{24,16},{9,1},{17,9},{25,17},{10,2},{18,10},{26,18},{... | collective-permute-start | bytes 884744 | tf_op jit(solution)/shard_map/ppermute | solution.py:17
  95.6 6.0 %copy-start.10 = (s32[4,6]{1,0:T(4,128)S(1)}, s32[4,6]{1,0:T(4,128)}, u32[]{:S(2)}) copy-start(s32[4,6]{1,0:T(4,128)} %param.15) | copy-start | bytes 292
  95.6 75.3 %all-to-all-start = ((bf16[8,2,98304]{2,1,0:T(2,128)(2,1)}), bf16[8,2,98304]{2,1,0:T(2,128)(2,1)}, u32[]{:S(2)}, u32[]{:S(2)}) async-start(bf16[8,2,98304]{2,1,0:T(2,128)(2,1)} %reshape.118), calls=%async_computation | async-start | bytes 6291456 | tf_op jit(solution)/shard_map/all_to_all | solution.py:92
  216.1 5.5 %copy-start.4 = (bf16[4,16,8,8,384]{4,2,1,3,0:T(8,128)(2,1)S(1)}, bf16[4,16,8,8,384]{4,2,1,3,0:T(8,128)(2,1)}, u32[]{:S(2)}) copy-start(bf16[4,16,8,8,384]{4,2,1,3,0:T(8,128)(2,1)} %copy.75) | copy-start | bytes 9437188
  222.9 1.2 copy-start.9
  244.2 7.0 %copy-start.5 = (f32[1,128,8,384]{3,2,1,0:T(8,128)S(1)}, f32[1,128,8,384]{3,2,1,0:T(8,128)}, u32[]{:S(2)}) copy-start(f32[1,128,8,384]{3,2,1,0:T(8,128)} %copy.76) | copy-start | bytes 4718596
  244.2 7.0 %copy-start.6 = (f32[1,128,8,384]{3,2,1,0:T(8,128)S(1)}, f32[1,128,8,384]{3,2,1,0:T(8,128)}, u32[]{:S(2)}) copy-start(f32[1,128,8,384]{3,2,1,0:T(8,128)} %copy.77) | copy-start | bytes 4718596
  244.2 7.0 %copy-start.7 = (f32[1,128,8,384]{3,2,1,0:T(8,128)S(1)}, f32[1,128,8,384]{3,2,1,0:T(8,128)}, u32[]{:S(2)}) copy-start(f32[1,128,8,384]{3,2,1,0:T(8,128)} %copy.79) | copy-start | bytes 4718596
  251.9 4.0 %copy-start.12 = (bf16[512,512]{1,0:T(8,128)(2,1)S(1)}, bf16[512,512]{1,0:T(8,128)(2,1)}, u32[]{:S(2)}) copy-start(bf16[512,512]{1,0:T(8,128)(2,1)} %param.11) | copy-start | bytes 1572868
  255.9 11.7 %copy-start.13 = (bf16[512,512]{1,0:T(8,128)(2,1)S(1)}, bf16[512,512]{1,0:T(8,128)(2,1)}, u32[]{:S(2)}) copy-start(bf16[512,512]{1,0:T(8,128)(2,1)} %param.13) | copy-start | bytes 1572868
where the time goes:
time: 297 us; the launch traced here: 292 us
  local copies, waits for them, and re-layouts  146 us (49%)
  waiting for transfers between devices  71.5 us (24%)
  matrix products  31.1 us (10%)
  other arithmetic  22.5 us (8%)
  starting transfers between devices  20.2 us (7%)
    all_to_all x1, waiting for transfers between devices, shards(): lax.all_to_all(packed, 'lev', split_axis=3, concat_axis=1, tiled=True)  69.1 us
    unnamed x38, local copies, waits for them, and re-layouts  67.4 us
    all_to_all x1, local copies, waits for them, and re-layouts, shards(): lax.all_to_all(packed, 'lev', split_axis=3, concat_axis=1, tiled=True)  25.1 us
    reshape x1, local copies, waits for them, and re-layouts, shards(): packed.astype(jnp.bfloat16)  22.6 us
    dot_general x1, matrix products, convect(): lax.dot_general(w_second, hidden_one, pattern, preferred_element_type=jnp...  11.6 us
    ppermute x2, starting transfers between devices, padded(): before = lax.ppermute(last, axis, up)  11.5 us
    another operation x4, local copies, waits for them, and re-layouts, shards(): jnp.stack([jnp.dot(remap_weight, block[index].reshape(count_m, count_r *...  11.4 us
    reshape x2, local copies, waits for them, and re-layouts, shards(): tendency = convect(features.reshape(feature_count, lat_rows * slot_width)...  10.8 us
  transfers between devices with their start and end apart: 5, of which 3 were waited for; matrix products, arithmetic and copies ran while one was open for 2% of the time, Pallas kernels for 0%

commit v1 on v0

v1 whole, which is shorter than its diff:
```python
import functools

import jax
import jax.numpy as jnp
from jax import lax
from jax.experimental import pallas as pl
from jax.experimental.pallas import tpu as pltpu
from jax.sharding import PartitionSpec as P

DIFFUSION = 0.15
LANES = 128
HALO = 2
VMEM_BYTES = 48 * 1024 * 1024


def face_weights(wind, axis):
    half = 0.25 * (pltpu.roll(wind, 1, axis) + wind)
    return half + DIFFUSION, half - DIFFUSION


def divergence(values, north, east):
    rows, lons = values.shape
    face = north[0] * pltpu.roll(values, 1, 0) + north[1] * values
    side = east[0] * pltpu.roll(values, 1, 1) + east[1] * values
    return (face - pltpu.roll(face, rows - 1, 0)) + (side - pltpu.roll(side, lons - 1, 1))


def heun(values, north, east):
    predicted = values + divergence(values, north, east)
    return 0.5 * (values + predicted + divergence(predicted, north, east))


def keep_rows(ref, place, values):
    rows, lons = values.shape
    for tile in range(lons // LANES):
        ref[tile, pl.ds(pl.multiple_of(place, rows), rows), :] = values[
            :, tile * LANES : (tile + 1) * LANES
        ]


def clear_tail(ref, tiles):
    for tile in range(tiles, ref.shape[0]):
        ref[tile] = jnp.zeros(ref.shape[1:], ref.dtype)


def slot_starts(counts_ref, owners):
    starts = []
    total = jnp.int32(0)
    for owner in range(owners):
        starts.append(total)
        total = total + counts_ref[0, owner]
    return starts


def pack_rows(starts, sources, out_ref, fields, levels, rows):
    blocks = out_ref.shape[1]
    lane = lax.broadcasted_iota(jnp.int32, (levels, LANES), 1)

    def one_field(field, carry):
        base = field * (levels * rows)
        for owner, start in enumerate(starts):
            tile = start // LANES
            inside = start - tile * LANES
            shift = (LANES - inside) % LANES
            keep = lane < LANES - inside
            for index, (ref, row) in enumerate(sources):
                turned = []
                for j in range(blocks + 1):
                    piece = ref[tile + j, pl.ds(base + row, levels, stride=rows), :]
                    turned.append(pltpu.roll(piece, shift, 1))
                for j in range(blocks):
                    joined = jnp.where(keep, turned[j], turned[j + 1])
                    out_ref[owner, j, index, field] = joined.astype(jnp.bfloat16)
        return carry

    lax.fori_loop(0, fields, one_field, 0)


def inner_kernel(counts_ref, fields_ref, winds_ref, out_ref, first_ref, last_ref, advected_ref):
    step = pl.program_id(0)
    fields, block, rows, lons = fields_ref.shape
    total_levels = advected_ref.shape[1] // (fields * rows)

    @pl.when(step == 0)
    def _():
        clear_tail(advected_ref, lons // LANES)

    def one_level(level, carry):
        east = face_weights(winds_ref[0, level], 1)
        north = face_weights(winds_ref[1, level], 0)
        for field in range(fields):
            values = fields_ref[field, level]
            place = (field * total_levels + step * block + level) * rows
            keep_rows(advected_ref, place, heun(values, north, east))
        return carry

    lax.fori_loop(0, block, one_level, 0)
    for field in range(fields):
        first_ref[field] = fields_ref[field, :, :HALO, :]
        last_ref[field] = fields_ref[field, :, rows - HALO :, :]
    for wind in range(2):
        first_ref[fields + wind] = winds_ref[wind, :, :HALO, :]
        last_ref[fields + wind] = winds_ref[wind, :, rows - HALO :, :]

    @pl.when(step == pl.num_programs(0) - 1)
    def _():
        starts = slot_starts(counts_ref, out_ref.shape[0])
        sources = [(advected_ref, row) for row in range(HALO, rows - HALO)]
        pack_rows(starts, sources, out_ref, fields, total_levels, rows)


def edge_kernel(
    counts_ref, band_ref, fields_ref, winds_ref, before_ref, after_ref, out_ref, top_ref, bottom_ref
):
    step = pl.program_id(0)
    fields, block, rows, lons = fields_ref.shape
    total_levels = top_ref.shape[1] // (fields * rows)
    row = lax.broadcasted_iota(jnp.int32, (rows, lons), 0)

    @pl.when(step == 0)
    def _():
        clear_tail(top_ref, lons // LANES)
        clear_tail(bottom_ref, lons // LANES)

    def upper(own, halo):
        padded = jnp.concatenate([halo, jnp.zeros((rows - HALO, lons), halo.dtype)], axis=0)
        return jnp.where(row < HALO, padded, pltpu.roll(own, HALO, 0))

    def lower(own, halo):
        padded = jnp.concatenate([jnp.zeros((rows - HALO, lons), halo.dtype), halo], axis=0)
        return jnp.where(row >= rows - HALO, padded, pltpu.roll(own, rows - HALO, 0))

    for extend, halo_ref, kept_ref, wall, flag in (
        (upper, before_ref, top_ref, HALO, band_ref[0]),
        (lower, after_ref, bottom_ref, rows - HALO, band_ref[1]),
    ):
        open_face = jnp.logical_not((row == wall) & (flag == 1)).astype(jnp.float32)

        def one_level(level, carry):
            east = face_weights(extend(winds_ref[0, level], halo_ref[fields, level]), 1)
            north = face_weights(extend(winds_ref[1, level], halo_ref[fields + 1, level]), 0)
            north = (north[0] * open_face, north[1] * open_face)
            for field in range(fields):
                values = extend(fields_ref[field, level], halo_ref[field, level])
                place = (field * total_levels + step * block + level) * rows
                keep_rows(kept_ref, place, heun(values, north, east))
            return carry

        lax.fori_loop(0, block, one_level, 0)

    @pl.when(step == pl.num_programs(0) - 1)
    def _():
        starts = slot_starts(counts_ref, out_ref.shape[0])
        sources = [(top_ref, HALO + i) for i in range(HALO)]
        sources += [(bottom_ref, rows - 2 * HALO + i) for i in range(HALO)]
        pack_rows(starts, sources, out_ref, fields, total_levels, rows)


def silu(x):
    half = 0.5 * x
    return half + half * jnp.tanh(half)


def dot(a, b):
    return jnp.dot(a, b, preferred_element_type=jnp.float32)


def column_update(block_ref, remap_ref, first_ref, second_ref, third_ref):
    sources, _, rows, fields = block_ref.shape[:4]
    remapped = []
    for field in range(fields):
        by_row = [
            jnp.concatenate([block_ref[source, 0, row, field] for source in range(sources)], axis=0)
            for row in range(rows)
        ]
        values = jnp.concatenate(by_row, axis=1)
        remapped.append(values.astype(jnp.float32) + dot(remap_ref[...], values))
    remapped = jnp.concatenate(remapped, axis=0)
    hidden = silu(dot(first_ref[...], remapped.astype(jnp.bfloat16))).astype(jnp.bfloat16)
    hidden = silu(dot(second_ref[...], hidden)).astype(jnp.bfloat16)
    tendency = dot(third_ref[...], hidden).astype(jnp.bfloat16).astype(jnp.float32)
    return remapped, tendency


def finished_row(remapped, tendency, listed, index, live):
    lanes = slice(index * LANES, (index + 1) * LANES)
    updated = remapped[:, lanes] + jnp.where(listed == 1, tendency[:, lanes], 0.0)
    return jnp.where(live, updated, 0.0)


def live_lanes(width_ref, features):
    lane = lax.broadcasted_iota(jnp.int32, (features, LANES), 1)
    return lane + pl.program_id(0) * LANES < width_ref[0]


def half_kernel(
    row_list, listed_ref, width_ref, block_ref, remap_ref, first_ref, second_ref, third_ref, out_ref
):
    remapped, tendency = column_update(block_ref, remap_ref, first_ref, second_ref, third_ref)
    live = live_lanes(width_ref, remapped.shape[0])
    for index, row in enumerate(row_list):
        out_ref[index] = finished_row(remapped, tendency, listed_ref[row], index, live).astype(
            jnp.bfloat16
        )


def last_kernel(
    row_list,
    done_list,
    listed_ref,
    width_ref,
    block_ref,
    done_ref,
    remap_ref,
    first_ref,
    second_ref,
    third_ref,
    out_ref,
    tiles_ref,
):
    features, rows, _ = out_ref.shape
    remapped, tendency = column_update(block_ref, remap_ref, first_ref, second_ref, third_ref)
    live = live_lanes(width_ref, features)
    for index, row in enumerate(done_list):
        tiles_ref[pl.ds(row, features, stride=rows), :] = done_ref[index].astype(jnp.float32)
    for index, row in enumerate(row_list):
        tiles_ref[pl.ds(row, features, stride=rows), :] = finished_row(
            remapped, tendency, listed_ref[row], index, live
        )
    out_ref[...] = tiles_ref[...].reshape(features, rows, LANES).astype(jnp.bfloat16)


def shards(fields, winds, remap_weight, w_first, w_second, w_third, lon_counts, group_list):
    field_count, level_count, lat_rows, lon_total = fields.shape
    band_count = lax.axis_size("lat")
    band_index = lax.axis_index("lat")
    owner_count = lax.axis_size("lev")
    first_row = band_index * lat_rows
    all_levels = level_count * owner_count
    features = field_count * all_levels
    blocks = (2 * lon_total // owner_count + LANES - 1) // LANES
    slot_width = blocks * LANES
    inner_rows = tuple(range(HALO, lat_rows - HALO))
    edge_rows = tuple(range(HALO)) + tuple(range(lat_rows - HALO, lat_rows))
    level_block = 4
    steps = level_count // level_block
    stacked = field_count + 2
    padded_lons = lon_total + slot_width
    smem = pl.BlockSpec(memory_space=pltpu.SMEM)
    params = pltpu.CompilerParams(
        dimension_semantics=("arbitrary",), vmem_limit_bytes=VMEM_BYTES
    )

    fields_spec = pl.BlockSpec((field_count, level_block, lat_rows, lon_total), lambda i: (0, i, 0, 0))
    winds_spec = pl.BlockSpec((2, level_block, lat_rows, lon_total), lambda i: (0, i, 0, 0))
    halo_spec = pl.BlockSpec((stacked, level_block, HALO, lon_total), lambda i: (0, i, 0, 0))
    halo_shape = jax.ShapeDtypeStruct((stacked, level_count, HALO, lon_total), jnp.float32)
    half_shape = (owner_count, blocks, len(inner_rows), field_count, level_count, LANES)
    half_spec = pl.BlockSpec(half_shape, lambda i: (0,) * 6)
    kept = pltpu.VMEM(
        (padded_lons // LANES, field_count * level_count * lat_rows, LANES), jnp.float32
    )
    grid_values = field_count * level_count * lat_rows * lon_total

    inner, first, last = pl.pallas_call(
        inner_kernel,
        grid=(steps,),
        in_specs=[smem, fields_spec, winds_spec],
        out_specs=[half_spec, halo_spec, halo_spec],
        out_shape=[jax.ShapeDtypeStruct(half_shape, jnp.bfloat16), halo_shape, halo_shape],
        scratch_shapes=[kept],
        compiler_params=params,
        cost_estimate=pl.CostEstimate(
            flops=40 * grid_values, bytes_accessed=8 * grid_values, transcendentals=0
        ),
        name="inner_rows",
    )(lon_counts, fields, winds)

    up = [(i, i + 1) for i in range(band_count - 1)]
    down = [(j, i) for i, j in up]
    inner_block = lax.all_to_all(inner, "lev", split_axis=0, concat_axis=0, tiled=True)
    before = lax.ppermute(last, "lat", up)
    after = lax.ppermute(first, "lat", down)

    walls = jnp.stack([band_index == 0, band_index == band_count - 1]).astype(jnp.int32)
    edge = pl.pallas_call(
        edge_kernel,
        grid=(steps,),
        in_specs=[smem, smem, fields_spec, winds_spec, halo_spec, halo_spec],
        out_specs=half_spec,
        out_shape=jax.ShapeDtypeStruct(half_shape, jnp.bfloat16),
        scratch_shapes=[kept, kept],
        compiler_params=params,
        cost_estimate=pl.CostEstimate(
            flops=80 * grid_values, bytes_accessed=10 * grid_values, transcendentals=0
        ),
        name="edge_rows",
    )(lon_counts, walls, fields, winds, before, after)
    edge_block = lax.all_to_all(edge, "lev", split_axis=0, concat_axis=0, tiled=True)

    listed = jnp.any(
        group_list[:, :, None] == (first_row + jnp.arange(lat_rows, dtype=jnp.int32))[None, None, :],
        axis=(0, 1),
    ).astype(jnp.int32)
    width = lax.dynamic_slice_in_dim(lon_counts[0], lax.axis_index("lev"), 1)
    weights = (remap_weight, w_first.T, w_second.T, w_third.T)

    def by_level(block):
        if level_count % 16 == 0:
            return block
        return block.transpose(1, 2, 3, 0, 4, 5).reshape(
            1, blocks, len(inner_rows), field_count, all_levels, LANES
        )

    def whole(shape):
        return pl.BlockSpec(shape, lambda i: (0,) * len(shape))

    inner_block, edge_block = by_level(inner_block), by_level(edge_block)
    sources, piece = inner_block.shape[0], inner_block.shape[4]
    block_spec = pl.BlockSpec(
        (sources, 1, len(inner_rows), field_count, piece, LANES), lambda i: (0, i, 0, 0, 0, 0)
    )
    weight_specs = [whole(w.shape) for w in weights]
    done_spec = pl.BlockSpec((len(inner_rows), features, LANES), lambda i: (0, 0, i))
    cost = pl.CostEstimate(
        flops=2 * features * len(inner_rows) * slot_width * (3 * w_first.shape[1] + all_levels),
        bytes_accessed=4 * features * len(inner_rows) * slot_width,
        transcendentals=2 * w_first.shape[1] * len(inner_rows) * slot_width,
    )
    done = pl.pallas_call(
        functools.partial(half_kernel, inner_rows),
        grid=(blocks,),
        in_specs=[smem, smem, block_spec] + weight_specs,
        out_specs=done_spec,
        out_shape=jax.ShapeDtypeStruct((len(inner_rows), features, slot_width), jnp.bfloat16),
        compiler_params=params,
        cost_estimate=cost,
        name="inner_columns",
    )(listed, width, inner_block, *weights)
    out = pl.pallas_call(
        functools.partial(last_kernel, edge_rows, inner_rows),
        grid=(blocks,),
        in_specs=[smem, smem, block_spec, done_spec] + weight_specs,
        out_specs=pl.BlockSpec((features, lat_rows, LANES), lambda i: (0, 0, i)),
        out_shape=jax.ShapeDtypeStruct((features, lat_rows, slot_width), jnp.bfloat16),
        scratch_shapes=[pltpu.VMEM((features * lat_rows, LANES), jnp.float32)],
        compiler_params=params,
        cost_estimate=cost,
        name="edge_columns",
    )(listed, width, edge_block, done, *weights)
    return out.reshape(field_count, all_levels, lat_rows, slot_width)


def solution(mesh):
    in_specs = (
        P(None, "lev", "lat", None),
        P(None, "lev", "lat", None),
        P(),
        P(),
        P(),
        P(),
        P("lat", None),
        P(),
    )
    out_specs = P(None, None, "lat", "lev")
    return jax.shard_map(shards, mesh=mesh, in_specs=in_specs, out_specs=out_specs, check_vma=False)
```

time: 297 us -> 109 us (0.37); the launches traced: 292 us -> 109 us
  local copies, waits for them, and re-layouts: 146 us -> 9.94 us
  Pallas kernels: 0 us -> 39.2 us
  matrix products: 31.1 us -> 0 us
  waiting for transfers between devices: 71.5 us -> 44 us
  other arithmetic: 22.5 us -> 0.18 us
  starting transfers between devices: 20.2 us -> 15.3 us
    unnamed x38 -> x30, local copies, waits for them, and re-layouts: 67.4 us -> 9.27 us
    pallas_call x0 -> x4, Pallas kernels: none -> 39.2 us  [the longest x1 16.6 us: shards(): pl.pallas_call(edge_kernel, grid=(steps,), in_specs=[smem, smem, fields_s...]
    reshape x3 -> x0, local copies, waits for them, and re-layouts: 33.4 us -> none  [the longest x1 22.6 us: shards(): packed.astype(jnp.bfloat16)]
    dot_general x7 -> x0, matrix products: 31.1 us -> none  [the longest x1 11.6 us: convect(): lax.dot_general(w_second, hidden_one, pattern, preferred_element_type=jnp...]
    all_to_all x1 -> x2, waiting for transfers between devices: 69.1 us -> 40 us  [the longest x1 27.3 us: shards(): lax.all_to_all(edge, 'lev', split_axis=0, concat_axis=0, tiled=True)]
    all_to_all x1 -> x0, local copies, waits for them, and re-layouts: 25.1 us -> none  [shards(): lax.all_to_all(packed, 'lev', split_axis=3, concat_axis=1, tiled=True)]
    convert_element_type x4 -> x2, other arithmetic: 13.9 us -> 0.08 us  [the longest x1 0.08 us: shards(): jnp.stack([band_index == 0, band_index == band_count - 1]).astype(jnp.int32)]
    another operation x4 -> x0, local copies, waits for them, and re-layouts: 11.4 us -> none  [shards(): jnp.stack([jnp.dot(remap_weight, block[index].reshape(count_m, count_r *...]
  transfers between devices with their start and end apart: 5 -> 4, of which waited for: 3 -> 4; matrix products, arithmetic and copies ran while one was open for 2% -> 2% of each run, Pallas kernels for 0% -> 21%
where the time goes in v1:
time: 109 us
  waiting for transfers between devices  44 us (40%)
  Pallas kernels  39.2 us (36%)
  starting transfers between devices  15.3 us (14%)
  local copies, waits for them, and re-layouts  9.94 us (9%)
    all_to_all x1, waiting for transfers between devices, shards(): lax.all_to_all(edge, 'lev', split_axis=0, concat_axis=0, tiled=True)  27.3 us
    pallas_call x1, Pallas kernels, shards(): pl.pallas_call(edge_kernel, grid=(steps,), in_specs=[smem, smem, fields_s...  16.6 us
    all_to_all x1, waiting for transfers between devices, shards(): lax.all_to_all(inner, 'lev', split_axis=0, concat_axis=0, tiled=True)  12.7 us
    unnamed x30, local copies, waits for them, and re-layouts  9.27 us
    pallas_call x1, Pallas kernels, shards(): pl.pallas_call(inner_kernel, grid=(steps,), in_specs=[smem, fields_spec,...  8.43 us
    pallas_call x1, Pallas kernels, shards(): pl.pallas_call(functools.partial(last_kernel, edge_rows, inner_rows), gri...  8.11 us
    all_to_all x1, starting transfers between devices, shards(): lax.all_to_all(inner, 'lev', split_axis=0, concat_axis=0, tiled=True)  7.38 us
    pallas_call x1, Pallas kernels, shards(): pl.pallas_call(functools.partial(half_kernel, inner_rows), grid=(blocks,)...  6.07 us
  transfers between devices with their start and end apart: 4, of which 4 were waited for; matrix products, arithmetic and copies ran while one was open for 2% of the time, Pallas kernels for 21%

profile of v1, /device:TPU:0, one launch (start us, length us, event | category | flops | bytes accessed | tf_op | source)
XLA Modules:
  0.0 108.8 jit_solution(12288665708212684349)
XLA Ops:
  0.0 1.3 %copy-done = f32[2,16,8,1152]{3,2,1,0:T(8,128)S(1)} copy-done((f32[2,16,8,1152]{3,2,1,0:T(8,128)S(1)}, f32[2,16,8,1152]{3,2,1,0:T(8,128)}, u32[]{:S(2)}) %copy-start) | copy-done | bytes 1179672
  1.3 0.7 copy-done.3
  1.9 8.4 %inner_rows.1 = (bf16[8,3,4,4,16,128]{5,4,3,2,1,0:T(8,128)(2,1)S(1)}, f32[6,16,2,1152]{3,2,1,0:T(2,128)S(1)}, f32[6,16,2,1152]{3,2,1,0:T(2,128)S(1)}) custom-call(s32[1,8]{1,0:T(1,128)S(1)} %copy-done.3, f32[4,16,8,1152]{3,2,1,0:T(8,128)} %fields_ref.3, f32[2,16,8,1152]{3,2,1,0:T(8,128)S(1)} %copy-done), custom_call_target="tpu_custom_call" | custom-call | flops 23592960 | bytes 4718592 | tf_op jit(solution)/shard_map/inner_rows/pallas_call | solution.py:265
  10.4 1.2 %copy-done.2 = bf16[8,3,4,4,16,128]{5,4,3,2,1,0:T(8,128)(2,1)} copy-done((bf16[8,3,4,4,16,128]{5,4,3,2,1,0:T(8,128)(2,1)}, bf16[8,3,4,4,16,128]{5,4,3,2,1,0:T(8,128)(2,1)S(1)}, u32[]{:S(2)}) %copy-start.2) | copy-done | bytes 1572888
  11.5 0.9 copy-done.5
  12.5 0.9 copy-done.6
  13.4 7.4 %all-to-all-start.1 = ((bf16[8,3,4,4,16,128]{5,4,3,2,1,0:T(8,128)(2,1)}), bf16[8,3,4,4,16,128]{5,4,3,2,1,0:T(8,128)(2,1)S(1)}, u32[]{:S(2)}, u32[]{:S(2)}) async-start(bf16[8,3,4,4,16,128]{5,4,3,2,1,0:T(8,128)(2,1)} %copy-done.2), calls=%async_computation.1 | async-start | bytes 3145728 | tf_op jit(solution)/shard_map/all_to_all | solution.py:281
  20.8 2.4 %collective-permute-start = (f32[6,16,2,1152]{3,2,1,0:T(2,128)}, f32[6,16,2,1152]{3,2,1,0:T(2,128)}, u32[]{:S(2)}, u32[]{:S(2)}) collective-permute-start(f32[6,16,2,1152]{3,2,1,0:T(2,128)} %copy-done.6), channel_id=1, source_target_pairs={{0,8},{8,16},{16,24},{1,9},{9,17},{17,25},{2,10},{10,18},{18,26},{... | collective-permute-start | bytes 2654216 | tf_op jit(solution)/shard_map/ppermute | solution.py:282
  23.1 1.3 %collective-permute-start.1 = (f32[6,16,2,1152]{3,2,1,0:T(2,128)}, f32[6,16,2,1152]{3,2,1,0:T(2,128)}, u32[]{:S(2)}, u32[]{:S(2)}) collective-permute-start(f32[6,16,2,1152]{3,2,1,0:T(2,128)} %copy-done.5), channel_id=1, source_target_pairs={{8,0},{16,8},{24,16},{9,1},{17,9},{25,17},{10,2},{18,10},{26,18},{... | collective-permute-start | bytes 2654216 | tf_op jit(solution)/shard_map/ppermute | solution.py:283
  24.6 3.9 %collective-permute-done.1.after_ref = f32[6,16,2,1152]{3,2,1,0:T(2,128)} collective-permute-done((f32[6,16,2,1152]{3,2,1,0:T(2,128)}, f32[6,16,2,1152]{3,2,1,0:T(2,128)}, u32[]{:S(2)}, u32[]{:S(2)}) %collective-permute-start.1) | collective-permute-done | bytes 884768 | tf_op jit(solution)/shard_map/ppermute | solution.py:283
  28.5 16.6 %edge_rows.1 = bf16[8,3,4,4,16,128]{5,4,3,2,1,0:T(8,128)(2,1)} custom-call(s32[1,8]{1,0:T(1,128)S(1)} %copy-done.4, s32[2]{0:T(128)S(1)} %add_convert_fusion.band_ref, f32[4,16,8,1152]{3,2,1,0:T(8,128)} %fields_ref.3, f32[2,16,8,1152]{3,2,1,0:T(8,128)S(1)} %copy-done.1, f32[6,16,2,1152]{3,2,1,0:T(2,128)} %collective-permute-done.before_ref, ...), custom_call_target="tpu_custom_call" | custom-call | flops 47185920 | bytes 5898240 | tf_op jit(solution)/shard_map/edge_rows/pallas_call | solution.py:286
  45.1 12.7 %all-to-all-done.1.block_ref = bf16[8,3,4,4,16,128]{5,4,3,2,1,0:T(8,128)(2,1)S(1)} async-done(((bf16[8,3,4,4,16,128]{5,4,3,2,1,0:T(8,128)(2,1)}), bf16[8,3,4,4,16,128]{5,4,3,2,1,0:T(8,128)(2,1)S(1)}, u32[]{:S(2)}, u32[]{:S(2)}) %all-to-all-start.1) | async-done | bytes 1572896 | tf_op jit(solution)/shard_map/all_to_all | solution.py:281
  57.8 4.3 %all-to-all-start = ((bf16[8,3,4,4,16,128]{5,4,3,2,1,0:T(8,128)(2,1)}), bf16[8,3,4,4,16,128]{5,4,3,2,1,0:T(8,128)(2,1)}, u32[]{:S(2)}, u32[]{:S(2)}) async-start(bf16[8,3,4,4,16,128]{5,4,3,2,1,0:T(8,128)(2,1)} %edge_rows.1), calls=%async_computation | async-start | bytes 3145728 | tf_op jit(solution)/shard_map/all_to_all | solution.py:299
  62.1 0.7 constant_dynamic-slice_fusion
  62.7 0.1 copy.12
  62.8 0.1 compare_reduce_fusion
  63.0 0.2 copy.13
  63.2 0.2 copy.14
  63.4 1.3 %copy.15 = bf16[512,512]{0,1:T(8,128)(2,1)S(1)} copy(bf16[512,512]{1,0:T(8,128)(2,1)} %param.13) | data formatting | bytes 1048576 | tf_op args[5]
  64.7 6.1 %inner_columns.1.done_ref = bf16[4,512,384]{2,1,0:T(8,128)(2,1)S(1)} custom-call(s32[8]{0:T(128)S(1)} %convert_element_type.6.listed_ref, s32[1]{0:T(128)} %bitcast.width_ref, bf16[8,3,4,4,16,128]{5,4,3,2,1,0:T(8,128)(2,1)S(1)} %all-to-all-done.1.block_ref, bf16[128,128]{1,0:T(8,128)(2,1)S(1)} %copy-done.7, bf16[512,512]{1,0:T(8,128)(2,1)S(1)} %bitcast.7, ...), custom_call_target="tpu_custom_call" | custom-call | flops 2617245696 | bytes 3145728 | tf_op jit(solution)/shard_map/inner_columns/pallas_call | solution.py:330
  70.8 1.1 %copy-done.8 = bf16[4,512,384]{2,1,0:T(8,128)(2,1)} copy-done((bf16[4,512,384]{2,1,0:T(8,128)(2,1)}, bf16[4,512,384]{2,1,0:T(8,128)(2,1)S(1)}, u32[]{:S(2)}) %copy-start.8) | copy-done | bytes 1572888
  71.9 27.3 %all-to-all-done.block_ref = bf16[8,3,4,4,16,128]{5,4,3,2,1,0:T(8,128)(2,1)} async-done(((bf16[8,3,4,4,16,128]{5,4,3,2,1,0:T(8,128)(2,1)}), bf16[8,3,4,4,16,128]{5,4,3,2,1,0:T(8,128)(2,1)}, u32[]{:S(2)}, u32[]{:S(2)}) %all-to-all-start) | async-done | bytes 1572896 | tf_op jit(solution)/shard_map/all_to_all | solution.py:299
  99.2 1.4 %copy-done.9 = bf16[4,512,384]{2,1,0:T(8,128)(2,1)S(1)} copy-done((bf16[4,512,384]{2,1,0:T(8,128)(2,1)S(1)}, bf16[4,512,384]{2,1,0:T(8,128)(2,1)}, u32[]{:S(2)}) %copy-start.9) | copy-done | bytes 1572888
  100.6 8.1 %edge_columns.1 = bf16[512,8,384]{2,1,0:T(8,128)(2,1)} custom-call(s32[8]{0:T(128)S(1)} %convert_element_type.6.listed_ref, s32[1]{0:T(128)} %bitcast.width_ref, bf16[8,3,4,4,16,128]{5,4,3,2,1,0:T(8,128)(2,1)} %all-to-all-done.block_ref, bf16[4,512,384]{2,1,0:T(8,128)(2,1)S(1)} %copy-done.9, bf16[128,128]{1,0:T(8,128)(2,1)S(1)} %copy-done.7, ...), custom_call_target="tpu_custom_call" | custom-call | flops 2617245696 | bytes 3145728 | tf_op jit(solution)/shard_map/edge_columns/pallas_call | solution.py:340
  (23 shorter events, 0.2 us)
Async XLA Ops:
  0.0 1.3 %copy-start = (f32[2,16,8,1152]{3,2,1,0:T(8,128)S(1)}, f32[2,16,8,1152]{3,2,1,0:T(8,128)}, u32[]{:S(2)}) copy-start(f32[2,16,8,1152]{3,2,1,0:T(8,128)} %winds_ref.3) | copy-start | bytes 3538948
  1.3 0.7 copy-start.3
  10.4 1.2 %copy-start.2 = (bf16[8,3,4,4,16,128]{5,4,3,2,1,0:T(8,128)(2,1)}, bf16[8,3,4,4,16,128]{5,4,3,2,1,0:T(8,128)(2,1)S(1)}, u32[]{:S(2)}) copy-start(bf16[8,3,4,4,16,128]{5,4,3,2,1,0:T(8,128)(2,1)S(1)} %get-tuple-element.10) | copy-start | bytes 4718596
  11.5 0.9 copy-start.5
  12.5 0.9 copy-start.6
  13.4 15.1 %copy-start.1 = (f32[2,16,8,1152]{3,2,1,0:T(8,128)S(1)}, f32[2,16,8,1152]{3,2,1,0:T(8,128)}, u32[]{:S(2)}) copy-start(f32[2,16,8,1152]{3,2,1,0:T(8,128)} %winds_ref.3) | copy-start | bytes 3538948
  13.4 15.1 %copy-start.4 = (s32[1,8]{1,0:T(1,128)S(1)}, s32[1,8]{1,0:T(1,128)}, u32[]{:S(2)}) copy-start(s32[1,8]{1,0:T(1,128)} %counts_ref.3) | copy-start | bytes 100
  13.4 44.4 %all-to-all-start.1 = ((bf16[8,3,4,4,16,128]{5,4,3,2,1,0:T(8,128)(2,1)}), bf16[8,3,4,4,16,128]{5,4,3,2,1,0:T(8,128)(2,1)S(1)}, u32[]{:S(2)}, u32[]{:S(2)}) async-start(bf16[8,3,4,4,16,128]{5,4,3,2,1,0:T(8,128)(2,1)} %copy-done.2), calls=%async_computation.1 | async-start | bytes 3145728 | tf_op jit(solution)/shard_map/all_to_all | solution.py:281
  20.8 3.8 %collective-permute-start = (f32[6,16,2,1152]{3,2,1,0:T(2,128)}, f32[6,16,2,1152]{3,2,1,0:T(2,128)}, u32[]{:S(2)}, u32[]{:S(2)}) collective-permute-start(f32[6,16,2,1152]{3,2,1,0:T(2,128)} %copy-done.6), channel_id=1, source_target_pairs={{0,8},{8,16},{16,24},{1,9},{9,17},{17,25},{2,10},{10,18},{18,26},{... | collective-permute-start | bytes 2654216 | tf_op jit(solution)/shard_map/ppermute | solution.py:282
  23.1 5.3 %collective-permute-start.1 = (f32[6,16,2,1152]{3,2,1,0:T(2,128)}, f32[6,16,2,1152]{3,2,1,0:T(2,128)}, u32[]{:S(2)}, u32[]{:S(2)}) collective-permute-start(f32[6,16,2,1152]{3,2,1,0:T(2,128)} %copy-done.5), channel_id=1, source_target_pairs={{8,0},{16,8},{24,16},{9,1},{17,9},{25,17},{10,2},{18,10},{26,18},{... | collective-permute-start | bytes 2654216 | tf_op jit(solution)/shard_map/ppermute | solution.py:283
  45.1 17.6 %copy-start.12 = (s32[4,6]{1,0:T(4,128)S(1)}, s32[4,6]{1,0:T(4,128)}, u32[]{:S(2)}) copy-start(s32[4,6]{1,0:T(4,128)} %param.15) | copy-start | bytes 292
  45.1 17.8 %copy-start.10 = (bf16[512,512]{1,0:T(8,128)(2,1)S(1)}, bf16[512,512]{1,0:T(8,128)(2,1)}, u32[]{:S(2)}) copy-start(bf16[512,512]{1,0:T(8,128)(2,1)} %param.11) | copy-start | bytes 1572868
  45.1 18.1 %copy-start.11 = (bf16[512,512]{1,0:T(8,128)(2,1)S(1)}, bf16[512,512]{1,0:T(8,128)(2,1)}, u32[]{:S(2)}) copy-start(bf16[512,512]{1,0:T(8,128)(2,1)} %param.12) | copy-start | bytes 1572868
  57.8 41.5 %all-to-all-start = ((bf16[8,3,4,4,16,128]{5,4,3,2,1,0:T(8,128)(2,1)}), bf16[8,3,4,4,16,128]{5,4,3,2,1,0:T(8,128)(2,1)}, u32[]{:S(2)}, u32[]{:S(2)}) async-start(bf16[8,3,4,4,16,128]{5,4,3,2,1,0:T(8,128)(2,1)} %edge_rows.1), calls=%async_computation | async-start | bytes 3145728 | tf_op jit(solution)/shard_map/all_to_all | solution.py:299
  63.0 1.7 %copy-start.7 = (bf16[128,128]{1,0:T(8,128)(2,1)S(1)}, bf16[128,128]{1,0:T(8,128)(2,1)}, u32[]{:S(2)}) copy-start(bf16[128,128]{1,0:T(8,128)(2,1)} %remap_ref.3) | copy-start | bytes 98308
  70.8 1.1 %copy-start.8 = (bf16[4,512,384]{2,1,0:T(8,128)(2,1)}, bf16[4,512,384]{2,1,0:T(8,128)(2,1)S(1)}, u32[]{:S(2)}) copy-start(bf16[4,512,384]{2,1,0:T(8,128)(2,1)S(1)} %inner_columns.1.done_ref) | copy-start | bytes 4718596
  99.2 1.4 %copy-start.9 = (bf16[4,512,384]{2,1,0:T(8,128)(2,1)S(1)}, bf16[4,512,384]{2,1,0:T(8,128)(2,1)}, u32[]{:S(2)}) copy-start(bf16[4,512,384]{2,1,0:T(8,128)(2,1)} %copy-done.8) | copy-start | bytes 4718596

commit v2 on v0

v2 whole, which is shorter than its diff:
```python
import functools

import jax
import jax.numpy as jnp
from jax import lax
from jax.experimental import pallas as pl
from jax.experimental.pallas import tpu as pltpu
from jax.sharding import PartitionSpec as P

DIFFUSION = 0.15
LANES = 128
HALO = 2
MIB = 1024 * 1024


def from_west(x):
    return pltpu.roll(x, 1, 1)


def from_east(x):
    return pltpu.roll(x, x.shape[1] - 1, 1)


def flux(weights, before, after):
    return weights[0] * before + weights[1] * after


def face_weights(before, after):
    half = 0.25 * (before + after)
    return half + DIFFUSION, half - DIFFUSION


def divergences(values, rows, north, east):
    above = flux(north(rows[0]), values[rows[0] - 1], values[rows[0]])
    result = {}
    for row in rows:
        below = flux(north(row + 1), values[row], values[row + 1])
        side = flux(east(row), from_west(values[row]), values[row])
        result[row] = (above - below) + (side - from_east(side))
        above = below
    return result


def heun_rows(values, north, east):
    count = len(values)
    first = divergences(values, range(1, count - 1), north, east)
    predicted = {row: values[row] + first[row] for row in first}
    inner = range(2, count - 2)
    second = divergences(predicted, inner, north, east)
    return [0.5 * (values[row] + predicted[row] + second[row]) for row in inner]


def start_grid(fields_ref, winds_ref, grid_ref, sems):
    fields, tiles = fields_ref.shape[0], grid_ref.shape[1]

    def copy(array, tile, source):
        lanes = pl.ds(tile * LANES, LANES)
        return pltpu.make_async_copy(
            source.at[:, lanes], grid_ref.at[array, tile], sems.at[array, tile]
        )

    for wind in range(2):
        for tile in range(tiles):
            copy(fields + wind, tile, winds_ref.at[wind]).start()
    for field in range(fields):
        for tile in range(tiles):
            copy(field, tile, fields_ref.at[field]).start()

    def wait(array):
        for tile in range(tiles):
            copy(array, tile, fields_ref.at[0]).wait()

    return wait


def load_row(grid_ref, array, row, group, size, rows):
    start = group * (size * rows) + row
    pieces = [
        grid_ref[array, tile, pl.ds(start, size, stride=rows), :]
        for tile in range(grid_ref.shape[1])
    ]
    return jnp.concatenate(pieces, axis=1)


def store_weights(north_ref, east_ref, levels, east_winds, north_winds, wall=None):
    count = len(north_winds)
    for face in range(1, count):
        pair = face_weights(north_winds[face - 1], north_winds[face])
        for side in range(2):
            shut = wall is not None and wall[0] == face
            north_ref[face, side, levels, :] = pair[side] * wall[1] if shut else pair[side]
    for row in range(1, count - 1):
        pair = face_weights(from_west(east_winds[row]), east_winds[row])
        for side in range(2):
            east_ref[row, side, levels, :] = pair[side]


def keep_row(kept_ref, index, levels, value):
    for tile in range(value.shape[1] // LANES):
        kept_ref[tile, index, levels, :] = value[:, tile * LANES : (tile + 1) * LANES]


def clear_tail(kept_ref, tiles):
    for tile in range(tiles, kept_ref.shape[0]):
        kept_ref[tile] = jnp.zeros(kept_ref.shape[1:], kept_ref.dtype)


def slot_starts(counts_ref, owners):
    starts = []
    total = jnp.int32(0)
    for owner in range(owners):
        starts.append(total)
        total = total + counts_ref[0, owner]
    return starts


def pack_rows(kept_ref, starts, blocks, store):
    _, rows, levels, _ = kept_ref.shape
    lane = lax.broadcasted_iota(jnp.int32, (levels, LANES), 1)
    for slot, start in enumerate(starts):
        tile = start // LANES
        inside = start - tile * LANES
        shift = (LANES - inside) % LANES
        keep = lane < LANES - inside
        for row in range(rows):
            turned = [
                pltpu.roll(kept_ref[tile + j, row], shift, 1) for j in range(blocks + 1)
            ]
            for j in range(blocks):
                joined = jnp.where(keep, turned[j], turned[j + 1])
                store(slot, j, row, joined.astype(jnp.bfloat16))


def inner_kernel(
    rows,
    counts_ref,
    fields_ref,
    winds_ref,
    out_ref,
    grid_ref,
    north_ref,
    east_ref,
    kept_ref,
    sems,
    packed_ref,
    sent,
):
    fields = fields_ref.shape[0]
    owners, _, blocks, _, levels, _ = out_ref.shape
    size = min(8, levels)
    groups = levels // size
    wait = start_grid(fields_ref, winds_ref, grid_ref, sems)
    clear_tail(kept_ref, grid_ref.shape[1])
    starts = slot_starts(counts_ref, owners)

    def field_out(field):
        return pltpu.make_async_copy(packed_ref.at[field], out_ref.at[:, field], sent.at[field])

    wait(fields)
    wait(fields + 1)

    def weights(group, carry):
        east = [load_row(grid_ref, fields, row, group, size, rows) for row in range(rows)]
        north = [load_row(grid_ref, fields + 1, row, group, size, rows) for row in range(rows)]
        store_weights(north_ref, east_ref, pl.ds(group * size, size), east, north)
        return carry

    lax.fori_loop(0, groups, weights, 0)

    def one_field(field, carry):
        wait(field)

        def one_group(group, carry):
            place = pl.ds(group * size, size)
            values = [load_row(grid_ref, field, row, group, size, rows) for row in range(rows)]

            def north(face):
                return north_ref[face, 0, place, :], north_ref[face, 1, place, :]

            def east(row):
                return east_ref[row, 0, place, :], east_ref[row, 1, place, :]

            for index, value in enumerate(heun_rows(values, north, east)):
                keep_row(kept_ref, index, place, value)
            return carry

        lax.fori_loop(0, groups, one_group, 0)

        def store(slot, block, row, value):
            packed_ref[field, slot, block, row] = value

        pack_rows(kept_ref, starts, blocks, store)
        field_out(field).start()
        return carry

    lax.fori_loop(0, fields, one_field, 0)
    for field in range(fields):
        field_out(field).wait()


def halo_kernel(rows, fields_ref, winds_ref, first_ref, last_ref, grid_ref, sems):
    fields = fields_ref.shape[0]
    levels = first_ref.shape[2]
    size = min(8, levels)
    wait = start_grid(fields_ref, winds_ref, grid_ref, sems)
    for array in (fields, fields + 1) + tuple(range(fields)):
        wait(array)
        for group in range(levels // size):
            place = pl.ds(group * size, size)
            for row in range(HALO):
                last = rows - HALO + row
                first_ref[array, row, place, :] = load_row(grid_ref, array, row, group, size, rows)
                last_ref[array, row, place, :] = load_row(grid_ref, array, last, group, size, rows)


def edge_kernel(
    rows,
    split,
    counts_ref,
    place_ref,
    fields_ref,
    winds_ref,
    before_ref,
    after_ref,
    *refs,
):
    outs, (grid_ref, north_ref, east_ref, kept_ref, sems, start_ref) = refs[:-6], refs[-6:]
    early_refs, late_refs = outs[: len(outs) // 2], outs[len(outs) // 2 :]
    fields = fields_ref.shape[0]
    owners = start_ref.shape[0]
    blocks = split + late_refs[0].shape[-4]
    levels = before_ref.shape[2]
    size = min(8, levels)
    groups = levels // size
    wait = start_grid(fields_ref, winds_ref, grid_ref, sems)
    clear_tail(kept_ref, grid_ref.shape[1])
    for owner, start in enumerate(slot_starts(counts_ref, owners)):
        start_ref[owner] = start
    count = 3 * HALO

    def run(array, group, top):
        place = pl.ds(group * size, size)
        own = range(2 * HALO) if top else range(rows - 2 * HALO, rows)
        own = [load_row(grid_ref, array, row, group, size, rows) for row in own]
        if top:
            return [before_ref[array, row, place, :] for row in range(HALO)] + own
        return own + [after_ref[array, row, place, :] for row in range(HALO)]

    wait(fields)
    wait(fields + 1)
    for top in (True, False):
        north_side, east_side = north_ref.at[int(top)], east_ref.at[int(top)]
        wall = HALO if top else count - HALO
        is_open = jnp.where(place_ref[0 if top else 1] == 1, 0.0, 1.0)

        def weights(group, carry):
            store_weights(
                north_side,
                east_side,
                pl.ds(group * size, size),
                run(fields, group, top),
                run(fields + 1, group, top),
                (wall, is_open),
            )
            return carry

        lax.fori_loop(0, groups, weights, 0)

    def one_field(field, carry):
        wait(field)

        def one_group(group, carry):
            place = pl.ds(group * size, size)
            for top in (True, False):
                side = int(top)

                def north(face):
                    return north_ref[side, face, 0, place, :], north_ref[side, face, 1, place, :]

                def east(row):
                    return east_ref[side, row, 0, place, :], east_ref[side, row, 1, place, :]

                done = heun_rows(run(field, group, top), north, east)
                for index, value in enumerate(done):
                    keep_row(kept_ref, index + (0 if top else HALO), place, value)
            return carry

        lax.fori_loop(0, groups, one_group, 0)

        def store(slot, block, row, value):
            if block < split:
                early_refs[slot][field, block, row] = value
            elif early_refs:
                late_refs[slot][field, block - split, row] = value
            else:
                late_refs[0][slot, field, block, row] = value

        slots = [start_ref[place_ref[2] ^ turn] for turn in range(owners)]
        if not early_refs:
            slots = [start_ref[owner] for owner in range(owners)]
        pack_rows(kept_ref, slots, blocks, store)
        return carry

    lax.fori_loop(0, fields, one_field, 0)


def silu(x):
    half = 0.5 * x
    return half + half * jnp.tanh(half)


def dot(a, b):
    return jnp.dot(a, b, preferred_element_type=jnp.float32)


def gathered(block_ref, field):
    sources, _, _, rows = block_ref.shape[:4]
    by_row = [
        jnp.concatenate([block_ref[source, field, 0, row] for source in range(sources)], axis=0)
        for row in range(rows)
    ]
    return jnp.concatenate(by_row, axis=1)


def sort_turns(own, refs, sorted_ref):
    fields, _, rows, levels, _ = refs[0].shape
    for turn, ref in enumerate(refs):
        place = pl.ds(pl.multiple_of((own ^ turn) * levels, levels), levels)
        for field in range(fields):
            for row in range(rows):
                sorted_ref[field, place, row * LANES : (row + 1) * LANES] = ref[field, 0, row]


def column_update(columns, fields, remap_ref, first_ref, second_ref, third_ref):
    remapped = []
    for field in range(fields):
        values = columns(field)
        remapped.append(values.astype(jnp.float32) + dot(remap_ref[...], values))
    remapped = jnp.concatenate(remapped, axis=0)
    hidden = silu(dot(first_ref[...], remapped.astype(jnp.bfloat16))).astype(jnp.bfloat16)
    hidden = silu(dot(second_ref[...], hidden)).astype(jnp.bfloat16)
    tendency = dot(third_ref[...], hidden).astype(jnp.bfloat16).astype(jnp.float32)
    return remapped, tendency


def finished_row(remapped, tendency, listed, index, live):
    lanes = slice(index * LANES, (index + 1) * LANES)
    updated = remapped[:, lanes] + jnp.where(listed == 1, tendency[:, lanes], 0.0)
    return jnp.where(live, updated, 0.0)


def live_lanes(width_ref, features, block):
    lane = lax.broadcasted_iota(jnp.int32, (features, LANES), 1)
    return lane + block * LANES < width_ref[0]


def half_kernel(
    row_list,
    listed_ref,
    width_ref,
    block_ref,
    remap_ref,
    first_ref,
    second_ref,
    third_ref,
    out_ref,
    first_out,
    second_out,
    third_out,
):
    @pl.when(pl.program_id(0) == 0)
    def _():
        first_out[...] = first_ref[...].T
        second_out[...] = second_ref[...].T
        third_out[...] = third_ref[...].T

    remapped, tendency = column_update(
        functools.partial(gathered, block_ref),
        block_ref.shape[1],
        remap_ref,
        first_out,
        second_out,
        third_out,
    )
    live = live_lanes(width_ref, remapped.shape[0], pl.program_id(0))
    for index, row in enumerate(row_list):
        out_ref[index] = finished_row(remapped, tendency, listed_ref[row], index, live).astype(
            jnp.bfloat16
        )


def last_kernel(row_list, done_list, base, turns, listed_ref, width_ref, *refs):
    *refs, done_ref, remap_ref, first_ref, second_ref, third_ref, out_ref, tiles_ref, sorted_ref = (
        refs
    )
    features, rows, _ = out_ref.shape
    fields = sorted_ref.shape[0]
    if turns:
        sort_turns(width_ref[1], refs[-turns:], sorted_ref)

        def columns(field):
            return sorted_ref[field]
    else:
        columns = functools.partial(gathered, refs[-1])
    remapped, tendency = column_update(
        columns, fields, remap_ref, first_ref, second_ref, third_ref
    )
    live = live_lanes(width_ref, features, pl.program_id(0) + base)
    for index, row in enumerate(done_list):
        tiles_ref[pl.ds(row, features, stride=rows), :] = done_ref[index].astype(jnp.float32)
    for index, row in enumerate(row_list):
        tiles_ref[pl.ds(row, features, stride=rows), :] = finished_row(
            remapped, tendency, listed_ref[row], index, live
        )
    out_ref[...] = tiles_ref[...].reshape(features, rows, LANES).astype(jnp.bfloat16)


def shards(fields, winds, remap_weight, w_first, w_second, w_third, lon_counts, group_list):
    field_count, level_count, lat_rows, lon_total = fields.shape
    band_count = lax.axis_size("lat")
    band_index = lax.axis_index("lat")
    owner_count = lax.axis_size("lev")
    first_row = band_index * lat_rows
    all_levels = level_count * owner_count
    features = field_count * all_levels
    blocks = (2 * lon_total // owner_count + LANES - 1) // LANES
    slot_width = blocks * LANES
    split = blocks - 1
    inner_rows = tuple(range(HALO, lat_rows - HALO))
    edge_rows = tuple(range(HALO)) + tuple(range(lat_rows - HALO, lat_rows))
    half = len(inner_rows)
    stacked = field_count + 2
    tiles = lon_total // LANES
    smem = pl.BlockSpec(memory_space=pltpu.SMEM)
    anywhere = pl.BlockSpec(memory_space=pl.ANY)
    params = pltpu.CompilerParams(vmem_limit_bytes=60 * MIB)
    values = field_count * level_count * lat_rows * lon_total

    def payload(count):
        return (owner_count, field_count, count, half, level_count, LANES)

    flat_fields = fields.reshape(field_count, level_count * lat_rows, lon_total)
    flat_winds = winds.reshape(2, level_count * lat_rows, lon_total)
    halo_shape = jax.ShapeDtypeStruct((stacked, HALO, level_count, lon_total), jnp.float32)

    def scratch(sides, count):
        return [
            pltpu.VMEM((stacked, tiles, level_count * lat_rows, LANES), jnp.float32),
            pltpu.VMEM(sides + (count, 2, level_count, lon_total), jnp.float32),
            pltpu.VMEM(sides + (count - 1, 2, level_count, lon_total), jnp.float32),
            pltpu.VMEM((tiles + blocks, half, level_count, LANES), jnp.float32),
            pltpu.SemaphoreType.DMA((stacked, tiles)),
        ]

    inner = pl.pallas_call(
        functools.partial(inner_kernel, lat_rows),
        in_specs=[smem, anywhere, anywhere],
        out_specs=anywhere,
        out_shape=jax.ShapeDtypeStruct(payload(blocks), jnp.bfloat16),
        scratch_shapes=scratch((), lat_rows)
        + [
            pltpu.VMEM((field_count, owner_count) + payload(blocks)[2:], jnp.bfloat16),
            pltpu.SemaphoreType.DMA((field_count,)),
        ],
        compiler_params=params,
        cost_estimate=pl.CostEstimate(
            flops=40 * values, bytes_accessed=8 * values, transcendentals=0
        ),
        name="inner_rows",
    )(lon_counts, flat_fields, flat_winds)

    late_fields, late_winds, inner = lax.optimization_barrier((flat_fields, flat_winds, inner))
    first, last = pl.pallas_call(
        functools.partial(halo_kernel, lat_rows),
        in_specs=[anywhere, anywhere],
        out_shape=[halo_shape, halo_shape],
        scratch_shapes=[scratch((), lat_rows)[0], scratch((), lat_rows)[-1]],
        compiler_params=params,
        cost_estimate=pl.CostEstimate(
            flops=values, bytes_accessed=8 * values, transcendentals=0
        ),
        name="halo_rows",
    )(late_fields, late_winds)

    up = [(i, i + 1) for i in range(band_count - 1)]
    down = [(j, i) for i, j in up]

    def exchange(x):
        return lax.all_to_all(x, "lev", split_axis=0, concat_axis=0, tiled=True)

    inner_block = exchange(inner)
    before = lax.ppermute(last, "lat", up)
    after = lax.ppermute(first, "lat", down)

    own = lax.axis_index("lev")
    place = jnp.stack([band_index == 0, band_index == band_count - 1, own]).astype(jnp.int32)
    by_turn = split > 0
    if by_turn:
        edge_shapes = [payload(split)[1:]] * owner_count
        edge_shapes += [payload(blocks - split)[1:]] * owner_count
    else:
        edge_shapes = [payload(blocks)]
    edge = pl.pallas_call(
        functools.partial(edge_kernel, lat_rows, split),
        in_specs=[smem, smem, anywhere, anywhere] + [pl.BlockSpec(memory_space=pltpu.VMEM)] * 2,
        out_shape=[jax.ShapeDtypeStruct(shape, jnp.bfloat16) for shape in edge_shapes],
        scratch_shapes=scratch((2,), 3 * HALO) + [pltpu.SMEM((owner_count,), jnp.int32)],
        compiler_params=params,
        cost_estimate=pl.CostEstimate(
            flops=80 * values, bytes_accessed=10 * values, transcendentals=0
        ),
        name="edge_rows",
    )(lon_counts, place, late_fields, late_winds, before, after)

    def turned_exchange(x, turn):
        return lax.ppermute(x, "lev", [(i, i ^ turn) for i in range(owner_count)]) if turn else x

    if by_turn:
        early, late = list(edge[:owner_count]), list(edge[owner_count:])
        early = [turned_exchange(x, turn) for turn, x in enumerate(early)]
    else:
        early, late = [], edge

    listed = jnp.any(
        group_list[:, :, None] == (first_row + jnp.arange(lat_rows, dtype=jnp.int32))[None, None, :],
        axis=(0, 1),
    ).astype(jnp.int32)
    width = jnp.stack([lon_counts[0][own], own]).astype(jnp.int32)

    def by_level(block):
        if level_count % 16 == 0:
            return block
        return block.transpose(1, 2, 3, 0, 4, 5).reshape(
            1, field_count, block.shape[2], half, all_levels, LANES
        )

    def whole(shape):
        return pl.BlockSpec(shape, lambda i: (0,) * len(shape))

    def block_spec(block):
        return pl.BlockSpec(
            block.shape[:2] + (1,) + block.shape[3:], lambda i: (0, 0, i, 0, 0, 0)
        )

    def cost(count):
        columns = half * count * LANES
        return pl.CostEstimate(
            flops=2 * features * columns * (3 * w_first.shape[1] + all_levels),
            bytes_accessed=4 * features * columns,
            transcendentals=2 * w_first.shape[1] * columns,
        )

    weights = (w_first, w_second, w_third)
    weight_specs = [whole(w.shape) for w in (remap_weight,) + weights]
    inner_block = by_level(inner_block)
    done, *turned = pl.pallas_call(
        functools.partial(half_kernel, inner_rows),
        grid=(blocks,),
        in_specs=[smem, smem, block_spec(inner_block)] + weight_specs,
        out_specs=[pl.BlockSpec((half, features, LANES), lambda i: (0, 0, i))]
        + [whole(w.shape[::-1]) for w in weights],
        out_shape=[jax.ShapeDtypeStruct((half, features, slot_width), jnp.bfloat16)]
        + [jax.ShapeDtypeStruct(w.shape[::-1], w.dtype) for w in weights],
        compiler_params=params,
        cost_estimate=cost(blocks),
        name="inner_columns",
    )(listed, width, inner_block, remap_weight, *weights)

    if by_turn:
        for turn in range(1, owner_count):
            early[turn], late[turn], done = lax.optimization_barrier(
                (early[turn], late[turn], done)
            )
        late = [turned_exchange(x, turn) for turn, x in enumerate(late)]
    else:
        late = [by_level(exchange(late[0]))]
    out = None
    base = 0
    for part in ([early] if early else []) + [late]:
        turns = len(part) if by_turn else 0
        count = part[0].shape[1 if turns else 2]
        offset = base
        if turns:
            specs = [
                pl.BlockSpec((field_count, 1, half, level_count, LANES), lambda i: (0, i, 0, 0, 0))
            ] * len(part)
        else:
            specs = [block_spec(part[0])]
        out = pl.pallas_call(
            functools.partial(last_kernel, edge_rows, inner_rows, offset, turns),
            grid=(count,),
            in_specs=[smem, smem]
            + [anywhere] * (base > 0)
            + specs
            + [pl.BlockSpec((half, features, LANES), lambda i, o=offset: (0, 0, i + o))]
            + weight_specs,
            out_specs=pl.BlockSpec((features, lat_rows, LANES), lambda i, o=offset: (0, 0, i + o)),
            out_shape=jax.ShapeDtypeStruct((features, lat_rows, slot_width), jnp.bfloat16),
            scratch_shapes=[
                pltpu.VMEM((features * lat_rows, LANES), jnp.float32),
                pltpu.VMEM((field_count, all_levels, half * LANES), jnp.bfloat16),
            ],
            input_output_aliases={2: 0} if base > 0 else {},
            compiler_params=params,
            cost_estimate=cost(count),
            name="edge_columns",
        )(listed, width, *([out] if base > 0 else []), *part, done, remap_weight, *turned)
        base += count
    return out.reshape(field_count, all_levels, lat_rows, slot_width)


def solution(mesh):
    in_specs = (
        P(None, "lev", "lat", None),
        P(None, "lev", "lat", None),
        P(),
        P(),
        P(),
        P(),
        P("lat", None),
        P(),
    )
    out_specs = P(None, None, "lat", "lev")
    return jax.shard_map(shards, mesh=mesh, in_specs=in_specs, out_specs=out_specs, check_vma=False)
```

time: 297 us -> 94.2 us (0.32)
  the two profiles are of different devices: /device:TPU:0 before, /device:TPU:4 now
where the time goes in v2:
time: 94.2 us; the launch traced here: 93.8 us
  Pallas kernels  39.9 us (42%)
  starting transfers between devices  36.6 us (39%)
  waiting for transfers between devices  10.9 us (12%)
  local copies, waits for them, and re-layouts  3.53 us (4%)
  other arithmetic  2.58 us (3%)
    ppermute x14, starting transfers between devices, turned_exchange(): lax.ppermute(x, 'lev', [(i, i ^ turn) for i in range(owner_count)])  25.2 us
    pallas_call x2, Pallas kernels, shards(): pl.pallas_call(functools.partial(last_kernel, edge_rows, inner_rows, offs...  11.1 us
    pallas_call x1, Pallas kernels, shards(): pl.pallas_call(functools.partial(edge_kernel, lat_rows, split), in_specs=...  9.88 us
    ppermute x1, waiting for transfers between devices, shards(): before = lax.ppermute(last, 'lat', up)  8.22 us
    pallas_call x1, Pallas kernels, shards(): pl.pallas_call(functools.partial(inner_kernel, lat_rows), in_specs=[smem,...  7.8 us
    pallas_call x1, Pallas kernels, shards(): pl.pallas_call(functools.partial(half_kernel, inner_rows), grid=(blocks,)...  7.34 us
    all_to_all x1, starting transfers between devices, exchange(): return lax.all_to_all(x, 'lev', split_axis=0, concat_axis=0, tiled=True)  5.82 us
    pallas_call x1, Pallas kernels, shards(): pl.pallas_call(functools.partial(halo_kernel, lat_rows), in_specs=[anywhe...  3.79 us
  transfers between devices with their start and end apart: 17, of which 3 were waited for; matrix products, arithmetic and copies ran while one was open for 4% of the time, Pallas kernels for 29%

profile of v2, /device:TPU:4, one launch (start us, length us, event | category | flops | bytes accessed | tf_op | source)
XLA Modules:
  0.0 93.8 jit_solution(675358120499502314)
XLA Ops:
  0.0 7.8 %inner_rows.1 = bf16[8,4,3,4,16,128]{5,4,3,2,1,0:T(8,128)(2,1)} custom-call(s32[1,8]{1,0:T(1,128)} %counts_ref.3, f32[4,128,1152]{2,1,0:T(8,128)} %bitcast.7, f32[2,128,1152]{2,1,0:T(8,128)} %bitcast.10), custom_call_target="tpu_custom_call" | custom-call | flops 23592960 | bytes 4718592 | tf_op jit(solution)/shard_map/inner_rows/pallas_call | solution.py:455
  7.8 5.8 %all-to-all-start = ((bf16[8,4,3,4,16,128]{5,4,3,2,1,0:T(8,128)(2,1)}), bf16[8,4,3,4,16,128]{5,4,3,2,1,0:T(8,128)(2,1)S(1)}, u32[]{:S(2)}, u32[]{:S(2)}) async-start(bf16[8,4,3,4,16,128]{5,4,3,2,1,0:T(8,128)(2,1)} %inner_rows.1), calls=%async_computation | async-start | bytes 3145728 | tf_op jit(solution)/shard_map/all_to_all | solution.py:489
  13.6 3.8 %halo_rows.1 = (f32[6,2,16,1152]{3,2,1,0:T(8,128)}, f32[6,2,16,1152]{3,2,1,0:T(8,128)}) custom-call(f32[4,128,1152]{2,1,0:T(8,128)} %bitcast.8, f32[2,128,1152]{2,1,0:T(8,128)} %bitcast.11), custom_call_target="tpu_custom_call" | custom-call | flops 589824 | bytes 4718592 | tf_op jit(solution)/shard_map/halo_rows/pallas_call | solution.py:473
  17.4 1.9 %collective-permute-start = (f32[6,2,16,1152]{3,2,1,0:T(8,128)}, f32[6,2,16,1152]{3,2,1,0:T(8,128)S(1)}, u32[]{:S(2)}, u32[]{:S(2)}) collective-permute-start(f32[6,2,16,1152]{3,2,1,0:T(8,128)} %get-tuple-element.53), channel_id=1, source_target_pairs={{0,8},{8,16},{16,24},{1,9},{9,17},{17,25},{2,10},{10,18},{18,26},{... | collective-permute-start | bytes 2654216 | tf_op jit(solution)/shard_map/ppermute | solution.py:492
  19.4 3.6 %collective-permute-start.1 = (f32[6,2,16,1152]{3,2,1,0:T(8,128)}, f32[6,2,16,1152]{3,2,1,0:T(8,128)S(1)}, u32[]{:S(2)}, u32[]{:S(2)}) collective-permute-start(f32[6,2,16,1152]{3,2,1,0:T(8,128)} %get-tuple-element.54), channel_id=1, source_target_pairs={{8,0},{16,8},{24,16},{9,1},{17,9},{25,17},{10,2},{18,10},{26,18},{... | collective-permute-start | bytes 2654216 | tf_op jit(solution)/shard_map/ppermute | solution.py:493
  23.8 8.2 %collective-permute-done.before_ref = f32[6,2,16,1152]{3,2,1,0:T(8,128)S(1)} collective-permute-done((f32[6,2,16,1152]{3,2,1,0:T(8,128)}, f32[6,2,16,1152]{3,2,1,0:T(8,128)S(1)}, u32[]{:S(2)}, u32[]{:S(2)}) %collective-permute-start) | collective-permute-done | bytes 884768 | tf_op jit(solution)/shard_map/ppermute | solution.py:492
  32.0 1.9 %collective-permute-done.1.after_ref = f32[6,2,16,1152]{3,2,1,0:T(8,128)S(1)} collective-permute-done((f32[6,2,16,1152]{3,2,1,0:T(8,128)}, f32[6,2,16,1152]{3,2,1,0:T(8,128)S(1)}, u32[]{:S(2)}, u32[]{:S(2)}) %collective-permute-start.1) | collective-permute-done | bytes 884768 | tf_op jit(solution)/shard_map/ppermute | solution.py:493
  33.9 0.9 copy-done.2
  34.8 9.9 %edge_rows.1 = (bf16[4,2,4,16,128]{4,3,2,1,0:T(8,128)(2,1)}, bf16[4,2,4,16,128]{4,3,2,1,0:T(8,128)(2,1)}, bf16[4,2,4,16,128]{4,3,2,1,0:T(8,128)(2,1)}, bf16[4,2,...) custom-call(s32[1,8]{1,0:T(1,128)} %counts_ref.3, ...), custom_call_target="tpu_custom_call" | custom-call | flops 47185920 | bytes 5898240 | tf_op jit(solution)/shard_map/edge_rows/pallas_call | solution.py:503
  44.7 2.1 %collective-permute-start.2 = (bf16[4,2,4,16,128]{4,3,2,1,0:T(8,128)(2,1)}, bf16[4,2,4,16,128]{4,3,2,1,0:T(8,128)(2,1)S(1)}, u32[]{:S(2)}, u32[]{:S(2)}) collective-permute-start(bf16[4,2,4,16,128]{4,3,2,1,0:T(8,128)(2,1)} %get-tuple-element.56), channel_id=1, source_target_pairs={{0,1},{1,0},{2,3},{3,2},{4,5},{5,4},{6,7},{7,6},{8,9},{9,8},{10,11... | collective-permute-start | bytes 393224 | tf_op jit(solution)/shard_map/ppermute | solution.py:516
  46.7 1.5 %collective-permute-start.3 = (bf16[4,2,4,16,128]{4,3,2,1,0:T(8,128)(2,1)}, bf16[4,2,4,16,128]{4,3,2,1,0:T(8,128)(2,1)S(1)}, u32[]{:S(2)}, u32[]{:S(2)}) collective-permute-start(bf16[4,2,4,16,128]{4,3,2,1,0:T(8,128)(2,1)} %get-tuple-element.61), channel_id=1, source_target_pairs={{0,2},{1,3},{2,0},{3,1},{4,6},{5,7},{6,4},{7,5},{8,10},{9,11},{10,... | collective-permute-start | bytes 393224 | tf_op jit(solution)/shard_map/ppermute | solution.py:516
  49.5 1.3 %pad_add_fusion.width_ref = s32[2]{0:T(128)} fusion(s32[1]{0:T(128)} %bitcast.1, s32[1]{0:T(128)} %bitcast), kind=kLoop, calls=%fused_computation.1 | loop fusion | flops 2 | bytes 16 | tf_op jit(solution)/shard_map/stack | solution.py:528
  50.9 2.8 %collective-permute-start.5 = (bf16[4,2,4,16,128]{4,3,2,1,0:T(8,128)(2,1)}, bf16[4,2,4,16,128]{4,3,2,1,0:T(8,128)(2,1)S(1)}, u32[]{:S(2)}, u32[]{:S(2)}) collective-permute-start(bf16[4,2,4,16,128]{4,3,2,1,0:T(8,128)(2,1)} %get-tuple-element.69), channel_id=1, source_target_pairs={{0,4},{1,5},{2,6},{3,7},{4,0},{5,1},{6,2},{7,3},{8,12},{9,13},{10,... | collective-permute-start | bytes 393224 | tf_op jit(solution)/shard_map/ppermute | solution.py:516
  53.7 1.5 %collective-permute-start.6 = (bf16[4,2,4,16,128]{4,3,2,1,0:T(8,128)(2,1)}, bf16[4,2,4,16,128]{4,3,2,1,0:T(8,128)(2,1)S(1)}, u32[]{:S(2)}, u32[]{:S(2)}) collective-permute-start(bf16[4,2,4,16,128]{4,3,2,1,0:T(8,128)(2,1)} %get-tuple-element.73), channel_id=1, source_target_pairs={{0,5},{1,4},{2,7},{3,6},{4,1},{5,0},{6,3},{7,2},{8,13},{9,12},{10,... | collective-permute-start | bytes 393224 | tf_op jit(solution)/shard_map/ppermute | solution.py:516
  55.2 3.3 %collective-permute-start.7 = (bf16[4,2,4,16,128]{4,3,2,1,0:T(8,128)(2,1)}, bf16[4,2,4,16,128]{4,3,2,1,0:T(8,128)(2,1)S(1)}, u32[]{:S(2)}, u32[]{:S(2)}) collective-permute-start(bf16[4,2,4,16,128]{4,3,2,1,0:T(8,128)(2,1)} %get-tuple-element.77), channel_id=1, source_target_pairs={{0,6},{1,7},{2,4},{3,5},{4,2},{5,3},{6,0},{7,1},{8,14},{9,15},{10,... | collective-permute-start | bytes 393224 | tf_op jit(solution)/shard_map/ppermute | solution.py:516
  59.3 2.5 %collective-permute-start.8 = (bf16[4,2,4,16,128]{4,3,2,1,0:T(8,128)(2,1)}, bf16[4,2,4,16,128]{4,3,2,1,0:T(8,128)(2,1)S(1)}, u32[]{:S(2)}, u32[]{:S(2)}) collective-permute-start(bf16[4,2,4,16,128]{4,3,2,1,0:T(8,128)(2,1)} %get-tuple-element.81), channel_id=1, source_target_pairs={{0,7},{1,6},{2,5},{3,4},{4,3},{5,2},{6,1},{7,0},{8,15},{9,14},{10,... | collective-permute-start | bytes 393224 | tf_op jit(solution)/shard_map/ppermute | solution.py:516
  61.8 1.1 %copy-done = bf16[8,4,3,4,16,128]{5,4,3,2,1,0:T(8,128)(2,1)} copy-done((bf16[8,4,3,4,16,128]{5,4,3,2,1,0:T(8,128)(2,1)}, bf16[8,4,3,4,16,128]{5,4,3,2,1,0:T(8,128)(2,1)S(1)}, u32[]{:S(2)}) %copy-start) | copy-done | bytes 1572888
  62.9 7.3 %inner_columns.1 = (bf16[4,512,384]{2,1,0:T(8,128)(2,1)}, bf16[512,512]{1,0:T(8,128)(2,1)}, bf16[512,512]{1,0:T(8,128)(2,1)}, bf16[512,512]{1,0:T(8,128)(2,1)}) custom-call(s32[8]{0:T(128)} %convert_element_type.2.listed_ref, s32[2]{0:T(128)} %pad_add_fusion.width_ref, bf16[8,4,3,4,16,128]{5,4,3,2,1,0:T(8,128)(2,1)} %copy-done, bf16[128,128]{1,0:T(8,128)(2,1)} %refs_10_.1, ...), custom_call_target="tpu_custom_call" | custom-call | flops 2617245696 | bytes 3145728 | tf_op jit(solution)/shard_map/inner_columns/pallas_call | solution.py:556
  71.0 3.0 %collective-permute-start.11 = (bf16[4,1,4,16,128]{4,3,2,1,0:T(8,128)(2,1)S(1)}, bf16[4,1,4,16,128]{4,3,2,1,0:T(8,128)(2,1)S(1)}, u32[]{:S(2)}, u32[]{:S(2)}) collective-permute-start(bf16[4,1,4,16,128]{4,3,2,1,0:T(8,128)(2,1)S(1)} %copy-done.23), channel_id=1, source_target_pairs={{0,3},{1,2},{2,1},{3,0},{4,7},{5,6},{6,5},{7,4},{8,11},{9,10},{10,... | collective-permute-start | bytes 196616 | tf_op jit(solution)/shard_map/ppermute | solution.py:516
  74.1 2.9 %collective-permute-start.13 = (bf16[4,1,4,16,128]{4,3,2,1,0:T(8,128)(2,1)S(1)}, bf16[4,1,4,16,128]{4,3,2,1,0:T(8,128)(2,1)S(1)}, u32[]{:S(2)}, u32[]{:S(2)}) collective-permute-start(bf16[4,1,4,16,128]{4,3,2,1,0:T(8,128)(2,1)S(1)} %copy-done.21), channel_id=1, source_target_pairs={{0,5},{1,4},{2,7},{3,6},{4,1},{5,0},{6,3},{7,2},{8,13},{9,12},{10,... | collective-permute-start | bytes 196616 | tf_op jit(solution)/shard_map/ppermute | solution.py:516
  77.0 2.4 %collective-permute-start.14 = (bf16[4,1,4,16,128]{4,3,2,1,0:T(8,128)(2,1)S(1)}, bf16[4,1,4,16,128]{4,3,2,1,0:T(8,128)(2,1)S(1)}, u32[]{:S(2)}, u32[]{:S(2)}) collective-permute-start(bf16[4,1,4,16,128]{4,3,2,1,0:T(8,128)(2,1)S(1)} %copy-done.20), channel_id=1, source_target_pairs={{0,6},{1,7},{2,4},{3,5},{4,2},{5,3},{6,0},{7,1},{8,14},{9,15},{10,... | collective-permute-start | bytes 196616 | tf_op jit(solution)/shard_map/ppermute | solution.py:516
  79.4 2.5 %collective-permute-start.15 = (bf16[4,1,4,16,128]{4,3,2,1,0:T(8,128)(2,1)S(1)}, bf16[4,1,4,16,128]{4,3,2,1,0:T(8,128)(2,1)S(1)}, u32[]{:S(2)}, u32[]{:S(2)}) collective-permute-start(bf16[4,1,4,16,128]{4,3,2,1,0:T(8,128)(2,1)S(1)} %copy-done.19), channel_id=1, source_target_pairs={{0,7},{1,6},{2,5},{3,4},{4,3},{5,2},{6,1},{7,0},{8,15},{9,14},{10,... | collective-permute-start | bytes 196616 | tf_op jit(solution)/shard_map/ppermute | solution.py:516
  81.9 6.5 %edge_columns.2.refs_0_ = bf16[512,8,384]{2,1,0:T(8,128)(2,1)} custom-call(s32[8]{0:T(128)} %convert_element_type.2.listed_ref, s32[2]{0:T(128)} %pad_add_fusion.width_ref, bf16[4,2,4,16,128]{4,3,2,1,0:T(8,128)(2,1)} %get-tuple-element.55.refs_0_, bf16[4,2,4,16,128]{4,3,2,1,0:T(8,128)(2,1)} %copy-done.3, bf16[4,2,4,16,128]{4,3,2,1,0:T(8,128)(2,1)} %copy-done.4, ...), custom_call_target="tpu_custom_call" | custom-call | flops 1744830464 | bytes 2097152 | tf_op jit(solution)/shard_map/edge_columns/pallas_call | solution.py:589
  89.2 4.6 %edge_columns.3 = bf16[512,8,384]{2,1,0:T(8,128)(2,1)} custom-call(s32[8]{0:T(128)} %convert_element_type.2.listed_ref, s32[2]{0:T(128)} %pad_add_fusion.width_ref, bf16[512,8,384]{2,1,0:T(8,128)(2,1)} %edge_columns.2.refs_0_, bf16[4,1,4,16,128]{4,3,2,1,0:T(8,128)(2,1)} %get-tuple-element.89.refs_1_, ...), custom_call_target="tpu_custom_call", output_to_operand_aliasing={{}: (2, {})} | custom-call | flops 872415232 | bytes 1048576 | tf_op jit(solution)/shard_map/edge_columns/pallas_call | solution.py:589
  (75 shorter events, 4.4 us)
Async XLA Ops:
  7.8 54.0 %all-to-all-start = ((bf16[8,4,3,4,16,128]{5,4,3,2,1,0:T(8,128)(2,1)}), bf16[8,4,3,4,16,128]{5,4,3,2,1,0:T(8,128)(2,1)S(1)}, u32[]{:S(2)}, u32[]{:S(2)}) async-start(bf16[8,4,3,4,16,128]{5,4,3,2,1,0:T(8,128)(2,1)} %inner_rows.1), calls=%async_computation | async-start | bytes 3145728 | tf_op jit(solution)/shard_map/all_to_all | solution.py:489
  17.4 14.6 %collective-permute-start = (f32[6,2,16,1152]{3,2,1,0:T(8,128)}, f32[6,2,16,1152]{3,2,1,0:T(8,128)S(1)}, u32[]{:S(2)}, u32[]{:S(2)}) collective-permute-start(f32[6,2,16,1152]{3,2,1,0:T(8,128)} %get-tuple-element.53), channel_id=1, source_target_pairs={{0,8},{8,16},{16,24},{1,9},{9,17},{17,25},{2,10},{10,18},{18,26},{... | collective-permute-start | bytes 2654216 | tf_op jit(solution)/shard_map/ppermute | solution.py:492
  19.4 14.5 %collective-permute-start.1 = (f32[6,2,16,1152]{3,2,1,0:T(8,128)}, f32[6,2,16,1152]{3,2,1,0:T(8,128)S(1)}, u32[]{:S(2)}, u32[]{:S(2)}) collective-permute-start(f32[6,2,16,1152]{3,2,1,0:T(8,128)} %get-tuple-element.54), channel_id=1, source_target_pairs={{8,0},{16,8},{24,16},{9,1},{17,9},{25,17},{10,2},{18,10},{26,18},{... | collective-permute-start | bytes 2654216 | tf_op jit(solution)/shard_map/ppermute | solution.py:493
  23.8 24.5 %copy-start.18 = (s32[1,8]{1,0:T(1,128)S(1)}, s32[1,8]{1,0:T(1,128)}, u32[]{:S(2)}) copy-start(s32[1,8]{1,0:T(1,128)} %counts_ref.3) | copy-start | bytes 100
  44.7 10.5 %collective-permute-start.2 = (bf16[4,2,4,16,128]{4,3,2,1,0:T(8,128)(2,1)}, bf16[4,2,4,16,128]{4,3,2,1,0:T(8,128)(2,1)S(1)}, u32[]{:S(2)}, u32[]{:S(2)}) collective-permute-start(bf16[4,2,4,16,128]{4,3,2,1,0:T(8,128)(2,1)} %get-tuple-element.56), channel_id=1, source_target_pairs={{0,1},{1,0},{2,3},{3,2},{4,5},{5,4},{6,7},{7,6},{8,9},{9,8},{10,11... | collective-permute-start | bytes 393224 | tf_op jit(solution)/shard_map/ppermute | solution.py:516
  46.7 12.5 %collective-permute-start.3 = (bf16[4,2,4,16,128]{4,3,2,1,0:T(8,128)(2,1)}, bf16[4,2,4,16,128]{4,3,2,1,0:T(8,128)(2,1)S(1)}, u32[]{:S(2)}, u32[]{:S(2)}) collective-permute-start(bf16[4,2,4,16,128]{4,3,2,1,0:T(8,128)(2,1)} %get-tuple-element.61), channel_id=1, source_target_pairs={{0,2},{1,3},{2,0},{3,1},{4,6},{5,7},{6,4},{7,5},{8,10},{9,11},{10,... | collective-permute-start | bytes 393224 | tf_op jit(solution)/shard_map/ppermute | solution.py:516
  50.8 19.5 %collective-permute-start.4 = (bf16[4,2,4,16,128]{4,3,2,1,0:T(8,128)(2,1)}, bf16[4,2,4,16,128]{4,3,2,1,0:T(8,128)(2,1)S(1)}, u32[]{:S(2)}, u32[]{:S(2)}) collective-permute-start(bf16[4,2,4,16,128]{4,3,2,1,0:T(8,128)(2,1)} %get-tuple-element.65), channel_id=1, source_target_pairs={{0,3},{1,2},{2,1},{3,0},{4,7},{5,6},{6,5},{7,4},{8,11},{9,10},{10,... | collective-permute-start | bytes 393224 | tf_op jit(solution)/shard_map/ppermute | solution.py:516
  50.9 20.1 %collective-permute-start.5 = (bf16[4,2,4,16,128]{4,3,2,1,0:T(8,128)(2,1)}, bf16[4,2,4,16,128]{4,3,2,1,0:T(8,128)(2,1)S(1)}, u32[]{:S(2)}, u32[]{:S(2)}) collective-permute-start(bf16[4,2,4,16,128]{4,3,2,1,0:T(8,128)(2,1)} %get-tuple-element.69), channel_id=1, source_target_pairs={{0,4},{1,5},{2,6},{3,7},{4,0},{5,1},{6,2},{7,3},{8,12},{9,13},{10,... | collective-permute-start | bytes 393224 | tf_op jit(solution)/shard_map/ppermute | solution.py:516
  53.7 17.3 %collective-permute-start.6 = (bf16[4,2,4,16,128]{4,3,2,1,0:T(8,128)(2,1)}, bf16[4,2,4,16,128]{4,3,2,1,0:T(8,128)(2,1)S(1)}, u32[]{:S(2)}, u32[]{:S(2)}) collective-permute-start(bf16[4,2,4,16,128]{4,3,2,1,0:T(8,128)(2,1)} %get-tuple-element.73), channel_id=1, source_target_pairs={{0,5},{1,4},{2,7},{3,6},{4,1},{5,0},{6,3},{7,2},{8,13},{9,12},{10,... | collective-permute-start | bytes 393224 | tf_op jit(solution)/shard_map/ppermute | solution.py:516
  55.2 15.1 %copy-start.3 = (bf16[4,2,4,16,128]{4,3,2,1,0:T(8,128)(2,1)}, bf16[4,2,4,16,128]{4,3,2,1,0:T(8,128)(2,1)S(1)}, u32[]{:S(2)}) copy-start(bf16[4,2,4,16,128]{4,3,2,1,0:T(8,128)(2,1)S(1)} %collective-permute-done.2.refs_1_) | copy-start | bytes 393220
  55.2 18.8 %collective-permute-start.7 = (bf16[4,2,4,16,128]{4,3,2,1,0:T(8,128)(2,1)}, bf16[4,2,4,16,128]{4,3,2,1,0:T(8,128)(2,1)S(1)}, u32[]{:S(2)}, u32[]{:S(2)}) collective-permute-start(bf16[4,2,4,16,128]{4,3,2,1,0:T(8,128)(2,1)} %get-tuple-element.77), channel_id=1, source_target_pairs={{0,6},{1,7},{2,4},{3,5},{4,2},{5,3},{6,0},{7,1},{8,14},{9,15},{10,... | collective-permute-start | bytes 393224 | tf_op jit(solution)/shard_map/ppermute | solution.py:516
  59.2 11.8 %copy-start.23 = (bf16[4,1,4,16,128]{4,3,2,1,0:T(8,128)(2,1)S(1)}, bf16[4,1,4,16,128]{4,3,2,1,0:T(8,128)(2,1)}, u32[]{:S(2)}) copy-start(bf16[4,1,4,16,128]{4,3,2,1,0:T(8,128)(2,1)} %get-tuple-element.92) | copy-start | bytes 196612
  59.2 14.7 %copy-start.22 = (bf16[4,1,4,16,128]{4,3,2,1,0:T(8,128)(2,1)S(1)}, bf16[4,1,4,16,128]{4,3,2,1,0:T(8,128)(2,1)}, u32[]{:S(2)}) copy-start(bf16[4,1,4,16,128]{4,3,2,1,0:T(8,128)(2,1)} %get-tuple-element.93) | copy-start | bytes 196612
  59.2 14.8 %copy-start.21 = (bf16[4,1,4,16,128]{4,3,2,1,0:T(8,128)(2,1)S(1)}, bf16[4,1,4,16,128]{4,3,2,1,0:T(8,128)(2,1)}, u32[]{:S(2)}) copy-start(bf16[4,1,4,16,128]{4,3,2,1,0:T(8,128)(2,1)} %get-tuple-element.94) | copy-start | bytes 196612
  59.3 17.8 %copy-start.20 = (bf16[4,1,4,16,128]{4,3,2,1,0:T(8,128)(2,1)S(1)}, bf16[4,1,4,16,128]{4,3,2,1,0:T(8,128)(2,1)}, u32[]{:S(2)}) copy-start(bf16[4,1,4,16,128]{4,3,2,1,0:T(8,128)(2,1)} %get-tuple-element.95) | copy-start | bytes 196612
  59.3 20.2 %copy-start.19 = (bf16[4,1,4,16,128]{4,3,2,1,0:T(8,128)(2,1)S(1)}, bf16[4,1,4,16,128]{4,3,2,1,0:T(8,128)(2,1)}, u32[]{:S(2)}) copy-start(bf16[4,1,4,16,128]{4,3,2,1,0:T(8,128)(2,1)} %get-tuple-element.96) | copy-start | bytes 196612
  59.3 14.8 %collective-permute-start.8 = (bf16[4,2,4,16,128]{4,3,2,1,0:T(8,128)(2,1)}, bf16[4,2,4,16,128]{4,3,2,1,0:T(8,128)(2,1)S(1)}, u32[]{:S(2)}, u32[]{:S(2)}) collective-permute-start(bf16[4,2,4,16,128]{4,3,2,1,0:T(8,128)(2,1)} %get-tuple-element.81), channel_id=1, source_target_pairs={{0,7},{1,6},{2,5},{3,4},{4,3},{5,2},{6,1},{7,0},{8,15},{9,14},{10,... | collective-permute-start | bytes 393224 | tf_op jit(solution)/shard_map/ppermute | solution.py:516
  70.3 6.8 %collective-permute-start.9 = (bf16[4,1,4,16,128]{4,3,2,1,0:T(8,128)(2,1)S(1)}, bf16[4,1,4,16,128]{4,3,2,1,0:T(8,128)(2,1)S(1)}, u32[]{:S(2)}, u32[]{:S(2)}) collective-permute-start(bf16[4,1,4,16,128]{4,3,2,1,0:T(8,128)(2,1)S(1)} %copy-done.25), channel_id=1, source_target_pairs={{0,1},{1,0},{2,3},{3,2},{4,5},{5,4},{6,7},{7,6},{8,9},{9,8},{10,11... | collective-permute-start | bytes 196616 | tf_op jit(solution)/shard_map/ppermute | solution.py:516
  70.9 8.5 %collective-permute-start.10 = (bf16[4,1,4,16,128]{4,3,2,1,0:T(8,128)(2,1)S(1)}, bf16[4,1,4,16,128]{4,3,2,1,0:T(8,128)(2,1)S(1)}, u32[]{:S(2)}, u32[]{:S(2)}) collective-permute-start(bf16[4,1,4,16,128]{4,3,2,1,0:T(8,128)(2,1)S(1)} %copy-done.24), channel_id=1, source_target_pairs={{0,2},{1,3},{2,0},{3,1},{4,6},{5,7},{6,4},{7,5},{8,10},{9,11},{10,... | collective-permute-start | bytes 196616 | tf_op jit(solution)/shard_map/ppermute | solution.py:516
  71.0 17.5 %collective-permute-start.11 = (bf16[4,1,4,16,128]{4,3,2,1,0:T(8,128)(2,1)S(1)}, bf16[4,1,4,16,128]{4,3,2,1,0:T(8,128)(2,1)S(1)}, u32[]{:S(2)}, u32[]{:S(2)}) collective-permute-start(bf16[4,1,4,16,128]{4,3,2,1,0:T(8,128)(2,1)S(1)} %copy-done.23), channel_id=1, source_target_pairs={{0,3},{1,2},{2,1},{3,0},{4,7},{5,6},{6,5},{7,4},{8,11},{9,10},{10,... | collective-permute-start | bytes 196616 | tf_op jit(solution)/shard_map/ppermute | solution.py:516
  74.0 14.5 %collective-permute-start.12 = (bf16[4,1,4,16,128]{4,3,2,1,0:T(8,128)(2,1)S(1)}, bf16[4,1,4,16,128]{4,3,2,1,0:T(8,128)(2,1)S(1)}, u32[]{:S(2)}, u32[]{:S(2)}) collective-permute-start(bf16[4,1,4,16,128]{4,3,2,1,0:T(8,128)(2,1)S(1)} %copy-done.22), channel_id=1, source_target_pairs={{0,4},{1,5},{2,6},{3,7},{4,0},{5,1},{6,2},{7,3},{8,12},{9,13},{10,... | collective-permute-start | bytes 196616 | tf_op jit(solution)/shard_map/ppermute | solution.py:516
  74.1 14.4 %collective-permute-start.13 = (bf16[4,1,4,16,128]{4,3,2,1,0:T(8,128)(2,1)S(1)}, bf16[4,1,4,16,128]{4,3,2,1,0:T(8,128)(2,1)S(1)}, u32[]{:S(2)}, u32[]{:S(2)}) collective-permute-start(bf16[4,1,4,16,128]{4,3,2,1,0:T(8,128)(2,1)S(1)} %copy-done.21), channel_id=1, source_target_pairs={{0,5},{1,4},{2,7},{3,6},{4,1},{5,0},{6,3},{7,2},{8,13},{9,12},{10,... | collective-permute-start | bytes 196616 | tf_op jit(solution)/shard_map/ppermute | solution.py:516
  77.0 11.5 %collective-permute-start.14 = (bf16[4,1,4,16,128]{4,3,2,1,0:T(8,128)(2,1)S(1)}, bf16[4,1,4,16,128]{4,3,2,1,0:T(8,128)(2,1)S(1)}, u32[]{:S(2)}, u32[]{:S(2)}) collective-permute-start(bf16[4,1,4,16,128]{4,3,2,1,0:T(8,128)(2,1)S(1)} %copy-done.20), channel_id=1, source_target_pairs={{0,6},{1,7},{2,4},{3,5},{4,2},{5,3},{6,0},{7,1},{8,14},{9,15},{10,... | collective-permute-start | bytes 196616 | tf_op jit(solution)/shard_map/ppermute | solution.py:516
  79.4 9.2 %collective-permute-start.15 = (bf16[4,1,4,16,128]{4,3,2,1,0:T(8,128)(2,1)S(1)}, bf16[4,1,4,16,128]{4,3,2,1,0:T(8,128)(2,1)S(1)}, u32[]{:S(2)}, u32[]{:S(2)}) collective-permute-start(bf16[4,1,4,16,128]{4,3,2,1,0:T(8,128)(2,1)S(1)} %copy-done.19), channel_id=1, source_target_pairs={{0,7},{1,6},{2,5},{3,4},{4,3},{5,2},{6,1},{7,0},{8,15},{9,14},{10,... | collective-permute-start | bytes 196616 | tf_op jit(solution)/shard_map/ppermute | solution.py:516
  (19 other events, 120.0 us)

commit v3 on v2

--- a/solution.py
+++ b/solution.py
@@ -205,30 +205,30 @@
     wait = start_grid(fields_ref, winds_ref, grid_ref, sems)
     for array in (fields, fields + 1) + tuple(range(fields)):
         wait(array)
-        for group in range(levels // size):
-            place = pl.ds(group * size, size)
-            for row in range(HALO):
-                last = rows - HALO + row
-                first_ref[array, row, place, :] = load_row(grid_ref, array, row, group, size, rows)
-                last_ref[array, row, place, :] = load_row(grid_ref, array, last, group, size, rows)
+        for row in range(HALO):
+            for ref, source in ((first_ref, row), (last_ref, rows - HALO + row)):
+                value = [
+                    load_row(grid_ref, array, source, group, size, rows)
+                    for group in range(levels // size)
+                ]
+                ref[array, row] = jnp.concatenate(value, axis=0).astype(ref.dtype)
 
 
 def edge_kernel(
     rows,
-    split,
+    by_turn,
     counts_ref,
-    place_ref,
     fields_ref,
     winds_ref,
     before_ref,
     after_ref,
     *refs,
 ):
-    outs, (grid_ref, north_ref, east_ref, kept_ref, sems, start_ref) = refs[:-6], refs[-6:]
-    early_refs, late_refs = outs[: len(outs) // 2], outs[len(outs) // 2 :]
+    outs, scratch = refs[:-7], refs[-7:]
+    grid_ref, north_ref, east_ref, kept_ref, sems, start_ref, halo_ref = scratch
     fields = fields_ref.shape[0]
     owners = start_ref.shape[0]
-    blocks = split + late_refs[0].shape[-4]
+    blocks = outs[0].shape[-4]
     levels = before_ref.shape[2]
     size = min(8, levels)
     groups = levels // size
@@ -239,19 +239,24 @@
     count = 3 * HALO
 
     def run(array, group, top):
-        place = pl.ds(group * size, size)
         own = range(2 * HALO) if top else range(rows - 2 * HALO, rows)
         own = [load_row(grid_ref, array, row, group, size, rows) for row in own]
-        if top:
-            return [before_ref[array, row, place, :] for row in range(HALO)] + own
-        return own + [after_ref[array, row, place, :] for row in range(HALO)]
+        place = pl.ds(group * size, size)
+        halo = [halo_ref[int(top), array, row, place, :] for row in range(HALO)]
+        return halo + own if top else own + halo
+
+    for side, ref in enumerate((after_ref, before_ref)):
+        for array in range(fields + 2):
+            for row in range(HALO):
+                halo_ref[side, array, row] = ref[array, row].astype(jnp.float32)
 
     wait(fields)
     wait(fields + 1)
     for top in (True, False):
         north_side, east_side = north_ref.at[int(top)], east_ref.at[int(top)]
         wall = HALO if top else count - HALO
-        is_open = jnp.where(place_ref[0 if top else 1] == 1, 0.0, 1.0)
+        band = lax.axis_index("lat")
+        is_open = jnp.where(band == (0 if top else lax.axis_size("lat") - 1), 0.0, 1.0)
 
         def weights(group, carry):
             store_weights(
@@ -288,16 +293,13 @@
         lax.fori_loop(0, groups, one_group, 0)
 
         def store(slot, block, row, value):
-            if block < split:
-                early_refs[slot][field, block, row] = value
-            elif early_refs:
-                late_refs[slot][field, block - split, row] = value
+            if by_turn:
+                outs[slot][field, block, row] = value
             else:
-                late_refs[0][slot, field, block, row] = value
-
-        slots = [start_ref[place_ref[2] ^ turn] for turn in range(owners)]
-        if not early_refs:
-            slots = [start_ref[owner] for owner in range(owners)]
+                outs[0][slot, field, block, row] = value
+
+        own = lax.axis_index("lev") if by_turn else 0
+        slots = [start_ref[own ^ turn] for turn in range(owners)]
         pack_rows(kept_ref, slots, blocks, store)
         return carry
 
@@ -345,19 +347,28 @@
 
 def finished_row(remapped, tendency, listed, index, live):
     lanes = slice(index * LANES, (index + 1) * LANES)
-    updated = remapped[:, lanes] + jnp.where(listed == 1, tendency[:, lanes], 0.0)
+    updated = remapped[:, lanes] + jnp.where(listed, tendency[:, lanes], 0.0)
     return jnp.where(live, updated, 0.0)
 
 
-def live_lanes(width_ref, features, block):
+def live_lanes(counts_ref, features, block):
     lane = lax.broadcasted_iota(jnp.int32, (features, LANES), 1)
-    return lane + block * LANES < width_ref[0]
+    return lane + block * LANES < counts_ref[0, lax.axis_index("lev")]
+
+
+def is_listed(groups_ref, row):
+    found = jnp.bool_(False)
+    for owner in range(groups_ref.shape[0]):
+        for index in range(groups_ref.shape[1]):
+            found = found | (groups_ref[owner, index] == row)
+    return found
 
 
 def half_kernel(
+    rows,
     row_list,
-    listed_ref,
-    width_ref,
+    groups_ref,
+    counts_ref,
     block_ref,
     remap_ref,
     first_ref,
@@ -382,35 +393,38 @@
         second_out,
         third_out,
     )
-    live = live_lanes(width_ref, remapped.shape[0], pl.program_id(0))
+    live = live_lanes(counts_ref, remapped.shape[0], pl.program_id(0))
+    first_row = lax.axis_index("lat") * rows
     for index, row in enumerate(row_list):
-        out_ref[index] = finished_row(remapped, tendency, listed_ref[row], index, live).astype(
-            jnp.bfloat16
-        )
-
-
-def last_kernel(row_list, done_list, base, turns, listed_ref, width_ref, *refs):
+        listed = is_listed(groups_ref, first_row + row)
+        updated = finished_row(remapped, tendency, listed, index, live)
+        out_ref[index] = updated.astype(jnp.bfloat16)
+
+
+def last_kernel(row_list, done_list, by_turn, groups_ref, counts_ref, *refs):
     *refs, done_ref, remap_ref, first_ref, second_ref, third_ref, out_ref, tiles_ref, sorted_ref = (
         refs
     )
     features, rows, _ = out_ref.shape
     fields = sorted_ref.shape[0]
-    if turns:
-        sort_turns(width_ref[1], refs[-turns:], sorted_ref)
+    if by_turn:
+        sort_turns(lax.axis_index("lev"), refs, sorted_ref)
 
         def columns(field):
             return sorted_ref[field]
     else:
-        columns = functools.partial(gathered, refs[-1])
+        columns = functools.partial(gathered, refs[0])
     remapped, tendency = column_update(
         columns, fields, remap_ref, first_ref, second_ref, third_ref
     )
-    live = live_lanes(width_ref, features, pl.program_id(0) + base)
+    live = live_lanes(counts_ref, features, pl.program_id(0))
+    first_row = lax.axis_index("lat") * rows
     for index, row in enumerate(done_list):
         tiles_ref[pl.ds(row, features, stride=rows), :] = done_ref[index].astype(jnp.float32)
     for index, row in enumerate(row_list):
+        listed = is_listed(groups_ref, first_row + row)
         tiles_ref[pl.ds(row, features, stride=rows), :] = finished_row(
-            remapped, tendency, listed_ref[row], index, live
+            remapped, tendency, listed, index, live
         )
     out_ref[...] = tiles_ref[...].reshape(features, rows, LANES).astype(jnp.bfloat16)
 
@@ -418,14 +432,11 @@
 def shards(fields, winds, remap_weight, w_first, w_second, w_third, lon_counts, group_list):
     field_count, level_count, lat_rows, lon_total = fields.shape
     band_count = lax.axis_size("lat")
-    band_index = lax.axis_index("lat")
     owner_count = lax.axis_size("lev")
-    first_row = band_index * lat_rows
     all_levels = level_count * owner_count
     features = field_count * all_levels
     blocks = (2 * lon_total // owner_count + LANES - 1) // LANES
     slot_width = blocks * LANES
-    split = blocks - 1
     inner_rows = tuple(range(HALO, lat_rows - HALO))
     edge_rows = tuple(range(HALO)) + tuple(range(lat_rows - HALO, lat_rows))
     half = len(inner_rows)
@@ -434,6 +445,7 @@
     smem = pl.BlockSpec(memory_space=pltpu.SMEM)
     anywhere = pl.BlockSpec(memory_space=pl.ANY)
     params = pltpu.CompilerParams(vmem_limit_bytes=60 * MIB)
+    light = pltpu.CompilerParams(vmem_limit_bytes=24 * MIB)
     values = field_count * level_count * lat_rows * lon_total
 
     def payload(count):
@@ -441,7 +453,7 @@
 
     flat_fields = fields.reshape(field_count, level_count * lat_rows, lon_total)
     flat_winds = winds.reshape(2, level_count * lat_rows, lon_total)
-    halo_shape = jax.ShapeDtypeStruct((stacked, HALO, level_count, lon_total), jnp.float32)
+    halo_shape = jax.ShapeDtypeStruct((stacked, HALO, level_count, lon_total), jnp.bfloat16)
 
     def scratch(sides, count):
         return [
@@ -492,40 +504,31 @@
     before = lax.ppermute(last, "lat", up)
     after = lax.ppermute(first, "lat", down)
 
-    own = lax.axis_index("lev")
-    place = jnp.stack([band_index == 0, band_index == band_count - 1, own]).astype(jnp.int32)
-    by_turn = split > 0
-    if by_turn:
-        edge_shapes = [payload(split)[1:]] * owner_count
-        edge_shapes += [payload(blocks - split)[1:]] * owner_count
-    else:
-        edge_shapes = [payload(blocks)]
+    by_turn = owner_count == 8
+    edge_shapes = [payload(blocks)[1:]] * owner_count if by_turn else [payload(blocks)]
     edge = pl.pallas_call(
-        functools.partial(edge_kernel, lat_rows, split),
-        in_specs=[smem, smem, anywhere, anywhere] + [pl.BlockSpec(memory_space=pltpu.VMEM)] * 2,
+        functools.partial(edge_kernel, lat_rows, by_turn),
+        in_specs=[smem, anywhere, anywhere] + [pl.BlockSpec(memory_space=pltpu.VMEM)] * 2,
         out_shape=[jax.ShapeDtypeStruct(shape, jnp.bfloat16) for shape in edge_shapes],
-        scratch_shapes=scratch((2,), 3 * HALO) + [pltpu.SMEM((owner_count,), jnp.int32)],
+        scratch_shapes=scratch((2,), 3 * HALO)
+        + [
+            pltpu.SMEM((owner_count,), jnp.int32),
+            pltpu.VMEM((2,) + halo_shape.shape, jnp.float32),
+        ],
         compiler_params=params,
         cost_estimate=pl.CostEstimate(
             flops=80 * values, bytes_accessed=10 * values, transcendentals=0
         ),
         name="edge_rows",
-    )(lon_counts, place, late_fields, late_winds, before, after)
-
-    def turned_exchange(x, turn):
-        return lax.ppermute(x, "lev", [(i, i ^ turn) for i in range(owner_count)]) if turn else x
+    )(lon_counts, late_fields, late_winds, before, after)
 
     if by_turn:
-        early, late = list(edge[:owner_count]), list(edge[owner_count:])
-        early = [turned_exchange(x, turn) for turn, x in enumerate(early)]
+        edge = [
+            lax.ppermute(x, "lev", [(i, i ^ turn) for i in range(owner_count)]) if turn else x
+            for turn, x in enumerate(edge)
+        ]
     else:
-        early, late = [], edge
-
-    listed = jnp.any(
-        group_list[:, :, None] == (first_row + jnp.arange(lat_rows, dtype=jnp.int32))[None, None, :],
-        axis=(0, 1),
-    ).astype(jnp.int32)
-    width = jnp.stack([lon_counts[0][own], own]).astype(jnp.int32)
+        edge = [exchange(edge[0])]
 
     def by_level(block):
         if level_count % 16 == 0:
@@ -551,61 +554,45 @@
         )
 
     weights = (w_first, w_second, w_third)
-    weight_specs = [whole(w.shape) for w in (remap_weight,) + weights]
+    weight_specs = [pl.BlockSpec(memory_space=pltpu.VMEM)] * 4
     inner_block = by_level(inner_block)
     done, *turned = pl.pallas_call(
-        functools.partial(half_kernel, inner_rows),
+        functools.partial(half_kernel, lat_rows, inner_rows),
         grid=(blocks,),
         in_specs=[smem, smem, block_spec(inner_block)] + weight_specs,
         out_specs=[pl.BlockSpec((half, features, LANES), lambda i: (0, 0, i))]
         + [whole(w.shape[::-1]) for w in weights],
         out_shape=[jax.ShapeDtypeStruct((half, features, slot_width), jnp.bfloat16)]
         + [jax.ShapeDtypeStruct(w.shape[::-1], w.dtype) for w in weights],
-        compiler_params=params,
+        compiler_params=light,
         cost_estimate=cost(blocks),
         name="inner_columns",
-    )(listed, width, inner_block, remap_weight, *weights)
+    )(group_list, lon_counts, inner_block, remap_weight, *weights)
 
     if by_turn:
-        for turn in range(1, owner_count):
-            early[turn], late[turn], done = lax.optimization_barrier(
-                (early[turn], late[turn], done)
-            )
-        late = [turned_exchange(x, turn) for turn, x in enumerate(late)]
+        edge_specs = [
+            pl.BlockSpec((field_count, 1, half, level_count, LANES), lambda i: (0, i, 0, 0, 0))
+        ] * owner_count
     else:
-        late = [by_level(exchange(late[0]))]
-    out = None
-    base = 0
-    for part in ([early] if early else []) + [late]:
-        turns = len(part) if by_turn else 0
-        count = part[0].shape[1 if turns else 2]
-        offset = base
-        if turns:
-            specs = [
-                pl.BlockSpec((field_count, 1, half, level_count, LANES), lambda i: (0, i, 0, 0, 0))
-            ] * len(part)
-        else:
-            specs = [block_spec(part[0])]
-        out = pl.pallas_call(
-            functools.partial(last_kernel, edge_rows, inner_rows, offset, turns),
-            grid=(count,),
-            in_specs=[smem, smem]
-            + [anywhere] * (base > 0)
-            + specs
-            + [pl.BlockSpec((half, features, LANES), lambda i, o=offset: (0, 0, i + o))]
-            + weight_specs,
-            out_specs=pl.BlockSpec((features, lat_rows, LANES), lambda i, o=offset: (0, 0, i + o)),
-            out_shape=jax.ShapeDtypeStruct((features, lat_rows, slot_width), jnp.bfloat16),
-            scratch_shapes=[
-                pltpu.VMEM((features * lat_rows, LANES), jnp.float32),
-                pltpu.VMEM((field_count, all_levels, half * LANES), jnp.bfloat16),
-            ],
-            input_output_aliases={2: 0} if base > 0 else {},
-            compiler_params=params,
-            cost_estimate=cost(count),
-            name="edge_columns",
-        )(listed, width, *([out] if base > 0 else []), *part, done, remap_weight, *turned)
-        base += count
+        edge = [by_level(edge[0])]
+        edge_specs = [block_spec(edge[0])]
+    out = pl.pallas_call(
+        functools.partial(last_kernel, edge_rows, inner_rows, by_turn),
+        grid=(blocks,),
+        in_specs=[smem, smem]
+        + edge_specs
+        + [pl.BlockSpec((half, features, LANES), lambda i: (0, 0, i))]
+        + weight_specs,
+        out_specs=pl.BlockSpec((features, lat_rows, LANES), lambda i: (0, 0, i)),
+        out_shape=jax.ShapeDtypeStruct((features, lat_rows, slot_width), jnp.bfloat16),
+        scratch_shapes=[
+            pltpu.VMEM((features * lat_rows, LANES), jnp.float32),
+            pltpu.VMEM((field_count, all_levels, half * LANES), jnp.bfloat16),
+        ],
+        compiler_params=light,
+        cost_estimate=cost(blocks),
+        name="edge_columns",
+    )(group_list, lon_counts, *edge, done, remap_weight, *turned)
     return out.reshape(field_count, all_levels, lat_rows, slot_width)
 
 

time: 94.2 us -> 93.3 us (level)
  the two profiles are of different devices: /device:TPU:4 before, /device:TPU:8 now
where the time goes in v3:
time: 93.3 us; the launch traced here: 92.9 us
  waiting for transfers between devices  36.5 us (39%)
  Pallas kernels  34.5 us (37%)
  starting transfers between devices  20.3 us (22%)
  local copies, waits for them, and re-layouts  1.47 us (2%)
    ppermute x7, waiting for transfers between devices, shards(): lax.ppermute(x, 'lev', [(i, i ^ turn) for i in range(owner_count)])  25.7 us
    ppermute x7, starting transfers between devices, shards(): lax.ppermute(x, 'lev', [(i, i ^ turn) for i in range(owner_count)])  11.3 us
    pallas_call x1, Pallas kernels, shards(): pl.pallas_call(functools.partial(edge_kernel, lat_rows, by_turn), in_spec...  9.64 us
    pallas_call x1, Pallas kernels, shards(): pl.pallas_call(functools.partial(inner_kernel, lat_rows), in_specs=[smem,...  7.8 us
    pallas_call x1, Pallas kernels, shards(): pl.pallas_call(functools.partial(last_kernel, edge_rows, inner_rows, by_t...  7.72 us
    all_to_all x1, waiting for transfers between devices, exchange(): return lax.all_to_all(x, 'lev', split_axis=0, concat_axis=0, tiled=True)  6.39 us
    all_to_all x1, starting transfers between devices, exchange(): return lax.all_to_all(x, 'lev', split_axis=0, concat_axis=0, tiled=True)  6.26 us
    pallas_call x1, Pallas kernels, shards(): pl.pallas_call(functools.partial(half_kernel, lat_rows, inner_rows), grid...  5.87 us
  transfers between devices with their start and end apart: 10, of which 7 were waited for; matrix products, arithmetic and copies ran while one was open for 0% of the time, Pallas kernels for 20%

profile of v3, /device:TPU:8, one launch (start us, length us, event | category | flops | bytes accessed | tf_op | source)
XLA Modules:
  0.0 92.9 jit_solution(2903570335351668746)
XLA Ops:
  0.0 7.8 %inner_rows.1 = bf16[8,4,3,4,16,128]{5,4,3,2,1,0:T(8,128)(2,1)} custom-call(s32[1,8]{1,0:T(1,128)} %counts_ref.7, f32[4,128,1152]{2,1,0:T(8,128)} %bitcast.3, f32[2,128,1152]{2,1,0:T(8,128)} %bitcast.6), custom_call_target="tpu_custom_call" | custom-call | flops 23592960 | bytes 4718592 | tf_op jit(solution)/shard_map/inner_rows/pallas_call | solution.py:467
  7.8 6.3 %all-to-all-start = ((bf16[8,4,3,4,16,128]{5,4,3,2,1,0:T(8,128)(2,1)}), bf16[8,4,3,4,16,128]{5,4,3,2,1,0:T(8,128)(2,1)S(1)}, u32[]{:S(2)}, u32[]{:S(2)}) async-start(bf16[8,4,3,4,16,128]{5,4,3,2,1,0:T(8,128)(2,1)} %inner_rows.1), calls=%async_computation | async-start | bytes 3145728 | tf_op jit(solution)/shard_map/all_to_all | solution.py:501
  14.1 3.5 %halo_rows.1 = (bf16[6,2,16,1152]{3,2,1,0:T(8,128)(2,1)}, bf16[6,2,16,1152]{3,2,1,0:T(8,128)(2,1)}) custom-call(f32[4,128,1152]{2,1,0:T(8,128)} %bitcast.4, f32[2,128,1152]{2,1,0:T(8,128)} %bitcast.7), custom_call_target="tpu_custom_call" | custom-call | flops 589824 | bytes 4718592 | tf_op jit(solution)/shard_map/halo_rows/pallas_call | solution.py:485
  17.5 1.3 %collective-permute-start = (bf16[6,2,16,1152]{3,2,1,0:T(8,128)(2,1)}, bf16[6,2,16,1152]{3,2,1,0:T(8,128)(2,1)S(1)}, u32[]{:S(2)}, u32[]{:S(2)}) collective-permute-start(bf16[6,2,16,1152]{3,2,1,0:T(8,128)(2,1)} %get-tuple-element.24), channel_id=1, source_target_pairs={{0,8},{8,16},{16,24},{1,9},{9,17},{17,25},{2,10},{10,18},{18,26},{... | collective-permute-start | bytes 1327112 | tf_op jit(solution)/shard_map/ppermute | solution.py:504
  18.9 1.4 %collective-permute-start.1 = (bf16[6,2,16,1152]{3,2,1,0:T(8,128)(2,1)}, bf16[6,2,16,1152]{3,2,1,0:T(8,128)(2,1)}, u32[]{:S(2)}, u32[]{:S(2)}) collective-permute-start(bf16[6,2,16,1152]{3,2,1,0:T(8,128)(2,1)} %get-tuple-element.25), channel_id=1, source_target_pairs={{8,0},{16,8},{24,16},{9,1},{17,9},{25,17},{10,2},{18,10},{26,18},{... | collective-permute-start | bytes 1327112 | tf_op jit(solution)/shard_map/ppermute | solution.py:505
  20.4 0.1 collective-permute-done.before_ref
  20.5 4.4 %collective-permute-done.1.after_ref = bf16[6,2,16,1152]{3,2,1,0:T(8,128)(2,1)} collective-permute-done((bf16[6,2,16,1152]{3,2,1,0:T(8,128)(2,1)}, bf16[6,2,16,1152]{3,2,1,0:T(8,128)(2,1)}, u32[]{:S(2)}, u32[]{:S(2)}) %collective-permute-start.1) | collective-permute-done | bytes 442400 | tf_op jit(solution)/shard_map/ppermute | solution.py:505
  24.8 9.6 %edge_rows.1 = (bf16[4,3,4,16,128]{4,3,2,1,0:T(8,128)(2,1)}, bf16[4,3,4,16,128]{4,3,2,1,0:T(8,128)(2,1)}, bf16[4,3,4,16,128]{4,3,2,1,0:T(8,128)(2,1)}, bf16[4,3,...) custom-call(s32[1,8]{1,0:T(1,128)} %counts_ref.7, ...), custom_call_target="tpu_custom_call" | custom-call | flops 47185920 | bytes 5898240 | tf_op jit(solution)/shard_map/edge_rows/pallas_call | solution.py:509
  34.5 1.5 %collective-permute-start.2 = (bf16[4,3,4,16,128]{4,3,2,1,0:T(8,128)(2,1)}, bf16[4,3,4,16,128]{4,3,2,1,0:T(8,128)(2,1)S(1)}, u32[]{:S(2)}, u32[]{:S(2)}) collective-permute-start(bf16[4,3,4,16,128]{4,3,2,1,0:T(8,128)(2,1)} %get-tuple-element.27), channel_id=1, source_target_pairs={{0,1},{1,0},{2,3},{3,2},{4,5},{5,4},{6,7},{7,6},{8,9},{9,8},{10,11... | collective-permute-start | bytes 589832 | tf_op jit(solution)/shard_map/ppermute | solution.py:527
  36.0 0.6 collective-permute-start.3
  36.6 1.5 %collective-permute-start.4 = (bf16[4,3,4,16,128]{4,3,2,1,0:T(8,128)(2,1)}, bf16[4,3,4,16,128]{4,3,2,1,0:T(8,128)(2,1)}, u32[]{:S(2)}, u32[]{:S(2)}) collective-permute-start(bf16[4,3,4,16,128]{4,3,2,1,0:T(8,128)(2,1)} %get-tuple-element.29), channel_id=1, source_target_pairs={{0,3},{1,2},{2,1},{3,0},{4,7},{5,6},{6,5},{7,4},{8,11},{9,10},{10,... | collective-permute-start | bytes 589832 | tf_op jit(solution)/shard_map/ppermute | solution.py:527
  38.0 2.4 %collective-permute-start.5 = (bf16[4,3,4,16,128]{4,3,2,1,0:T(8,128)(2,1)}, bf16[4,3,4,16,128]{4,3,2,1,0:T(8,128)(2,1)}, u32[]{:S(2)}, u32[]{:S(2)}) collective-permute-start(bf16[4,3,4,16,128]{4,3,2,1,0:T(8,128)(2,1)} %get-tuple-element.30), channel_id=1, source_target_pairs={{0,4},{1,5},{2,6},{3,7},{4,0},{5,1},{6,2},{7,3},{8,12},{9,13},{10,... | collective-permute-start | bytes 589832 | tf_op jit(solution)/shard_map/ppermute | solution.py:527
  40.4 1.5 %collective-permute-start.6 = (bf16[4,3,4,16,128]{4,3,2,1,0:T(8,128)(2,1)}, bf16[4,3,4,16,128]{4,3,2,1,0:T(8,128)(2,1)}, u32[]{:S(2)}, u32[]{:S(2)}) collective-permute-start(bf16[4,3,4,16,128]{4,3,2,1,0:T(8,128)(2,1)} %get-tuple-element.31), channel_id=1, source_target_pairs={{0,5},{1,4},{2,7},{3,6},{4,1},{5,0},{6,3},{7,2},{8,13},{9,12},{10,... | collective-permute-start | bytes 589832 | tf_op jit(solution)/shard_map/ppermute | solution.py:527
  41.9 1.5 %collective-permute-start.7 = (bf16[4,3,4,16,128]{4,3,2,1,0:T(8,128)(2,1)}, bf16[4,3,4,16,128]{4,3,2,1,0:T(8,128)(2,1)}, u32[]{:S(2)}, u32[]{:S(2)}) collective-permute-start(bf16[4,3,4,16,128]{4,3,2,1,0:T(8,128)(2,1)} %get-tuple-element.32), channel_id=1, source_target_pairs={{0,6},{1,7},{2,4},{3,5},{4,2},{5,3},{6,0},{7,1},{8,14},{9,15},{10,... | collective-permute-start | bytes 589832 | tf_op jit(solution)/shard_map/ppermute | solution.py:527
  43.3 0.7 copy-done.5
  44.0 2.4 %collective-permute-start.8 = (bf16[4,3,4,16,128]{4,3,2,1,0:T(8,128)(2,1)}, bf16[4,3,4,16,128]{4,3,2,1,0:T(8,128)(2,1)}, u32[]{:S(2)}, u32[]{:S(2)}) collective-permute-start(bf16[4,3,4,16,128]{4,3,2,1,0:T(8,128)(2,1)} %get-tuple-element.33), channel_id=1, source_target_pairs={{0,7},{1,6},{2,5},{3,4},{4,3},{5,2},{6,1},{7,0},{8,15},{9,14},{10,... | collective-permute-start | bytes 589832 | tf_op jit(solution)/shard_map/ppermute | solution.py:527
  46.4 6.4 %all-to-all-done.block_ref = bf16[8,4,3,4,16,128]{5,4,3,2,1,0:T(8,128)(2,1)S(1)} async-done(((bf16[8,4,3,4,16,128]{5,4,3,2,1,0:T(8,128)(2,1)}), bf16[8,4,3,4,16,128]{5,4,3,2,1,0:T(8,128)(2,1)S(1)}, u32[]{:S(2)}, u32[]{:S(2)}) %all-to-all-start) | async-done | bytes 1572896 | tf_op jit(solution)/shard_map/all_to_all | solution.py:501
  52.9 0.7 copy-done.7
  53.6 5.9 %inner_columns.1 = (bf16[4,512,384]{2,1,0:T(8,128)(2,1)S(1)}, bf16[512,512]{1,0:T(8,128)(2,1)S(1)}, bf16[512,512]{1,0:T(8,128)(2,1)S(1)}, bf16[512,512]{1,0:T(8,128)(2,1)S(1)}) custom-call(s32[4,6]{1,0:T(4,128)S(1)} %copy-done.8, s32[1,8]{1,0:T(1,128)S(1)} %copy-done, bf16[8,4,3,4,16,128]{5,4,3,2,1,0:T(8,128)(2,1)S(1)} %all-to-all-done.block_ref, ...), custom_call_target="tpu_custom_call" | custom-call | flops 2617245696 | bytes 3145728 | tf_op jit(solution)/shard_map/inner_columns/pallas_call | solution.py:559
  59.5 10.1 %collective-permute-done.5.refs_4_ = bf16[4,3,4,16,128]{4,3,2,1,0:T(8,128)(2,1)} collective-permute-done((bf16[4,3,4,16,128]{4,3,2,1,0:T(8,128)(2,1)}, bf16[4,3,4,16,128]{4,3,2,1,0:T(8,128)(2,1)}, u32[]{:S(2)}, u32[]{:S(2)}) %collective-permute-start.5) | collective-permute-done | bytes 196640 | tf_op jit(solution)/shard_map/ppermute | solution.py:527
  69.6 4.2 %collective-permute-done.6.refs_5_ = bf16[4,3,4,16,128]{4,3,2,1,0:T(8,128)(2,1)} collective-permute-done((bf16[4,3,4,16,128]{4,3,2,1,0:T(8,128)(2,1)}, bf16[4,3,4,16,128]{4,3,2,1,0:T(8,128)(2,1)}, u32[]{:S(2)}, u32[]{:S(2)}) %collective-permute-start.6) | collective-permute-done | bytes 196640 | tf_op jit(solution)/shard_map/ppermute | solution.py:527
  73.8 6.9 %collective-permute-done.7.refs_6_ = bf16[4,3,4,16,128]{4,3,2,1,0:T(8,128)(2,1)} collective-permute-done((bf16[4,3,4,16,128]{4,3,2,1,0:T(8,128)(2,1)}, bf16[4,3,4,16,128]{4,3,2,1,0:T(8,128)(2,1)}, u32[]{:S(2)}, u32[]{:S(2)}) %collective-permute-start.7) | collective-permute-done | bytes 196640 | tf_op jit(solution)/shard_map/ppermute | solution.py:527
  80.7 4.5 %collective-permute-done.8.refs_7_ = bf16[4,3,4,16,128]{4,3,2,1,0:T(8,128)(2,1)} collective-permute-done((bf16[4,3,4,16,128]{4,3,2,1,0:T(8,128)(2,1)}, bf16[4,3,4,16,128]{4,3,2,1,0:T(8,128)(2,1)}, u32[]{:S(2)}, u32[]{:S(2)}) %collective-permute-start.8) | collective-permute-done | bytes 196640 | tf_op jit(solution)/shard_map/ppermute | solution.py:527
  85.2 7.7 %edge_columns.1 = bf16[512,8,384]{2,1,0:T(8,128)(2,1)} custom-call(s32[4,6]{1,0:T(4,128)S(1)} %copy-done.8, s32[1,8]{1,0:T(1,128)S(1)} %copy-done, bf16[4,3,4,16,128]{4,3,2,1,0:T(8,128)(2,1)S(1)} %copy-done.4, bf16[4,3,4,16,128]{4,3,2,1,0:T(8,128)(2,1)S(1)} %collective-permute-done.2.refs_1_, bf16[4,3,4,16,128]{4,3,2,1,0:T(8,128)(2,1)S(1)} %copy-done.6, ...), custom_call_target="tpu_custom_call" | custom-call | flops 2617245696 | bytes 3145728 | tf_op jit(solution)/shard_map/edge_columns/pallas_call | solution.py:579
  (21 shorter events, 0.1 us)
Async XLA Ops:
  7.8 45.0 %all-to-all-start = ((bf16[8,4,3,4,16,128]{5,4,3,2,1,0:T(8,128)(2,1)}), bf16[8,4,3,4,16,128]{5,4,3,2,1,0:T(8,128)(2,1)S(1)}, u32[]{:S(2)}, u32[]{:S(2)}) async-start(bf16[8,4,3,4,16,128]{5,4,3,2,1,0:T(8,128)(2,1)} %inner_rows.1), calls=%async_computation | async-start | bytes 3145728 | tf_op jit(solution)/shard_map/all_to_all | solution.py:501
  17.5 2.9 %collective-permute-start = (bf16[6,2,16,1152]{3,2,1,0:T(8,128)(2,1)}, bf16[6,2,16,1152]{3,2,1,0:T(8,128)(2,1)S(1)}, u32[]{:S(2)}, u32[]{:S(2)}) collective-permute-start(bf16[6,2,16,1152]{3,2,1,0:T(8,128)(2,1)} %get-tuple-element.24), channel_id=1, source_target_pairs={{0,8},{8,16},{16,24},{1,9},{9,17},{17,25},{2,10},{10,18},{18,26},{... | collective-permute-start | bytes 1327112 | tf_op jit(solution)/shard_map/ppermute | solution.py:504
  18.9 34.0 %copy-start = (s32[1,8]{1,0:T(1,128)S(1)}, s32[1,8]{1,0:T(1,128)}, u32[]{:S(2)}) copy-start(s32[1,8]{1,0:T(1,128)} %counts_ref.7) | copy-start | bytes 100
  18.9 33.9 %copy-start.1 = (bf16[512,512]{1,0:T(8,128)(2,1)S(1)}, bf16[512,512]{1,0:T(8,128)(2,1)}, u32[]{:S(2)}) copy-start(bf16[512,512]{1,0:T(8,128)(2,1)} %first_ref.1) | copy-start | bytes 1572868
  18.9 33.9 %copy-start.2 = (bf16[512,512]{1,0:T(8,128)(2,1)S(1)}, bf16[512,512]{1,0:T(8,128)(2,1)}, u32[]{:S(2)}) copy-start(bf16[512,512]{1,0:T(8,128)(2,1)} %second_ref.1) | copy-start | bytes 1572868
  18.9 33.9 %copy-start.3 = (bf16[512,512]{1,0:T(8,128)(2,1)S(1)}, bf16[512,512]{1,0:T(8,128)(2,1)}, u32[]{:S(2)}) copy-start(bf16[512,512]{1,0:T(8,128)(2,1)} %third_ref.1) | copy-start | bytes 1572868
  18.9 33.9 %copy-start.8 = (s32[4,6]{1,0:T(4,128)S(1)}, s32[4,6]{1,0:T(4,128)}, u32[]{:S(2)}) copy-start(s32[4,6]{1,0:T(4,128)} %groups_ref.3) | copy-start | bytes 292
  18.9 5.9 %collective-permute-start.1 = (bf16[6,2,16,1152]{3,2,1,0:T(8,128)(2,1)}, bf16[6,2,16,1152]{3,2,1,0:T(8,128)(2,1)}, u32[]{:S(2)}, u32[]{:S(2)}) collective-permute-start(bf16[6,2,16,1152]{3,2,1,0:T(8,128)(2,1)} %get-tuple-element.25), channel_id=1, source_target_pairs={{8,0},{16,8},{24,16},{9,1},{17,9},{25,17},{10,2},{18,10},{26,18},{... | collective-permute-start | bytes 1327112 | tf_op jit(solution)/shard_map/ppermute | solution.py:505
  20.5 4.4 %copy-start.9 = (bf16[6,2,16,1152]{3,2,1,0:T(8,128)(2,1)}, bf16[6,2,16,1152]{3,2,1,0:T(8,128)(2,1)S(1)}, u32[]{:S(2)}) copy-start(bf16[6,2,16,1152]{3,2,1,0:T(8,128)(2,1)S(1)} %collective-permute-done.before_ref) | copy-start | bytes 1327108
  34.5 7.4 %collective-permute-start.2 = (bf16[4,3,4,16,128]{4,3,2,1,0:T(8,128)(2,1)}, bf16[4,3,4,16,128]{4,3,2,1,0:T(8,128)(2,1)S(1)}, u32[]{:S(2)}, u32[]{:S(2)}) collective-permute-start(bf16[4,3,4,16,128]{4,3,2,1,0:T(8,128)(2,1)} %get-tuple-element.27), channel_id=1, source_target_pairs={{0,1},{1,0},{2,3},{3,2},{4,5},{5,4},{6,7},{7,6},{8,9},{9,8},{10,11... | collective-permute-start | bytes 589832 | tf_op jit(solution)/shard_map/ppermute | solution.py:527
  36.0 7.3 %collective-permute-start.3 = (bf16[4,3,4,16,128]{4,3,2,1,0:T(8,128)(2,1)}, bf16[4,3,4,16,128]{4,3,2,1,0:T(8,128)(2,1)S(1)}, u32[]{:S(2)}, u32[]{:S(2)}) collective-permute-start(bf16[4,3,4,16,128]{4,3,2,1,0:T(8,128)(2,1)} %get-tuple-element.28), channel_id=1, source_target_pairs={{0,2},{1,3},{2,0},{3,1},{4,6},{5,7},{6,4},{7,5},{8,10},{9,11},{10,... | collective-permute-start | bytes 589832 | tf_op jit(solution)/shard_map/ppermute | solution.py:527
  36.6 22.9 %collective-permute-start.4 = (bf16[4,3,4,16,128]{4,3,2,1,0:T(8,128)(2,1)}, bf16[4,3,4,16,128]{4,3,2,1,0:T(8,128)(2,1)}, u32[]{:S(2)}, u32[]{:S(2)}) collective-permute-start(bf16[4,3,4,16,128]{4,3,2,1,0:T(8,128)(2,1)} %get-tuple-element.29), channel_id=1, source_target_pairs={{0,3},{1,2},{2,1},{3,0},{4,7},{5,6},{6,5},{7,4},{8,11},{9,10},{10,... | collective-permute-start | bytes 589832 | tf_op jit(solution)/shard_map/ppermute | solution.py:527
  38.0 31.5 %collective-permute-start.5 = (bf16[4,3,4,16,128]{4,3,2,1,0:T(8,128)(2,1)}, bf16[4,3,4,16,128]{4,3,2,1,0:T(8,128)(2,1)}, u32[]{:S(2)}, u32[]{:S(2)}) collective-permute-start(bf16[4,3,4,16,128]{4,3,2,1,0:T(8,128)(2,1)} %get-tuple-element.30), channel_id=1, source_target_pairs={{0,4},{1,5},{2,6},{3,7},{4,0},{5,1},{6,2},{7,3},{8,12},{9,13},{10,... | collective-permute-start | bytes 589832 | tf_op jit(solution)/shard_map/ppermute | solution.py:527
  40.4 33.4 %collective-permute-start.6 = (bf16[4,3,4,16,128]{4,3,2,1,0:T(8,128)(2,1)}, bf16[4,3,4,16,128]{4,3,2,1,0:T(8,128)(2,1)}, u32[]{:S(2)}, u32[]{:S(2)}) collective-permute-start(bf16[4,3,4,16,128]{4,3,2,1,0:T(8,128)(2,1)} %get-tuple-element.31), channel_id=1, source_target_pairs={{0,5},{1,4},{2,7},{3,6},{4,1},{5,0},{6,3},{7,2},{8,13},{9,12},{10,... | collective-permute-start | bytes 589832 | tf_op jit(solution)/shard_map/ppermute | solution.py:527
  41.9 38.8 %collective-permute-start.7 = (bf16[4,3,4,16,128]{4,3,2,1,0:T(8,128)(2,1)}, bf16[4,3,4,16,128]{4,3,2,1,0:T(8,128)(2,1)}, u32[]{:S(2)}, u32[]{:S(2)}) collective-permute-start(bf16[4,3,4,16,128]{4,3,2,1,0:T(8,128)(2,1)} %get-tuple-element.32), channel_id=1, source_target_pairs={{0,6},{1,7},{2,4},{3,5},{4,2},{5,3},{6,0},{7,1},{8,14},{9,15},{10,... | collective-permute-start | bytes 589832 | tf_op jit(solution)/shard_map/ppermute | solution.py:527
  43.3 0.7 copy-start.5
  44.0 41.2 %copy-start.4 = (bf16[4,3,4,16,128]{4,3,2,1,0:T(8,128)(2,1)S(1)}, bf16[4,3,4,16,128]{4,3,2,1,0:T(8,128)(2,1)}, u32[]{:S(2)}) copy-start(bf16[4,3,4,16,128]{4,3,2,1,0:T(8,128)(2,1)} %get-tuple-element.26.refs_0_) | copy-start | bytes 589828
  44.0 41.2 %collective-permute-start.8 = (bf16[4,3,4,16,128]{4,3,2,1,0:T(8,128)(2,1)}, bf16[4,3,4,16,128]{4,3,2,1,0:T(8,128)(2,1)}, u32[]{:S(2)}, u32[]{:S(2)}) collective-permute-start(bf16[4,3,4,16,128]{4,3,2,1,0:T(8,128)(2,1)} %get-tuple-element.33), channel_id=1, source_target_pairs={{0,7},{1,6},{2,5},{3,4},{4,3},{5,2},{6,1},{7,0},{8,15},{9,14},{10,... | collective-permute-start | bytes 589832 | tf_op jit(solution)/shard_map/ppermute | solution.py:527
  52.8 0.8 copy-start.7
  53.6 31.6 %copy-start.6 = (bf16[4,3,4,16,128]{4,3,2,1,0:T(8,128)(2,1)S(1)}, bf16[4,3,4,16,128]{4,3,2,1,0:T(8,128)(2,1)}, u32[]{:S(2)}) copy-start(bf16[4,3,4,16,128]{4,3,2,1,0:T(8,128)(2,1)} %copy-done.5) | copy-start | bytes 589828

commit v4 on v3

v4 whole, which is shorter than its diff:
```python
import functools

import jax
import jax.numpy as jnp
from jax import lax
from jax.experimental import pallas as pl
from jax.experimental.pallas import tpu as pltpu
from jax.sharding import PartitionSpec as P

DIFFUSION = 0.15
LANES = 128
HALO = 2
MIB = 1024 * 1024


def from_west(x):
    return pltpu.roll(x, 1, 1)


def from_east(x):
    return pltpu.roll(x, x.shape[1] - 1, 1)


def face_weights(before, after):
    half = 0.25 * (before + after)
    return half + DIFFUSION, half - DIFFUSION


def step_rows(values, rows, weights):
    result = {}
    for row in rows:
        here, west, away, above, below = weights(row)
        side = west * from_west(values[row]) + away * from_east(values[row])
        across = above * values[row - 1] + below * values[row + 1]
        result[row] = here * values[row] + (side + across)
    return result


def heun_rows(values, weights):
    count = len(values)
    predicted = step_rows(values, range(1, count - 1), weights)
    stepped = step_rows(predicted, range(2, count - 2), weights)
    return [0.5 * (values[row] + stepped[row]) for row in stepped]


def start_grid(fields_ref, winds_ref, grid_ref, sems):
    fields, tiles = fields_ref.shape[0], grid_ref.shape[1]

    def copy(array, tile, source):
        lanes = pl.ds(tile * LANES, LANES)
        return pltpu.make_async_copy(
            source.at[:, lanes], grid_ref.at[array, tile], sems.at[array, tile]
        )

    for wind in range(2):
        for tile in range(tiles):
            copy(fields + wind, tile, winds_ref.at[wind]).start()
    for field in range(fields):
        for tile in range(tiles):
            copy(field, tile, fields_ref.at[field]).start()

    def wait(array):
        for tile in range(tiles):
            copy(array, tile, fields_ref.at[0]).wait()

    return wait


def load_row(grid_ref, array, row, group, size, rows):
    start = group * (size * rows) + row
    pieces = [
        grid_ref[array, tile, pl.ds(start, size, stride=rows), :]
        for tile in range(grid_ref.shape[1])
    ]
    return jnp.concatenate(pieces, axis=1)


def store_weights(weight_ref, levels, east_winds, north_winds, wall=None):
    count = len(north_winds)
    faces = {}
    for face in range(1, count):
        pair = face_weights(north_winds[face - 1], north_winds[face])
        shut = wall is not None and wall[0] == face
        faces[face] = [part * wall[1] for part in pair] if shut else pair
    for row in range(1, count - 1):
        west, own = face_weights(from_west(east_winds[row]), east_winds[row])
        here = 1.0 + (own - from_east(west)) + (faces[row][1] - faces[row + 1][0])
        parts = (here, west, -from_east(own), faces[row][0], -faces[row + 1][1])
        for part, value in enumerate(parts):
            weight_ref[row, part, levels, :] = value


def keep_row(kept_ref, index, levels, value):
    for tile in range(value.shape[1] // LANES):
        kept_ref[tile, index, levels, :] = value[:, tile * LANES : (tile + 1) * LANES]


def clear_tail(kept_ref, tiles):
    for tile in range(tiles, kept_ref.shape[0]):
        kept_ref[tile] = jnp.zeros(kept_ref.shape[1:], kept_ref.dtype)


def keep_starts(counts_ref, start_ref):
    total = jnp.int32(0)
    for owner in range(start_ref.shape[0]):
        start_ref[owner] = total
        total = total + counts_ref[0, owner]


def turned_starts(start_ref, by_turn, slots):
    own = lax.axis_index("lev") if by_turn else 0
    return [start_ref[own ^ turn] for turn in range(slots)]


def pack_rows(kept_ref, starts, blocks, store):
    _, rows, levels, _ = kept_ref.shape
    lane = lax.broadcasted_iota(jnp.int32, (levels, LANES), 1)
    for slot, start in enumerate(starts):
        tile = start // LANES
        inside = start - tile * LANES
        shift = (LANES - inside) % LANES
        keep = lane < LANES - inside
        for row in range(rows):
            turned = [
                pltpu.roll(kept_ref[tile + j, row], shift, 1) for j in range(blocks + 1)
            ]
            for j in range(blocks):
                joined = jnp.where(keep, turned[j], turned[j + 1])
                store(slot, j, row, joined.astype(jnp.bfloat16))


def inner_kernel(
    rows,
    by_turn,
    counts_ref,
    fields_ref,
    winds_ref,
    *refs,
):
    outs, scratch = refs[:-9], refs[-9:]
    grid_ref, weight_ref, kept_ref, sems = scratch[:4]
    start_ref, packed_ref, raw_ref, halo_ref, sent = scratch[4:]
    *outs, first_ref, last_ref = outs
    fields = fields_ref.shape[0]
    owners = start_ref.shape[0]
    _, slots, blocks, _, levels, _ = packed_ref.shape
    tiles = grid_ref.shape[1]
    size = min(8, levels)
    groups = levels // size
    wait = start_grid(fields_ref, winds_ref, grid_ref, sems)
    clear_tail(kept_ref, grid_ref.shape[1])
    keep_starts(counts_ref, start_ref)

    def field_out(field):
        if not by_turn:
            return [
                pltpu.make_async_copy(
                    packed_ref.at[field], outs[0].at[:, field], sent.at[field, 0]
                )
            ]
        copies = [
            pltpu.make_async_copy(
                packed_ref.at[field, slot], outs[slot].at[field], sent.at[field, slot]
            )
            for slot in range(slots)
        ]
        copies.append(
            pltpu.make_async_copy(raw_ref.at[field], outs[slots].at[field], sent.at[field, slots])
        )
        return copies

    def keep_halo(array):
        for row in range(HALO):
            for side, source in enumerate((row, rows - HALO + row)):
                value = [
                    load_row(grid_ref, array, source, group, size, rows) for group in range(groups)
                ]
                halo_ref[side, array, row] = jnp.concatenate(value, axis=0).astype(halo_ref.dtype)

    def halo_out(array):
        return [
            pltpu.make_async_copy(
                halo_ref.at[side, array], ref.at[array], sent.at[array, slots + 1 + side]
            )
            for side, ref in enumerate((first_ref, last_ref))
        ]

    wait(fields)
    wait(fields + 1)

    def weights(group, carry):
        east = [load_row(grid_ref, fields, row, group, size, rows) for row in range(rows)]
        north = [load_row(grid_ref, fields + 1, row, group, size, rows) for row in range(rows)]
        store_weights(weight_ref, pl.ds(group * size, size), east, north)
        return carry

    lax.fori_loop(0, groups, weights, 0)
    for array in (fields, fields + 1):
        keep_halo(array)
        for copy in halo_out(array):
            copy.start()

    def one_field(field, carry):
        wait(field)
        keep_halo(field)

        def one_group(group, carry):
            place = pl.ds(group * size, size)
            values = [load_row(grid_ref, field, row, group, size, rows) for row in range(rows)]

            def row_weights(row):
                return [weight_ref[row, part, place, :] for part in range(5)]

            for index, value in enumerate(heun_rows(values, row_weights)):
                keep_row(kept_ref, index, place, value)
            return carry

        lax.fori_loop(0, groups, one_group, 0)

        def store(slot, block, row, value):
            packed_ref[field, slot, block, row] = value

        if by_turn:
            for tile in range(tiles):
                raw_ref[field, tile] = kept_ref[tile].astype(raw_ref.dtype)
        pack_rows(kept_ref, turned_starts(start_ref, by_turn, slots), blocks, store)
        for copy in halo_out(field) + field_out(field):
            copy.start()
        return carry

    lax.fori_loop(0, fields, one_field, 0)
    for field in range(fields):
        for copy in field_out(field):
            copy.wait()
    for array in range(fields + 2):
        for copy in halo_out(array):
            copy.wait()


def mirror_kernel(counts_ref, raw_ref, *refs):
    outs, (kept_ref, start_ref) = refs[:-2], refs[-2:]
    fields, tiles = raw_ref.shape[:2]
    keep_starts(counts_ref, start_ref)
    clear_tail(kept_ref, tiles)

    def one_field(field, carry):
        for tile in range(tiles):
            kept_ref[tile] = raw_ref[field, tile].astype(jnp.float32)

        def store(slot, block, row, value):
            outs[slot][field, block, row] = value

        starts = turned_starts(start_ref, True, len(outs))
        pack_rows(kept_ref, starts, outs[0].shape[1], store)
        return carry

    lax.fori_loop(0, fields, one_field, 0)


def edge_kernel(
    rows,
    by_turn,
    counts_ref,
    fields_ref,
    winds_ref,
    before_ref,
    after_ref,
    *refs,
):
    outs, scratch = refs[:-6], refs[-6:]
    grid_ref, weight_ref, kept_ref, sems, start_ref, halo_ref = scratch
    fields = fields_ref.shape[0]
    owners = start_ref.shape[0]
    blocks = outs[0].shape[-4]
    levels = before_ref.shape[2]
    size = min(8, levels)
    groups = levels // size
    wait = start_grid(fields_ref, winds_ref, grid_ref, sems)
    clear_tail(kept_ref, grid_ref.shape[1])
    keep_starts(counts_ref, start_ref)
    count = 3 * HALO

    def run(array, group, top):
        own = range(2 * HALO) if top else range(rows - 2 * HALO, rows)
        own = [load_row(grid_ref, array, row, group, size, rows) for row in own]
        place = pl.ds(group * size, size)
        halo = [halo_ref[int(top), array, row, place, :] for row in range(HALO)]
        return halo + own if top else own + halo

    for side, ref in enumerate((after_ref, before_ref)):
        for array in range(fields + 2):
            for row in range(HALO):
                halo_ref[side, array, row] = ref[array, row].astype(jnp.float32)

    wait(fields)
    wait(fields + 1)
    for top in (True, False):
        wall = HALO if top else count - HALO
        band = lax.axis_index("lat")
        is_open = jnp.where(band == (0 if top else lax.axis_size("lat") - 1), 0.0, 1.0)

        def weights(group, carry):
            store_weights(
                weight_ref.at[int(top)],
                pl.ds(group * size, size),
                run(fields, group, top),
                run(fields + 1, group, top),
                (wall, is_open),
            )
            return carry

        lax.fori_loop(0, groups, weights, 0)

    def one_field(field, carry):
        wait(field)

        def one_group(group, carry):
            place = pl.ds(group * size, size)
            for top in (True, False):
                side = int(top)

                def row_weights(row):
                    return [weight_ref[side, row, part, place, :] for part in range(5)]

                done = heun_rows(run(field, group, top), row_weights)
                for index, value in enumerate(done):
                    keep_row(kept_ref, index + (0 if top else HALO), place, value)
            return carry

        lax.fori_loop(0, groups, one_group, 0)

        def store(slot, block, row, value):
            if by_turn:
                outs[slot][field, block, row] = value
            else:
                outs[0][slot, field, block, row] = value

        pack_rows(kept_ref, turned_starts(start_ref, by_turn, owners), blocks, store)
        return carry

    lax.fori_loop(0, fields, one_field, 0)


def silu(x):
    half = 0.5 * x
    return half + half * jnp.tanh(half)


def dot(a, b):
    return jnp.dot(a, b, preferred_element_type=jnp.float32)


def gathered(block_ref, field):
    sources, _, _, rows = block_ref.shape[:4]
    by_row = [
        jnp.concatenate([block_ref[source, field, 0, row] for source in range(sources)], axis=0)
        for row in range(rows)
    ]
    return jnp.concatenate(by_row, axis=1)


def sort_turns(own, refs, sorted_ref):
    fields, _, rows, levels, _ = refs[0].shape
    for turn, ref in enumerate(refs):
        place = pl.ds(pl.multiple_of((own ^ turn) * levels, levels), levels)
        for field in range(fields):
            for row in range(rows):
                sorted_ref[field, place, row * LANES : (row + 1) * LANES] = ref[field, 0, row]


def column_update(columns, fields, remap_ref, first_ref, second_ref, third_ref):
    remapped = []
    for field in range(fields):
        values = columns(field)
        remapped.append(values.astype(jnp.float32) + dot(remap_ref[...], values))
    remapped = jnp.concatenate(remapped, axis=0)
    hidden = silu(dot(first_ref[...], remapped.astype(jnp.bfloat16))).astype(jnp.bfloat16)
    hidden = silu(dot(second_ref[...], hidden)).astype(jnp.bfloat16)
    tendency = dot(third_ref[...], hidden).astype(jnp.bfloat16).astype(jnp.float32)
    return remapped, tendency


def finished_row(remapped, tendency, listed, index, live):
    lanes = slice(index * LANES, (index + 1) * LANES)
    updated = remapped[:, lanes] + jnp.where(listed, tendency[:, lanes], 0.0)
    return jnp.where(live, updated, 0.0)


def live_lanes(counts_ref, features, block):
    lane = lax.broadcasted_iota(jnp.int32, (features, LANES), 1)
    return lane + block * LANES < counts_ref[0, lax.axis_index("lev")]


def is_listed(groups_ref, row):
    found = jnp.bool_(False)
    for owner in range(groups_ref.shape[0]):
        for index in range(groups_ref.shape[1]):
            found = found | (groups_ref[owner, index] == row)
    return found


def column_source(by_turn, refs, sorted_ref):
    if not by_turn:
        return functools.partial(gathered, refs[0])
    sort_turns(lax.axis_index("lev"), refs, sorted_ref)
    return lambda field: sorted_ref[field]


def half_kernel(rows, row_list, by_turn, groups_ref, counts_ref, *refs):
    out_ref, first_out, second_out, third_out, sorted_ref = refs[-5:]
    *refs, remap_ref, first_ref, second_ref, third_ref = refs[:-5]

    @pl.when(pl.program_id(0) == 0)
    def _():
        first_out[...] = first_ref[...].T
        second_out[...] = second_ref[...].T
        third_out[...] = third_ref[...].T

    columns = column_source(by_turn, refs, sorted_ref)
    fields = sorted_ref.shape[0]
    remapped, tendency = column_update(
        columns, fields, remap_ref, first_out, second_out, third_out
    )
    live = live_lanes(counts_ref, remapped.shape[0], pl.program_id(0))
    first_row = lax.axis_index("lat") * rows
    for index, row in enumerate(row_list):
        listed = is_listed(groups_ref, first_row + row)
        updated = finished_row(remapped, tendency, listed, index, live)
        out_ref[index] = updated.astype(jnp.bfloat16)


def last_kernel(row_list, done_list, by_turn, groups_ref, counts_ref, *refs):
    *refs, done_ref, remap_ref, first_ref, second_ref, third_ref, out_ref, tiles_ref, sorted_ref = (
        refs
    )
    features, rows, _ = out_ref.shape
    fields = sorted_ref.shape[0]
    columns = column_source(by_turn, refs, sorted_ref)
    remapped, tendency = column_update(
        columns, fields, remap_ref, first_ref, second_ref, third_ref
    )
    live = live_lanes(counts_ref, features, pl.program_id(0))
    first_row = lax.axis_index("lat") * rows
    for index, row in enumerate(done_list):
        tiles_ref[pl.ds(row, features, stride=rows), :] = done_ref[index].astype(jnp.float32)
    for index, row in enumerate(row_list):
        listed = is_listed(groups_ref, first_row + row)
        tiles_ref[pl.ds(row, features, stride=rows), :] = finished_row(
            remapped, tendency, listed, index, live
        )
    out_ref[...] = tiles_ref[...].reshape(features, rows, LANES).astype(jnp.bfloat16)


def shards(fields, winds, remap_weight, w_first, w_second, w_third, lon_counts, group_list):
    field_count, level_count, lat_rows, lon_total = fields.shape
    band_count = lax.axis_size("lat")
    owner_count = lax.axis_size("lev")
    all_levels = level_count * owner_count
    features = field_count * all_levels
    blocks = (2 * lon_total // owner_count + LANES - 1) // LANES
    slot_width = blocks * LANES
    inner_rows = tuple(range(HALO, lat_rows - HALO))
    edge_rows = tuple(range(HALO)) + tuple(range(lat_rows - HALO, lat_rows))
    half = len(inner_rows)
    stacked = field_count + 2
    tiles = lon_total // LANES
    smem = pl.BlockSpec(memory_space=pltpu.SMEM)
    anywhere = pl.BlockSpec(memory_space=pl.ANY)
    params = pltpu.CompilerParams(vmem_limit_bytes=60 * MIB)
    light = pltpu.CompilerParams(vmem_limit_bytes=24 * MIB)
    values = field_count * level_count * lat_rows * lon_total

    def payload(count):
        return (owner_count, field_count, count, half, level_count, LANES)

    flat_fields = fields.reshape(field_count, level_count * lat_rows, lon_total)
    flat_winds = winds.reshape(2, level_count * lat_rows, lon_total)
    halo_shape = jax.ShapeDtypeStruct((stacked, HALO, level_count, lon_total), jnp.bfloat16)

    def scratch(sides, count):
        return [
            pltpu.VMEM((stacked, tiles, level_count * lat_rows, LANES), jnp.float32),
            pltpu.VMEM(sides + (count - 1, 5, level_count, lon_total), jnp.float32),
            pltpu.VMEM((tiles + blocks, half, level_count, LANES), jnp.float32),
            pltpu.SemaphoreType.DMA((stacked, tiles)),
        ]

    by_turn = owner_count == 8
    near = owner_count // 2
    slots = near if by_turn else owner_count
    raw_shape = (field_count, tiles, half, level_count, LANES)
    piece = jax.ShapeDtypeStruct(payload(blocks)[1:], jnp.bfloat16)
    whole_payload = jax.ShapeDtypeStruct(payload(blocks), jnp.bfloat16)
    raw = jax.ShapeDtypeStruct(raw_shape, jnp.bfloat16)
    inner_shapes = [piece] * near + [raw] if by_turn else [whole_payload]
    starts_scratch = pltpu.SMEM((owner_count,), jnp.int32)
    *inner, first, last = pl.pallas_call(
        functools.partial(inner_kernel, lat_rows, by_turn),
        in_specs=[smem, anywhere, anywhere],
        out_specs=[anywhere] * (len(inner_shapes) + 2),
        out_shape=inner_shapes + [halo_shape, halo_shape],
        scratch_shapes=scratch((), lat_rows)
        + [
            starts_scratch,
            pltpu.VMEM((field_count, slots) + payload(blocks)[2:], jnp.bfloat16),
            pltpu.VMEM(raw_shape, jnp.bfloat16),
            pltpu.VMEM((2,) + halo_shape.shape, halo_shape.dtype),
            pltpu.SemaphoreType.DMA((stacked, slots + 3)),
        ],
        compiler_params=params,
        cost_estimate=pl.CostEstimate(flops=1, bytes_accessed=1, transcendentals=0),
        name="inner_rows",
    )(lon_counts, flat_fields, flat_winds)

    up = [(i, i + 1) for i in range(band_count - 1)]
    down = [(j, i) for i, j in up]

    def exchange(x):
        return lax.all_to_all(x, "lev", split_axis=0, concat_axis=0, tiled=True)

    def turned_exchange(x, turn):
        return lax.ppermute(x, "lev", [(i, i ^ turn) for i in range(owner_count)]) if turn else x

    if by_turn:
        crossed = turned_exchange(inner[near], near)
        inner_parts = [turned_exchange(x, turn) for turn, x in enumerate(inner[:near])]
    else:
        inner_parts = [exchange(inner[0])]
    before = lax.ppermute(last, "lat", up)
    after = lax.ppermute(first, "lat", down)

    edge_shapes = [piece] * owner_count if by_turn else [whole_payload]
    edge = pl.pallas_call(
        functools.partial(edge_kernel, lat_rows, by_turn),
        in_specs=[smem, anywhere, anywhere] + [pl.BlockSpec(memory_space=pltpu.VMEM)] * 2,
        out_shape=edge_shapes,
        scratch_shapes=scratch((2,), 3 * HALO)
        + [
            starts_scratch,
            pltpu.VMEM((2,) + halo_shape.shape, jnp.float32),
        ],
        compiler_params=params,
        cost_estimate=pl.CostEstimate(flops=1, bytes_accessed=1, transcendentals=0),
        name="edge_rows",
    )(lon_counts, flat_fields, flat_winds, before, after)

    if by_turn:
        edge = list(edge)
        mirrored = pl.pallas_call(
            mirror_kernel,
            in_specs=[smem, pl.BlockSpec(memory_space=pltpu.VMEM)],
            out_shape=[piece] * near,
            scratch_shapes=[scratch((), lat_rows)[2], starts_scratch],
            compiler_params=light,
            cost_estimate=pl.CostEstimate(flops=1, bytes_accessed=1, transcendentals=0),
            name="mirror_rows",
        )(lon_counts, crossed)
        edge[1:near], mirrored = lax.optimization_barrier((edge[1:near], mirrored))
        near_parts = inner_parts[1:]
        near_parts, edge[near + 1 :] = lax.optimization_barrier((near_parts, edge[near + 1 :]))
        inner_parts = inner_parts[:1] + near_parts
        edge_parts = [turned_exchange(x, turn) for turn, x in enumerate(edge)]
        inner_parts += [turned_exchange(x, turn) for turn, x in enumerate(mirrored)]
    else:
        edge_parts = [exchange(edge[0])]

    def by_level(block):
        if level_count % 16 == 0:
            return block
        return block.transpose(1, 2, 3, 0, 4, 5).reshape(
            1, field_count, block.shape[2], half, all_levels, LANES
        )

    def whole(shape):
        return pl.BlockSpec(shape, lambda i: (0,) * len(shape))

    def block_spec(block):
        return pl.BlockSpec(
            block.shape[:2] + (1,) + block.shape[3:], lambda i: (0, 0, i, 0, 0, 0)
        )

    def cost(count):
        return pl.CostEstimate(flops=1, bytes_accessed=1, transcendentals=0)

    weights = (w_first, w_second, w_third)
    weight_specs = [pl.BlockSpec(memory_space=pltpu.VMEM)] * 4
    if by_turn:
        part_specs = [
            pl.BlockSpec((field_count, 1, half, level_count, LANES), lambda i: (0, i, 0, 0, 0))
        ] * owner_count
    else:
        inner_parts = [by_level(inner_parts[0])]
        edge_parts = [by_level(edge_parts[0])]
        part_specs = [block_spec(edge_parts[0])]
    sorted_scratch = pltpu.VMEM((field_count, all_levels, half * LANES), jnp.bfloat16)
    done_spec = pl.BlockSpec((half, features, LANES), lambda i: (0, 0, i))
    done, *turned = pl.pallas_call(
        functools.partial(half_kernel, lat_rows, inner_rows, by_turn),
        grid=(blocks,),
        in_specs=[smem, smem] + part_specs + weight_specs,
        out_specs=[done_spec] + [whole(w.shape[::-1]) for w in weights],
        out_shape=[jax.ShapeDtypeStruct((half, features, slot_width), jnp.bfloat16)]
        + [jax.ShapeDtypeStruct(w.shape[::-1], w.dtype) for w in weights],
        scratch_shapes=[sorted_scratch],
        compiler_params=light,
        cost_estimate=cost(blocks),
        name="inner_columns",
    )(group_list, lon_counts, *inner_parts, remap_weight, *weights)
    out = pl.pallas_call(
        functools.partial(last_kernel, edge_rows, inner_rows, by_turn),
        grid=(blocks,),
        in_specs=[smem, smem] + part_specs + [done_spec] + weight_specs,
        out_specs=pl.BlockSpec((features, lat_rows, LANES), lambda i: (0, 0, i)),
        out_shape=jax.ShapeDtypeStruct((features, lat_rows, slot_width), jnp.bfloat16),
        scratch_shapes=[pltpu.VMEM((features * lat_rows, LANES), jnp.float32), sorted_scratch],
        compiler_params=light,
        cost_estimate=cost(blocks),
        name="edge_columns",
    )(group_list, lon_counts, *edge_parts, done, remap_weight, *turned)
    return out.reshape(field_count, all_levels, lat_rows, slot_width)


def solution(mesh):
    in_specs = (
        P(None, "lev", "lat", None),
        P(None, "lev", "lat", None),
        P(),
        P(),
        P(),
        P(),
        P("lat", None),
        P(),
    )
    out_specs = P(None, None, "lat", "lev")
    return jax.shard_map(shards, mesh=mesh, in_specs=in_specs, out_specs=out_specs, check_vma=False)
```

time: 93.3 us -> 88.8 us (0.952)
  the two profiles are of different devices: /device:TPU:8 before, /device:TPU:0 now
where the time goes in v4:
time: 88.8 us; the launch traced here: 88.6 us
  starting transfers between devices  41.5 us (47%)
  Pallas kernels  31.6 us (36%)
  waiting for transfers between devices  14.3 us (16%)
  local copies, waits for them, and re-layouts  1.04 us (1%)
    ppermute x14, starting transfers between devices, turned_exchange(): lax.ppermute(x, 'lev', [(i, i ^ turn) for i in range(owner_count)])  37.8 us
    ppermute x14, waiting for transfers between devices, turned_exchange(): lax.ppermute(x, 'lev', [(i, i ^ turn) for i in range(owner_count)])  14.3 us
    pallas_call x1, Pallas kernels, shards(): pl.pallas_call(functools.partial(edge_kernel, lat_rows, by_turn), in_spec...  8.96 us
    pallas_call x1, Pallas kernels, shards(): pl.pallas_call(functools.partial(inner_kernel, lat_rows, by_turn), in_spe...  7.72 us
    pallas_call x1, Pallas kernels, shards(): pl.pallas_call(functools.partial(last_kernel, edge_rows, inner_rows, by_t...  7.45 us
    pallas_call x1, Pallas kernels, shards(): pl.pallas_call(functools.partial(half_kernel, lat_rows, inner_rows, by_tu...  6.27 us
    ppermute x1, starting transfers between devices, shards(): before = lax.ppermute(last, 'lat', up)  2.38 us
  transfers between devices with their start and end apart: 16, of which 6 were waited for; matrix products, arithmetic and copies ran while one was open for 0% of the time, Pallas kernels for 19%

profile of v4, /device:TPU:0, one launch (start us, length us, event | category | flops | bytes accessed | tf_op | source)
XLA Modules:
  0.0 88.6 jit_solution(10143545849234862469)
XLA Ops:
  0.0 7.7 %inner_rows.1 = (bf16[4,3,4,16,128]{4,3,2,1,0:T(8,128)(2,1)}, bf16[4,3,4,16,128]{4,3,2,1,0:T(8,128)(2,1)}, bf16[4,3,4,16,128]{4,3,2,1,0:T(8,128)(2,1)}, bf16[4,3...) custom-call(s32[1,8]{1,0:T(1,128)} %counts_ref.9, ...), custom_call_target="tpu_custom_call" | custom-call | flops 1 | bytes 1 | tf_op jit(solution)/shard_map/inner_rows/pallas_call | solution.py:497
  7.7 2.4 %collective-permute-start = (bf16[6,2,16,1152]{3,2,1,0:T(8,128)(2,1)}, bf16[6,2,16,1152]{3,2,1,0:T(8,128)(2,1)S(1)}, u32[]{:S(2)}, u32[]{:S(2)}) collective-permute-start(bf16[6,2,16,1152]{3,2,1,0:T(8,128)(2,1)} %get-tuple-element.41), channel_id=1, source_target_pairs={{0,8},{8,16},{16,24},{1,9},{9,17},{17,25},{2,10},{10,18},{18,26},{... | collective-permute-start | bytes 1327112 | tf_op jit(solution)/shard_map/ppermute | solution.py:529
  10.1 3.5 %collective-permute-start.2 = (bf16[4,9,4,16,128]{4,3,2,1,0:T(8,128)(2,1)}, bf16[4,9,4,16,128]{4,3,2,1,0:T(8,128)(2,1)S(1)}, u32[]{:S(2)}, u32[]{:S(2)}) collective-permute-start(bf16[4,9,4,16,128]{4,3,2,1,0:T(8,128)(2,1)} %get-tuple-element.47), channel_id=1, source_target_pairs={{0,4},{1,5},{2,6},{3,7},{4,0},{5,1},{6,2},{7,3},{8,12},{9,13},{10,... | collective-permute-start | bytes 1769480 | tf_op jit(solution)/shard_map/ppermute | solution.py:522
  13.6 1.3 %collective-permute-start.1 = (bf16[6,2,16,1152]{3,2,1,0:T(8,128)(2,1)}, bf16[6,2,16,1152]{3,2,1,0:T(8,128)(2,1)S(1)}, u32[]{:S(2)}, u32[]{:S(2)}) collective-permute-start(bf16[6,2,16,1152]{3,2,1,0:T(8,128)(2,1)} %get-tuple-element.42), channel_id=1, source_target_pairs={{8,0},{16,8},{24,16},{9,1},{17,9},{25,17},{10,2},{18,10},{26,18},{... | collective-permute-start | bytes 1327112 | tf_op jit(solution)/shard_map/ppermute | solution.py:530
  14.9 1.6 %collective-permute-start.7 = (bf16[4,3,4,16,128]{4,3,2,1,0:T(8,128)(2,1)}, bf16[4,3,4,16,128]{4,3,2,1,0:T(8,128)(2,1)S(1)}, u32[]{:S(2)}, u32[]{:S(2)}) collective-permute-start(bf16[4,3,4,16,128]{4,3,2,1,0:T(8,128)(2,1)} %get-tuple-element.56), channel_id=1, source_target_pairs={{0,1},{1,0},{2,3},{3,2},{4,5},{5,4},{6,7},{7,6},{8,9},{9,8},{10,11... | collective-permute-start | bytes 589832 | tf_op jit(solution)/shard_map/ppermute | solution.py:522
  16.5 1.6 %collective-permute-start.8 = (bf16[4,3,4,16,128]{4,3,2,1,0:T(8,128)(2,1)}, bf16[4,3,4,16,128]{4,3,2,1,0:T(8,128)(2,1)S(1)}, u32[]{:S(2)}, u32[]{:S(2)}) collective-permute-start(bf16[4,3,4,16,128]{4,3,2,1,0:T(8,128)(2,1)} %get-tuple-element.57), channel_id=1, source_target_pairs={{0,2},{1,3},{2,0},{3,1},{4,6},{5,7},{6,4},{7,5},{8,10},{9,11},{10,... | collective-permute-start | bytes 589832 | tf_op jit(solution)/shard_map/ppermute | solution.py:522
  19.6 9.0 %edge_rows.1 = (bf16[4,3,4,16,128]{4,3,2,1,0:T(8,128)(2,1)}, bf16[4,3,4,16,128]{4,3,2,1,0:T(8,128)(2,1)}, bf16[4,3,4,16,128]{4,3,2,1,0:T(8,128)(2,1)}, bf16[4,3,...) custom-call(s32[1,8]{1,0:T(1,128)} %counts_ref.9, ...), custom_call_target="tpu_custom_call" | custom-call | flops 1 | bytes 1 | tf_op jit(solution)/shard_map/edge_rows/pallas_call | solution.py:533
  28.6 2.5 %collective-permute-done.8.refs_2_ = bf16[4,3,4,16,128]{4,3,2,1,0:T(8,128)(2,1)S(1)} collective-permute-done((bf16[4,3,4,16,128]{4,3,2,1,0:T(8,128)(2,1)}, bf16[4,3,4,16,128]{4,3,2,1,0:T(8,128)(2,1)S(1)}, u32[]{:S(2)}, u32[]{:S(2)}) %collective-permute-start.8) | collective-permute-done | bytes 196640 | tf_op jit(solution)/shard_map/ppermute | solution.py:522
  31.1 4.2 %collective-permute-done.9.refs_3_ = bf16[4,3,4,16,128]{4,3,2,1,0:T(8,128)(2,1)S(1)} collective-permute-done((bf16[4,3,4,16,128]{4,3,2,1,0:T(8,128)(2,1)}, bf16[4,3,4,16,128]{4,3,2,1,0:T(8,128)(2,1)S(1)}, u32[]{:S(2)}, u32[]{:S(2)}) %collective-permute-start.9) | collective-permute-done | bytes 196640 | tf_op jit(solution)/shard_map/ppermute | solution.py:522
  35.3 3.2 %collective-permute-start.10 = (bf16[4,3,4,16,128]{4,3,2,1,0:T(8,128)(2,1)}, bf16[4,3,4,16,128]{4,3,2,1,0:T(8,128)(2,1)S(1)}, u32[]{:S(2)}, u32[]{:S(2)}) collective-permute-start(bf16[4,3,4,16,128]{4,3,2,1,0:T(8,128)(2,1)} %get-tuple-element.62), channel_id=1, source_target_pairs={{0,5},{1,4},{2,7},{3,6},{4,1},{5,0},{6,3},{7,2},{8,13},{9,12},{10,... | collective-permute-start | bytes 589832 | tf_op jit(solution)/shard_map/ppermute | solution.py:522
  38.5 2.5 %collective-permute-start.11 = (bf16[4,3,4,16,128]{4,3,2,1,0:T(8,128)(2,1)}, bf16[4,3,4,16,128]{4,3,2,1,0:T(8,128)(2,1)S(1)}, u32[]{:S(2)}, u32[]{:S(2)}) collective-permute-start(bf16[4,3,4,16,128]{4,3,2,1,0:T(8,128)(2,1)} %get-tuple-element.63), channel_id=1, source_target_pairs={{0,6},{1,7},{2,4},{3,5},{4,2},{5,3},{6,0},{7,1},{8,14},{9,15},{10,... | collective-permute-start | bytes 589832 | tf_op jit(solution)/shard_map/ppermute | solution.py:522
  41.0 1.2 %mirror_rows.1 = (bf16[4,3,4,16,128]{4,3,2,1,0:T(8,128)(2,1)S(1)}, bf16[4,3,4,16,128]{4,3,2,1,0:T(8,128)(2,1)S(1)}, bf16[4,3,4,16,128]{4,3,2,1,0:T(8,128)(2,1)S(1)}, bf16[4,3,4,16,128]{4,3,2,1,0:T(8,128)(2,1)S(1)}) custom-call(s32[1,8]{1,0:T(1,128)S(1)} %copy-done.6, bf16[4,9,4,16,128]{4,3,2,1,0:T(8,128)(2,1)S(1)} %collective-permute-done.2.raw_ref), custom_call_target="tpu_custom_call" | custom-call | flops 1 | bytes 1 | tf_op jit(solution)/shard_map/mirror_rows/pallas_call | solution.py:549
  42.2 1.6 %collective-permute-start.13 = (bf16[4,3,4,16,128]{4,3,2,1,0:T(8,128)(2,1)S(1)}, bf16[4,3,4,16,128]{4,3,2,1,0:T(8,128)(2,1)S(1)}, u32[]{:S(2)}, u32[]{:S(2)}) collective-permute-start(bf16[4,3,4,16,128]{4,3,2,1,0:T(8,128)(2,1)S(1)} %get-tuple-element.70), channel_id=1, source_target_pairs={{0,1},{1,0},{2,3},{3,2},{4,5},{5,4},{6,7},{7,6},{8,9},{9,8},{10,11... | collective-permute-start | bytes 589832 | tf_op jit(solution)/shard_map/ppermute | solution.py:522
  43.7 9.0 %collective-permute-start.14 = (bf16[4,3,4,16,128]{4,3,2,1,0:T(8,128)(2,1)S(1)}, bf16[4,3,4,16,128]{4,3,2,1,0:T(8,128)(2,1)S(1)}, u32[]{:S(2)}, u32[]{:S(2)}) collective-permute-start(bf16[4,3,4,16,128]{4,3,2,1,0:T(8,128)(2,1)S(1)} %get-tuple-element.71), channel_id=1, source_target_pairs={{0,2},{1,3},{2,0},{3,1},{4,6},{5,7},{6,4},{7,5},{8,10},{9,11},{10,... | collective-permute-start | bytes 589832 | tf_op jit(solution)/shard_map/ppermute | solution.py:522
  52.7 1.0 %collective-permute-done.10.refs_5_ = bf16[4,3,4,16,128]{4,3,2,1,0:T(8,128)(2,1)S(1)} collective-permute-done((bf16[4,3,4,16,128]{4,3,2,1,0:T(8,128)(2,1)}, bf16[4,3,4,16,128]{4,3,2,1,0:T(8,128)(2,1)S(1)}, u32[]{:S(2)}, u32[]{:S(2)}) %collective-permute-start.10) | collective-permute-done | bytes 196640 | tf_op jit(solution)/shard_map/ppermute | solution.py:522
  53.8 4.7 %collective-permute-start.12 = (bf16[4,3,4,16,128]{4,3,2,1,0:T(8,128)(2,1)}, bf16[4,3,4,16,128]{4,3,2,1,0:T(8,128)(2,1)S(1)}, u32[]{:S(2)}, u32[]{:S(2)}) collective-permute-start(bf16[4,3,4,16,128]{4,3,2,1,0:T(8,128)(2,1)} %get-tuple-element.64), channel_id=1, source_target_pairs={{0,7},{1,6},{2,5},{3,4},{4,3},{5,2},{6,1},{7,0},{8,15},{9,14},{10,... | collective-permute-start | bytes 589832 | tf_op jit(solution)/shard_map/ppermute | solution.py:522
  58.5 1.8 %collective-permute-start.6 = (bf16[4,3,4,16,128]{4,3,2,1,0:T(8,128)(2,1)}, bf16[4,3,4,16,128]{4,3,2,1,0:T(8,128)(2,1)S(1)}, u32[]{:S(2)}, u32[]{:S(2)}) collective-permute-start(bf16[4,3,4,16,128]{4,3,2,1,0:T(8,128)(2,1)} %get-tuple-element.55), channel_id=1, source_target_pairs={{0,4},{1,5},{2,6},{3,7},{4,0},{5,1},{6,2},{7,3},{8,12},{9,13},{10,... | collective-permute-start | bytes 589832 | tf_op jit(solution)/shard_map/ppermute | solution.py:522
  60.3 1.5 %collective-permute-start.3 = (bf16[4,3,4,16,128]{4,3,2,1,0:T(8,128)(2,1)}, bf16[4,3,4,16,128]{4,3,2,1,0:T(8,128)(2,1)S(1)}, u32[]{:S(2)}, u32[]{:S(2)}) collective-permute-start(bf16[4,3,4,16,128]{4,3,2,1,0:T(8,128)(2,1)} %get-tuple-element.52), channel_id=1, source_target_pairs={{0,1},{1,0},{2,3},{3,2},{4,5},{5,4},{6,7},{7,6},{8,9},{9,8},{10,11... | collective-permute-start | bytes 589832 | tf_op jit(solution)/shard_map/ppermute | solution.py:522
  61.8 6.5 %collective-permute-start.4 = (bf16[4,3,4,16,128]{4,3,2,1,0:T(8,128)(2,1)}, bf16[4,3,4,16,128]{4,3,2,1,0:T(8,128)(2,1)S(1)}, u32[]{:S(2)}, u32[]{:S(2)}) collective-permute-start(bf16[4,3,4,16,128]{4,3,2,1,0:T(8,128)(2,1)} %get-tuple-element.53), channel_id=1, source_target_pairs={{0,2},{1,3},{2,0},{3,1},{4,6},{5,7},{6,4},{7,5},{8,10},{9,11},{10,... | collective-permute-start | bytes 589832 | tf_op jit(solution)/shard_map/ppermute | solution.py:522
  68.4 6.3 %inner_columns.1 = (bf16[4,512,384]{2,1,0:T(8,128)(2,1)S(1)}, bf16[512,512]{1,0:T(8,128)(2,1)S(1)}, bf16[512,512]{1,0:T(8,128)(2,1)S(1)}, bf16[512,512]{1,0:T(8,128)(2,1)S(1)}) custom-call(s32[4,6]{1,0:T(4,128)S(1)} %copy-done.7, s32[1,8]{1,0:T(1,128)S(1)} %copy-done.6, bf16[4,3,4,16,128]{4,3,2,1,0:T(8,128)(2,1)S(1)} %copy-done.3, ...), custom_call_target="tpu_custom_call" | custom-call | flops 1 | bytes 1 | tf_op jit(solution)/shard_map/inner_columns/pallas_call | solution.py:597
  74.7 0.9 %collective-permute-done.6.refs_4_ = bf16[4,3,4,16,128]{4,3,2,1,0:T(8,128)(2,1)S(1)} collective-permute-done((bf16[4,3,4,16,128]{4,3,2,1,0:T(8,128)(2,1)}, bf16[4,3,4,16,128]{4,3,2,1,0:T(8,128)(2,1)S(1)}, u32[]{:S(2)}, u32[]{:S(2)}) %collective-permute-start.6) | collective-permute-done | bytes 196640 | tf_op jit(solution)/shard_map/ppermute | solution.py:522
  75.6 1.4 %collective-permute-done.4.refs_2_ = bf16[4,3,4,16,128]{4,3,2,1,0:T(8,128)(2,1)S(1)} collective-permute-done((bf16[4,3,4,16,128]{4,3,2,1,0:T(8,128)(2,1)}, bf16[4,3,4,16,128]{4,3,2,1,0:T(8,128)(2,1)S(1)}, u32[]{:S(2)}, u32[]{:S(2)}) %collective-permute-start.4) | collective-permute-done | bytes 196640 | tf_op jit(solution)/shard_map/ppermute | solution.py:522
  77.0 4.1 %collective-permute-done.5.refs_3_ = bf16[4,3,4,16,128]{4,3,2,1,0:T(8,128)(2,1)S(1)} collective-permute-done((bf16[4,3,4,16,128]{4,3,2,1,0:T(8,128)(2,1)}, bf16[4,3,4,16,128]{4,3,2,1,0:T(8,128)(2,1)S(1)}, u32[]{:S(2)}, u32[]{:S(2)}) %collective-permute-start.5) | collective-permute-done | bytes 196640 | tf_op jit(solution)/shard_map/ppermute | solution.py:522
  81.1 7.5 %edge_columns.1 = bf16[512,8,384]{2,1,0:T(8,128)(2,1)} custom-call(s32[4,6]{1,0:T(4,128)S(1)} %copy-done.7, s32[1,8]{1,0:T(1,128)S(1)} %copy-done.6, bf16[4,3,4,16,128]{4,3,2,1,0:T(8,128)(2,1)S(1)} %copy-done.4, bf16[4,3,4,16,128]{4,3,2,1,0:T(8,128)(2,1)S(1)} %collective-permute-done.3.refs_1_, ...), custom_call_target="tpu_custom_call" | custom-call | flops 1 | bytes 1 | tf_op jit(solution)/shard_map/edge_columns/pallas_call | solution.py:609
  (33 shorter events, 1.6 us)
Async XLA Ops:
  7.7 33.3 %copy-start.6 = (s32[1,8]{1,0:T(1,128)S(1)}, s32[1,8]{1,0:T(1,128)}, u32[]{:S(2)}) copy-start(s32[1,8]{1,0:T(1,128)} %counts_ref.9) | copy-start | bytes 100
  7.7 10.3 %collective-permute-start = (bf16[6,2,16,1152]{3,2,1,0:T(8,128)(2,1)}, bf16[6,2,16,1152]{3,2,1,0:T(8,128)(2,1)S(1)}, u32[]{:S(2)}, u32[]{:S(2)}) collective-permute-start(bf16[6,2,16,1152]{3,2,1,0:T(8,128)(2,1)} %get-tuple-element.41), channel_id=1, source_target_pairs={{0,8},{8,16},{16,24},{1,9},{9,17},{17,25},{2,10},{10,18},{18,26},{... | collective-permute-start | bytes 1327112 | tf_op jit(solution)/shard_map/ppermute | solution.py:529
  10.1 30.8 %collective-permute-start.2 = (bf16[4,9,4,16,128]{4,3,2,1,0:T(8,128)(2,1)}, bf16[4,9,4,16,128]{4,3,2,1,0:T(8,128)(2,1)S(1)}, u32[]{:S(2)}, u32[]{:S(2)}) collective-permute-start(bf16[4,9,4,16,128]{4,3,2,1,0:T(8,128)(2,1)} %get-tuple-element.47), channel_id=1, source_target_pairs={{0,4},{1,5},{2,6},{3,7},{4,0},{5,1},{6,2},{7,3},{8,12},{9,13},{10,... | collective-permute-start | bytes 1769480 | tf_op jit(solution)/shard_map/ppermute | solution.py:522
  13.6 5.0 %collective-permute-start.1 = (bf16[6,2,16,1152]{3,2,1,0:T(8,128)(2,1)}, bf16[6,2,16,1152]{3,2,1,0:T(8,128)(2,1)S(1)}, u32[]{:S(2)}, u32[]{:S(2)}) collective-permute-start(bf16[6,2,16,1152]{3,2,1,0:T(8,128)(2,1)} %get-tuple-element.42), channel_id=1, source_target_pairs={{8,0},{16,8},{24,16},{9,1},{17,9},{25,17},{10,2},{18,10},{26,18},{... | collective-permute-start | bytes 1327112 | tf_op jit(solution)/shard_map/ppermute | solution.py:530
  14.9 13.7 %collective-permute-start.7 = (bf16[4,3,4,16,128]{4,3,2,1,0:T(8,128)(2,1)}, bf16[4,3,4,16,128]{4,3,2,1,0:T(8,128)(2,1)S(1)}, u32[]{:S(2)}, u32[]{:S(2)}) collective-permute-start(bf16[4,3,4,16,128]{4,3,2,1,0:T(8,128)(2,1)} %get-tuple-element.56), channel_id=1, source_target_pairs={{0,1},{1,0},{2,3},{3,2},{4,5},{5,4},{6,7},{7,6},{8,9},{9,8},{10,11... | collective-permute-start | bytes 589832 | tf_op jit(solution)/shard_map/ppermute | solution.py:522
  16.5 14.7 %collective-permute-start.8 = (bf16[4,3,4,16,128]{4,3,2,1,0:T(8,128)(2,1)}, bf16[4,3,4,16,128]{4,3,2,1,0:T(8,128)(2,1)S(1)}, u32[]{:S(2)}, u32[]{:S(2)}) collective-permute-start(bf16[4,3,4,16,128]{4,3,2,1,0:T(8,128)(2,1)} %get-tuple-element.57), channel_id=1, source_target_pairs={{0,2},{1,3},{2,0},{3,1},{4,6},{5,7},{6,4},{7,5},{8,10},{9,11},{10,... | collective-permute-start | bytes 589832 | tf_op jit(solution)/shard_map/ppermute | solution.py:522
  18.0 50.3 %copy-start = (bf16[512,512]{1,0:T(8,128)(2,1)S(1)}, bf16[512,512]{1,0:T(8,128)(2,1)}, u32[]{:S(2)}) copy-start(bf16[512,512]{1,0:T(8,128)(2,1)} %refs_9_.2) | copy-start | bytes 1572868
  18.0 50.3 %copy-start.1 = (bf16[512,512]{1,0:T(8,128)(2,1)S(1)}, bf16[512,512]{1,0:T(8,128)(2,1)}, u32[]{:S(2)}) copy-start(bf16[512,512]{1,0:T(8,128)(2,1)} %refs_10_.1) | copy-start | bytes 1572868
  18.0 50.3 %copy-start.2 = (bf16[512,512]{1,0:T(8,128)(2,1)S(1)}, bf16[512,512]{1,0:T(8,128)(2,1)}, u32[]{:S(2)}) copy-start(bf16[512,512]{1,0:T(8,128)(2,1)} %refs_11_.1) | copy-start | bytes 1572868
  18.1 50.3 %copy-start.3 = (bf16[4,3,4,16,128]{4,3,2,1,0:T(8,128)(2,1)S(1)}, bf16[4,3,4,16,128]{4,3,2,1,0:T(8,128)(2,1)}, u32[]{:S(2)}) copy-start(bf16[4,3,4,16,128]{4,3,2,1,0:T(8,128)(2,1)} %get-tuple-element.65.refs_0_) | copy-start | bytes 589828
  18.1 50.3 %copy-start.5 = (bf16[128,128]{1,0:T(8,128)(2,1)S(1)}, bf16[128,128]{1,0:T(8,128)(2,1)}, u32[]{:S(2)}) copy-start(bf16[128,128]{1,0:T(8,128)(2,1)} %refs_9_.3) | copy-start | bytes 98308
  18.1 50.3 %copy-start.7 = (s32[4,6]{1,0:T(4,128)S(1)}, s32[4,6]{1,0:T(4,128)}, u32[]{:S(2)}) copy-start(s32[4,6]{1,0:T(4,128)} %groups_ref.3) | copy-start | bytes 292
  18.1 17.2 %collective-permute-start.9 = (bf16[4,3,4,16,128]{4,3,2,1,0:T(8,128)(2,1)}, bf16[4,3,4,16,128]{4,3,2,1,0:T(8,128)(2,1)S(1)}, u32[]{:S(2)}, u32[]{:S(2)}) collective-permute-start(bf16[4,3,4,16,128]{4,3,2,1,0:T(8,128)(2,1)} %get-tuple-element.58), channel_id=1, source_target_pairs={{0,3},{1,2},{2,1},{3,0},{4,7},{5,6},{6,5},{7,4},{8,11},{9,10},{10,... | collective-permute-start | bytes 589832 | tf_op jit(solution)/shard_map/ppermute | solution.py:522
  28.6 52.6 %copy-start.4 = (bf16[4,3,4,16,128]{4,3,2,1,0:T(8,128)(2,1)S(1)}, bf16[4,3,4,16,128]{4,3,2,1,0:T(8,128)(2,1)}, u32[]{:S(2)}) copy-start(bf16[4,3,4,16,128]{4,3,2,1,0:T(8,128)(2,1)} %get-tuple-element.43.refs_0_) | copy-start | bytes 589828
  35.3 18.4 %collective-permute-start.10 = (bf16[4,3,4,16,128]{4,3,2,1,0:T(8,128)(2,1)}, bf16[4,3,4,16,128]{4,3,2,1,0:T(8,128)(2,1)S(1)}, u32[]{:S(2)}, u32[]{:S(2)}) collective-permute-start(bf16[4,3,4,16,128]{4,3,2,1,0:T(8,128)(2,1)} %get-tuple-element.62), channel_id=1, source_target_pairs={{0,5},{1,4},{2,7},{3,6},{4,1},{5,0},{6,3},{7,2},{8,13},{9,12},{10,... | collective-permute-start | bytes 589832 | tf_op jit(solution)/shard_map/ppermute | solution.py:522
  38.5 20.0 %collective-permute-start.11 = (bf16[4,3,4,16,128]{4,3,2,1,0:T(8,128)(2,1)}, bf16[4,3,4,16,128]{4,3,2,1,0:T(8,128)(2,1)S(1)}, u32[]{:S(2)}, u32[]{:S(2)}) collective-permute-start(bf16[4,3,4,16,128]{4,3,2,1,0:T(8,128)(2,1)} %get-tuple-element.63), channel_id=1, source_target_pairs={{0,6},{1,7},{2,4},{3,5},{4,2},{5,3},{6,0},{7,1},{8,14},{9,15},{10,... | collective-permute-start | bytes 589832 | tf_op jit(solution)/shard_map/ppermute | solution.py:522
  42.2 18.2 %collective-permute-start.13 = (bf16[4,3,4,16,128]{4,3,2,1,0:T(8,128)(2,1)S(1)}, bf16[4,3,4,16,128]{4,3,2,1,0:T(8,128)(2,1)S(1)}, u32[]{:S(2)}, u32[]{:S(2)}) collective-permute-start(bf16[4,3,4,16,128]{4,3,2,1,0:T(8,128)(2,1)S(1)} %get-tuple-element.70), channel_id=1, source_target_pairs={{0,1},{1,0},{2,3},{3,2},{4,5},{5,4},{6,7},{7,6},{8,9},{9,8},{10,11... | collective-permute-start | bytes 589832 | tf_op jit(solution)/shard_map/ppermute | solution.py:522
  43.7 18.1 %collective-permute-start.14 = (bf16[4,3,4,16,128]{4,3,2,1,0:T(8,128)(2,1)S(1)}, bf16[4,3,4,16,128]{4,3,2,1,0:T(8,128)(2,1)S(1)}, u32[]{:S(2)}, u32[]{:S(2)}) collective-permute-start(bf16[4,3,4,16,128]{4,3,2,1,0:T(8,128)(2,1)S(1)} %get-tuple-element.71), channel_id=1, source_target_pairs={{0,2},{1,3},{2,0},{3,1},{4,6},{5,7},{6,4},{7,5},{8,10},{9,11},{10,... | collective-permute-start | bytes 589832 | tf_op jit(solution)/shard_map/ppermute | solution.py:522
  52.7 15.6 %collective-permute-start.15 = (bf16[4,3,4,16,128]{4,3,2,1,0:T(8,128)(2,1)S(1)}, bf16[4,3,4,16,128]{4,3,2,1,0:T(8,128)(2,1)S(1)}, u32[]{:S(2)}, u32[]{:S(2)}) collective-permute-start(bf16[4,3,4,16,128]{4,3,2,1,0:T(8,128)(2,1)S(1)} %get-tuple-element.72), channel_id=1, source_target_pairs={{0,3},{1,2},{2,1},{3,0},{4,7},{5,6},{6,5},{7,4},{8,11},{9,10},{10,... | collective-permute-start | bytes 589832 | tf_op jit(solution)/shard_map/ppermute | solution.py:522
  53.8 20.9 %collective-permute-start.12 = (bf16[4,3,4,16,128]{4,3,2,1,0:T(8,128)(2,1)}, bf16[4,3,4,16,128]{4,3,2,1,0:T(8,128)(2,1)S(1)}, u32[]{:S(2)}, u32[]{:S(2)}) collective-permute-start(bf16[4,3,4,16,128]{4,3,2,1,0:T(8,128)(2,1)} %get-tuple-element.64), channel_id=1, source_target_pairs={{0,7},{1,6},{2,5},{3,4},{4,3},{5,2},{6,1},{7,0},{8,15},{9,14},{10,... | collective-permute-start | bytes 589832 | tf_op jit(solution)/shard_map/ppermute | solution.py:522
  58.5 17.1 %collective-permute-start.6 = (bf16[4,3,4,16,128]{4,3,2,1,0:T(8,128)(2,1)}, bf16[4,3,4,16,128]{4,3,2,1,0:T(8,128)(2,1)S(1)}, u32[]{:S(2)}, u32[]{:S(2)}) collective-permute-start(bf16[4,3,4,16,128]{4,3,2,1,0:T(8,128)(2,1)} %get-tuple-element.55), channel_id=1, source_target_pairs={{0,4},{1,5},{2,6},{3,7},{4,0},{5,1},{6,2},{7,3},{8,12},{9,13},{10,... | collective-permute-start | bytes 589832 | tf_op jit(solution)/shard_map/ppermute | solution.py:522
  60.3 15.2 %collective-permute-start.3 = (bf16[4,3,4,16,128]{4,3,2,1,0:T(8,128)(2,1)}, bf16[4,3,4,16,128]{4,3,2,1,0:T(8,128)(2,1)S(1)}, u32[]{:S(2)}, u32[]{:S(2)}) collective-permute-start(bf16[4,3,4,16,128]{4,3,2,1,0:T(8,128)(2,1)} %get-tuple-element.52), channel_id=1, source_target_pairs={{0,1},{1,0},{2,3},{3,2},{4,5},{5,4},{6,7},{7,6},{8,9},{9,8},{10,11... | collective-permute-start | bytes 589832 | tf_op jit(solution)/shard_map/ppermute | solution.py:522
  61.8 15.2 %collective-permute-start.4 = (bf16[4,3,4,16,128]{4,3,2,1,0:T(8,128)(2,1)}, bf16[4,3,4,16,128]{4,3,2,1,0:T(8,128)(2,1)S(1)}, u32[]{:S(2)}, u32[]{:S(2)}) collective-permute-start(bf16[4,3,4,16,128]{4,3,2,1,0:T(8,128)(2,1)} %get-tuple-element.53), channel_id=1, source_target_pairs={{0,2},{1,3},{2,0},{3,1},{4,6},{5,7},{6,4},{7,5},{8,10},{9,11},{10,... | collective-permute-start | bytes 589832 | tf_op jit(solution)/shard_map/ppermute | solution.py:522
  68.3 12.8 %collective-permute-start.5 = (bf16[4,3,4,16,128]{4,3,2,1,0:T(8,128)(2,1)}, bf16[4,3,4,16,128]{4,3,2,1,0:T(8,128)(2,1)S(1)}, u32[]{:S(2)}, u32[]{:S(2)}) collective-permute-start(bf16[4,3,4,16,128]{4,3,2,1,0:T(8,128)(2,1)} %get-tuple-element.54), channel_id=1, source_target_pairs={{0,3},{1,2},{2,1},{3,0},{4,7},{5,6},{6,5},{7,4},{8,11},{9,10},{10,... | collective-permute-start | bytes 589832 | tf_op jit(solution)/shard_map/ppermute | solution.py:522
  (2 other events, 1.5 us)

commit v5 on v4

--- a/solution.py
+++ b/solution.py
@@ -522,7 +522,7 @@
         return lax.ppermute(x, "lev", [(i, i ^ turn) for i in range(owner_count)]) if turn else x
 
     if by_turn:
-        crossed = turned_exchange(inner[near], near)
+        crossed = turned_exchange(inner[near], near + near // 2)
         inner_parts = [turned_exchange(x, turn) for turn, x in enumerate(inner[:near])]
     else:
         inner_parts = [exchange(inner[0])]
@@ -560,7 +560,8 @@
         near_parts, edge[near + 1 :] = lax.optimization_barrier((near_parts, edge[near + 1 :]))
         inner_parts = inner_parts[:1] + near_parts
         edge_parts = [turned_exchange(x, turn) for turn, x in enumerate(edge)]
-        inner_parts += [turned_exchange(x, turn) for turn, x in enumerate(mirrored)]
+        mirrored = [turned_exchange(x, turn) for turn, x in enumerate(mirrored)]
+        inner_parts += [mirrored[turn ^ (near // 2)] for turn in range(near)]
     else:
         edge_parts = [exchange(edge[0])]
 

time: 88.8 us -> 87.1 us (0.981)
  starting transfers between devices: 41.5 us -> 24.9 us
  waiting for transfers between devices: 14.3 us -> 29.4 us
    ppermute x14, starting transfers between devices: 37.8 us -> 21.3 us  [turned_exchange(): lax.ppermute(x, 'lev', [(i, i ^ turn) for i in range(owner_count)])]
    ppermute x14, waiting for transfers between devices: 14.3 us -> 29.4 us  [turned_exchange(): lax.ppermute(x, 'lev', [(i, i ^ turn) for i in range(owner_count)])]
  transfers between devices with their start and end apart: 16 -> 16, of which waited for: 6 -> 7; matrix products, arithmetic and copies ran while one was open for 0% -> 0% of each run, Pallas kernels for 19% -> 19%
where the time goes in v5:
time: 87.1 us; the launch traced here: 86.9 us
  Pallas kernels  31.6 us (36%)
  waiting for transfers between devices  29.4 us (34%)
  starting transfers between devices  24.9 us (29%)
    ppermute x14, waiting for transfers between devices, turned_exchange(): lax.ppermute(x, 'lev', [(i, i ^ turn) for i in range(owner_count)])  29.4 us
    ppermute x14, starting transfers between devices, turned_exchange(): lax.ppermute(x, 'lev', [(i, i ^ turn) for i in range(owner_count)])  21.3 us
    pallas_call x1, Pallas kernels, shards(): pl.pallas_call(functools.partial(edge_kernel, lat_rows, by_turn), in_spec...  8.96 us
    pallas_call x1, Pallas kernels, shards(): pl.pallas_call(functools.partial(inner_kernel, lat_rows, by_turn), in_spe...  7.72 us
    pallas_call x1, Pallas kernels, shards(): pl.pallas_call(functools.partial(last_kernel, edge_rows, inner_rows, by_t...  7.46 us
    pallas_call x1, Pallas kernels, shards(): pl.pallas_call(functools.partial(half_kernel, lat_rows, inner_rows, by_tu...  6.26 us
    ppermute x1, starting transfers between devices, shards(): before = lax.ppermute(last, 'lat', up)  2.38 us
  transfers between devices with their start and end apart: 16, of which 7 were waited for; matrix products, arithmetic and copies ran while one was open for 0% of the time, Pallas kernels for 19%

profile of v5, /device:TPU:0, one launch (start us, length us, event | category | flops | bytes accessed | tf_op | source)
XLA Modules:
  0.0 86.9 jit_solution(5581055936213462096)
XLA Ops:
  0.0 7.7 %inner_rows.1 = (bf16[4,3,4,16,128]{4,3,2,1,0:T(8,128)(2,1)}, bf16[4,3,4,16,128]{4,3,2,1,0:T(8,128)(2,1)}, bf16[4,3,4,16,128]{4,3,2,1,0:T(8,128)(2,1)}, bf16[4,3...) custom-call(s32[1,8]{1,0:T(1,128)} %counts_ref.9, ...), custom_call_target="tpu_custom_call" | custom-call | flops 1 | bytes 1 | tf_op jit(solution)/shard_map/inner_rows/pallas_call | solution.py:497
  7.7 2.4 %collective-permute-start = (bf16[6,2,16,1152]{3,2,1,0:T(8,128)(2,1)}, bf16[6,2,16,1152]{3,2,1,0:T(8,128)(2,1)S(1)}, u32[]{:S(2)}, u32[]{:S(2)}) collective-permute-start(bf16[6,2,16,1152]{3,2,1,0:T(8,128)(2,1)} %get-tuple-element.41), channel_id=1, source_target_pairs={{0,8},{8,16},{16,24},{1,9},{9,17},{17,25},{2,10},{10,18},{18,26},{... | collective-permute-start | bytes 1327112 | tf_op jit(solution)/shard_map/ppermute | solution.py:529
  10.1 4.5 %collective-permute-start.2 = (bf16[4,9,4,16,128]{4,3,2,1,0:T(8,128)(2,1)}, bf16[4,9,4,16,128]{4,3,2,1,0:T(8,128)(2,1)S(1)}, u32[]{:S(2)}, u32[]{:S(2)}) collective-permute-start(bf16[4,9,4,16,128]{4,3,2,1,0:T(8,128)(2,1)} %get-tuple-element.47), channel_id=1, source_target_pairs={{0,6},{1,7},{2,4},{3,5},{4,2},{5,3},{6,0},{7,1},{8,14},{9,15},{10,... | collective-permute-start | bytes 1769480 | tf_op jit(solution)/shard_map/ppermute | solution.py:522
  14.6 1.3 %collective-permute-start.1 = (bf16[6,2,16,1152]{3,2,1,0:T(8,128)(2,1)}, bf16[6,2,16,1152]{3,2,1,0:T(8,128)(2,1)S(1)}, u32[]{:S(2)}, u32[]{:S(2)}) collective-permute-start(bf16[6,2,16,1152]{3,2,1,0:T(8,128)(2,1)} %get-tuple-element.42), channel_id=1, source_target_pairs={{8,0},{16,8},{24,16},{9,1},{17,9},{25,17},{10,2},{18,10},{26,18},{... | collective-permute-start | bytes 1327112 | tf_op jit(solution)/shard_map/ppermute | solution.py:530
  15.9 1.6 %collective-permute-start.7 = (bf16[4,3,4,16,128]{4,3,2,1,0:T(8,128)(2,1)}, bf16[4,3,4,16,128]{4,3,2,1,0:T(8,128)(2,1)S(1)}, u32[]{:S(2)}, u32[]{:S(2)}) collective-permute-start(bf16[4,3,4,16,128]{4,3,2,1,0:T(8,128)(2,1)} %get-tuple-element.56), channel_id=1, source_target_pairs={{0,1},{1,0},{2,3},{3,2},{4,5},{5,4},{6,7},{7,6},{8,9},{9,8},{10,11... | collective-permute-start | bytes 589832 | tf_op jit(solution)/shard_map/ppermute | solution.py:522
  17.6 2.0 %collective-permute-start.9 = (bf16[4,3,4,16,128]{4,3,2,1,0:T(8,128)(2,1)}, bf16[4,3,4,16,128]{4,3,2,1,0:T(8,128)(2,1)S(1)}, u32[]{:S(2)}, u32[]{:S(2)}) collective-permute-start(bf16[4,3,4,16,128]{4,3,2,1,0:T(8,128)(2,1)} %get-tuple-element.58), channel_id=1, source_target_pairs={{0,3},{1,2},{2,1},{3,0},{4,7},{5,6},{6,5},{7,4},{8,11},{9,10},{10,... | collective-permute-start | bytes 589832 | tf_op jit(solution)/shard_map/ppermute | solution.py:522
  19.6 0.8 copy-done.9
  20.4 9.0 %edge_rows.1 = (bf16[4,3,4,16,128]{4,3,2,1,0:T(8,128)(2,1)}, bf16[4,3,4,16,128]{4,3,2,1,0:T(8,128)(2,1)}, bf16[4,3,4,16,128]{4,3,2,1,0:T(8,128)(2,1)}, bf16[4,3,...) custom-call(s32[1,8]{1,0:T(1,128)} %counts_ref.9, ...), custom_call_target="tpu_custom_call" | custom-call | flops 1 | bytes 1 | tf_op jit(solution)/shard_map/edge_rows/pallas_call | solution.py:533
  29.4 3.9 %collective-permute-done.8.refs_2_ = bf16[4,3,4,16,128]{4,3,2,1,0:T(8,128)(2,1)S(1)} collective-permute-done((bf16[4,3,4,16,128]{4,3,2,1,0:T(8,128)(2,1)}, bf16[4,3,4,16,128]{4,3,2,1,0:T(8,128)(2,1)S(1)}, u32[]{:S(2)}, u32[]{:S(2)}) %collective-permute-start.8) | collective-permute-done | bytes 196640 | tf_op jit(solution)/shard_map/ppermute | solution.py:522
  33.2 5.4 %collective-permute-done.9.refs_3_ = bf16[4,3,4,16,128]{4,3,2,1,0:T(8,128)(2,1)S(1)} collective-permute-done((bf16[4,3,4,16,128]{4,3,2,1,0:T(8,128)(2,1)}, bf16[4,3,4,16,128]{4,3,2,1,0:T(8,128)(2,1)S(1)}, u32[]{:S(2)}, u32[]{:S(2)}) %collective-permute-start.9) | collective-permute-done | bytes 196640 | tf_op jit(solution)/shard_map/ppermute | solution.py:522
  38.6 1.8 %collective-permute-start.10 = (bf16[4,3,4,16,128]{4,3,2,1,0:T(8,128)(2,1)}, bf16[4,3,4,16,128]{4,3,2,1,0:T(8,128)(2,1)S(1)}, u32[]{:S(2)}, u32[]{:S(2)}) collective-permute-start(bf16[4,3,4,16,128]{4,3,2,1,0:T(8,128)(2,1)} %get-tuple-element.62), channel_id=1, source_target_pairs={{0,5},{1,4},{2,7},{3,6},{4,1},{5,0},{6,3},{7,2},{8,13},{9,12},{10,... | collective-permute-start | bytes 589832 | tf_op jit(solution)/shard_map/ppermute | solution.py:522
  40.4 1.8 %collective-permute-start.11 = (bf16[4,3,4,16,128]{4,3,2,1,0:T(8,128)(2,1)}, bf16[4,3,4,16,128]{4,3,2,1,0:T(8,128)(2,1)S(1)}, u32[]{:S(2)}, u32[]{:S(2)}) collective-permute-start(bf16[4,3,4,16,128]{4,3,2,1,0:T(8,128)(2,1)} %get-tuple-element.63), channel_id=1, source_target_pairs={{0,6},{1,7},{2,4},{3,5},{4,2},{5,3},{6,0},{7,1},{8,14},{9,15},{10,... | collective-permute-start | bytes 589832 | tf_op jit(solution)/shard_map/ppermute | solution.py:522
  42.2 1.2 %mirror_rows.1 = (bf16[4,3,4,16,128]{4,3,2,1,0:T(8,128)(2,1)S(1)}, bf16[4,3,4,16,128]{4,3,2,1,0:T(8,128)(2,1)S(1)}, bf16[4,3,4,16,128]{4,3,2,1,0:T(8,128)(2,1)S(1)}, bf16[4,3,4,16,128]{4,3,2,1,0:T(8,128)(2,1)S(1)}) custom-call(s32[1,8]{1,0:T(1,128)S(1)} %copy-done.6, bf16[4,9,4,16,128]{4,3,2,1,0:T(8,128)(2,1)S(1)} %collective-permute-done.2.raw_ref), custom_call_target="tpu_custom_call" | custom-call | flops 1 | bytes 1 | tf_op jit(solution)/shard_map/mirror_rows/pallas_call | solution.py:549
  44.0 2.2 %collective-permute-start.14 = (bf16[4,3,4,16,128]{4,3,2,1,0:T(8,128)(2,1)S(1)}, bf16[4,3,4,16,128]{4,3,2,1,0:T(8,128)(2,1)S(1)}, u32[]{:S(2)}, u32[]{:S(2)}) collective-permute-start(bf16[4,3,4,16,128]{4,3,2,1,0:T(8,128)(2,1)S(1)} %get-tuple-element.70), channel_id=1, source_target_pairs={{0,3},{1,2},{2,1},{3,0},{4,7},{5,6},{6,5},{7,4},{8,11},{9,10},{10,... | collective-permute-start | bytes 589832 | tf_op jit(solution)/shard_map/ppermute | solution.py:522
  47.0 9.9 %collective-permute-done.10.refs_5_ = bf16[4,3,4,16,128]{4,3,2,1,0:T(8,128)(2,1)S(1)} collective-permute-done((bf16[4,3,4,16,128]{4,3,2,1,0:T(8,128)(2,1)}, bf16[4,3,4,16,128]{4,3,2,1,0:T(8,128)(2,1)S(1)}, u32[]{:S(2)}, u32[]{:S(2)}) %collective-permute-start.10) | collective-permute-done | bytes 196640 | tf_op jit(solution)/shard_map/ppermute | solution.py:522
  56.8 2.0 %collective-permute-start.12 = (bf16[4,3,4,16,128]{4,3,2,1,0:T(8,128)(2,1)}, bf16[4,3,4,16,128]{4,3,2,1,0:T(8,128)(2,1)S(1)}, u32[]{:S(2)}, u32[]{:S(2)}) collective-permute-start(bf16[4,3,4,16,128]{4,3,2,1,0:T(8,128)(2,1)} %get-tuple-element.64), channel_id=1, source_target_pairs={{0,7},{1,6},{2,5},{3,4},{4,3},{5,2},{6,1},{7,0},{8,15},{9,14},{10,... | collective-permute-start | bytes 589832 | tf_op jit(solution)/shard_map/ppermute | solution.py:522
  58.9 2.4 %collective-permute-start.6 = (bf16[4,3,4,16,128]{4,3,2,1,0:T(8,128)(2,1)}, bf16[4,3,4,16,128]{4,3,2,1,0:T(8,128)(2,1)S(1)}, u32[]{:S(2)}, u32[]{:S(2)}) collective-permute-start(bf16[4,3,4,16,128]{4,3,2,1,0:T(8,128)(2,1)} %get-tuple-element.55), channel_id=1, source_target_pairs={{0,4},{1,5},{2,6},{3,7},{4,0},{5,1},{6,2},{7,3},{8,12},{9,13},{10,... | collective-permute-start | bytes 589832 | tf_op jit(solution)/shard_map/ppermute | solution.py:522
  61.9 5.0 %collective-permute-done.14.refs_5_ = bf16[4,3,4,16,128]{4,3,2,1,0:T(8,128)(2,1)S(1)} collective-permute-done((bf16[4,3,4,16,128]{4,3,2,1,0:T(8,128)(2,1)S(1)}, bf16[4,3,4,16,128]{4,3,2,1,0:T(8,128)(2,1)S(1)}, u32[]{:S(2)}, u32[]{:S(2)}) %collective-permute-start.14) | collective-permute-done | bytes 196640 | tf_op jit(solution)/shard_map/ppermute | solution.py:522
  66.9 1.0 %collective-permute-start.5 = (bf16[4,3,4,16,128]{4,3,2,1,0:T(8,128)(2,1)}, bf16[4,3,4,16,128]{4,3,2,1,0:T(8,128)(2,1)S(1)}, u32[]{:S(2)}, u32[]{:S(2)}) collective-permute-start(bf16[4,3,4,16,128]{4,3,2,1,0:T(8,128)(2,1)} %get-tuple-element.54), channel_id=1, source_target_pairs={{0,3},{1,2},{2,1},{3,0},{4,7},{5,6},{6,5},{7,4},{8,11},{9,10},{10,... | collective-permute-start | bytes 589832 | tf_op jit(solution)/shard_map/ppermute | solution.py:522
  67.9 6.3 %inner_columns.1 = (bf16[4,512,384]{2,1,0:T(8,128)(2,1)S(1)}, bf16[512,512]{1,0:T(8,128)(2,1)S(1)}, bf16[512,512]{1,0:T(8,128)(2,1)S(1)}, bf16[512,512]{1,0:T(8,128)(2,1)S(1)}) custom-call(s32[4,6]{1,0:T(4,128)S(1)} %copy-done.7, s32[1,8]{1,0:T(1,128)S(1)} %copy-done.6, bf16[4,3,4,16,128]{4,3,2,1,0:T(8,128)(2,1)S(1)} %copy-done.3, ...), custom_call_target="tpu_custom_call" | custom-call | flops 1 | bytes 1 | tf_op jit(solution)/shard_map/inner_columns/pallas_call | solution.py:598
  74.2 1.8 %collective-permute-done.6.refs_4_ = bf16[4,3,4,16,128]{4,3,2,1,0:T(8,128)(2,1)S(1)} collective-permute-done((bf16[4,3,4,16,128]{4,3,2,1,0:T(8,128)(2,1)}, bf16[4,3,4,16,128]{4,3,2,1,0:T(8,128)(2,1)S(1)}, u32[]{:S(2)}, u32[]{:S(2)}) %collective-permute-start.6) | collective-permute-done | bytes 196640 | tf_op jit(solution)/shard_map/ppermute | solution.py:522
  76.0 1.6 %collective-permute-done.4.refs_2_ = bf16[4,3,4,16,128]{4,3,2,1,0:T(8,128)(2,1)S(1)} collective-permute-done((bf16[4,3,4,16,128]{4,3,2,1,0:T(8,128)(2,1)}, bf16[4,3,4,16,128]{4,3,2,1,0:T(8,128)(2,1)S(1)}, u32[]{:S(2)}, u32[]{:S(2)}) %collective-permute-start.4) | collective-permute-done | bytes 196640 | tf_op jit(solution)/shard_map/ppermute | solution.py:522
  77.6 1.8 %collective-permute-done.5.refs_3_ = bf16[4,3,4,16,128]{4,3,2,1,0:T(8,128)(2,1)S(1)} collective-permute-done((bf16[4,3,4,16,128]{4,3,2,1,0:T(8,128)(2,1)}, bf16[4,3,4,16,128]{4,3,2,1,0:T(8,128)(2,1)S(1)}, u32[]{:S(2)}, u32[]{:S(2)}) %collective-permute-start.5) | collective-permute-done | bytes 196640 | tf_op jit(solution)/shard_map/ppermute | solution.py:522
  79.5 7.5 %edge_columns.1 = bf16[512,8,384]{2,1,0:T(8,128)(2,1)} custom-call(s32[4,6]{1,0:T(4,128)S(1)} %copy-done.7, s32[1,8]{1,0:T(1,128)S(1)} %copy-done.6, bf16[4,3,4,16,128]{4,3,2,1,0:T(8,128)(2,1)S(1)} %copy-done.4, bf16[4,3,4,16,128]{4,3,2,1,0:T(8,128)(2,1)S(1)} %collective-permute-done.3.refs_1_, ...), custom_call_target="tpu_custom_call" | custom-call | flops 1 | bytes 1 | tf_op jit(solution)/shard_map/edge_columns/pallas_call | solution.py:610
  (33 shorter events, 2.0 us)
Async XLA Ops:
  7.7 34.5 %copy-start.6 = (s32[1,8]{1,0:T(1,128)S(1)}, s32[1,8]{1,0:T(1,128)}, u32[]{:S(2)}) copy-start(s32[1,8]{1,0:T(1,128)} %counts_ref.9) | copy-start | bytes 100
  7.7 9.7 %collective-permute-start = (bf16[6,2,16,1152]{3,2,1,0:T(8,128)(2,1)}, bf16[6,2,16,1152]{3,2,1,0:T(8,128)(2,1)S(1)}, u32[]{:S(2)}, u32[]{:S(2)}) collective-permute-start(bf16[6,2,16,1152]{3,2,1,0:T(8,128)(2,1)} %get-tuple-element.41), channel_id=1, source_target_pairs={{0,8},{8,16},{16,24},{1,9},{9,17},{17,25},{2,10},{10,18},{18,26},{... | collective-permute-start | bytes 1327112 | tf_op jit(solution)/shard_map/ppermute | solution.py:529
  10.1 32.1 %collective-permute-start.2 = (bf16[4,9,4,16,128]{4,3,2,1,0:T(8,128)(2,1)}, bf16[4,9,4,16,128]{4,3,2,1,0:T(8,128)(2,1)S(1)}, u32[]{:S(2)}, u32[]{:S(2)}) collective-permute-start(bf16[4,9,4,16,128]{4,3,2,1,0:T(8,128)(2,1)} %get-tuple-element.47), channel_id=1, source_target_pairs={{0,6},{1,7},{2,4},{3,5},{4,2},{5,3},{6,0},{7,1},{8,14},{9,15},{10,... | collective-permute-start | bytes 1769480 | tf_op jit(solution)/shard_map/ppermute | solution.py:522
  14.6 5.0 %collective-permute-start.1 = (bf16[6,2,16,1152]{3,2,1,0:T(8,128)(2,1)}, bf16[6,2,16,1152]{3,2,1,0:T(8,128)(2,1)S(1)}, u32[]{:S(2)}, u32[]{:S(2)}) collective-permute-start(bf16[6,2,16,1152]{3,2,1,0:T(8,128)(2,1)} %get-tuple-element.42), channel_id=1, source_target_pairs={{8,0},{16,8},{24,16},{9,1},{17,9},{25,17},{10,2},{18,10},{26,18},{... | collective-permute-start | bytes 1327112 | tf_op jit(solution)/shard_map/ppermute | solution.py:530
  15.9 13.4 %collective-permute-start.7 = (bf16[4,3,4,16,128]{4,3,2,1,0:T(8,128)(2,1)}, bf16[4,3,4,16,128]{4,3,2,1,0:T(8,128)(2,1)S(1)}, u32[]{:S(2)}, u32[]{:S(2)}) collective-permute-start(bf16[4,3,4,16,128]{4,3,2,1,0:T(8,128)(2,1)} %get-tuple-element.56), channel_id=1, source_target_pairs={{0,1},{1,0},{2,3},{3,2},{4,5},{5,4},{6,7},{7,6},{8,9},{9,8},{10,11... | collective-permute-start | bytes 589832 | tf_op jit(solution)/shard_map/ppermute | solution.py:522
  17.5 15.8 %collective-permute-start.8 = (bf16[4,3,4,16,128]{4,3,2,1,0:T(8,128)(2,1)}, bf16[4,3,4,16,128]{4,3,2,1,0:T(8,128)(2,1)S(1)}, u32[]{:S(2)}, u32[]{:S(2)}) collective-permute-start(bf16[4,3,4,16,128]{4,3,2,1,0:T(8,128)(2,1)} %get-tuple-element.57), channel_id=1, source_target_pairs={{0,2},{1,3},{2,0},{3,1},{4,6},{5,7},{6,4},{7,5},{8,10},{9,11},{10,... | collective-permute-start | bytes 589832 | tf_op jit(solution)/shard_map/ppermute | solution.py:522
  17.5 50.4 %copy-start = (bf16[512,512]{1,0:T(8,128)(2,1)S(1)}, bf16[512,512]{1,0:T(8,128)(2,1)}, u32[]{:S(2)}) copy-start(bf16[512,512]{1,0:T(8,128)(2,1)} %refs_9_.2) | copy-start | bytes 1572868
  17.5 50.4 %copy-start.1 = (bf16[512,512]{1,0:T(8,128)(2,1)S(1)}, bf16[512,512]{1,0:T(8,128)(2,1)}, u32[]{:S(2)}) copy-start(bf16[512,512]{1,0:T(8,128)(2,1)} %refs_10_.1) | copy-start | bytes 1572868
  17.5 50.4 %copy-start.2 = (bf16[512,512]{1,0:T(8,128)(2,1)S(1)}, bf16[512,512]{1,0:T(8,128)(2,1)}, u32[]{:S(2)}) copy-start(bf16[512,512]{1,0:T(8,128)(2,1)} %refs_11_.1) | copy-start | bytes 1572868
  17.5 50.4 %copy-start.3 = (bf16[4,3,4,16,128]{4,3,2,1,0:T(8,128)(2,1)S(1)}, bf16[4,3,4,16,128]{4,3,2,1,0:T(8,128)(2,1)}, u32[]{:S(2)}) copy-start(bf16[4,3,4,16,128]{4,3,2,1,0:T(8,128)(2,1)} %get-tuple-element.65.refs_0_) | copy-start | bytes 589828
  17.5 50.4 %copy-start.5 = (bf16[128,128]{1,0:T(8,128)(2,1)S(1)}, bf16[128,128]{1,0:T(8,128)(2,1)}, u32[]{:S(2)}) copy-start(bf16[128,128]{1,0:T(8,128)(2,1)} %refs_9_.3) | copy-start | bytes 98308
  17.5 50.4 %copy-start.7 = (s32[4,6]{1,0:T(4,128)S(1)}, s32[4,6]{1,0:T(4,128)}, u32[]{:S(2)}) copy-start(s32[4,6]{1,0:T(4,128)} %groups_ref.3) | copy-start | bytes 292
  17.6 21.1 %collective-permute-start.9 = (bf16[4,3,4,16,128]{4,3,2,1,0:T(8,128)(2,1)}, bf16[4,3,4,16,128]{4,3,2,1,0:T(8,128)(2,1)S(1)}, u32[]{:S(2)}, u32[]{:S(2)}) collective-permute-start(bf16[4,3,4,16,128]{4,3,2,1,0:T(8,128)(2,1)} %get-tuple-element.58), channel_id=1, source_target_pairs={{0,3},{1,2},{2,1},{3,0},{4,7},{5,6},{6,5},{7,4},{8,11},{9,10},{10,... | collective-permute-start | bytes 589832 | tf_op jit(solution)/shard_map/ppermute | solution.py:522
  29.3 50.1 %copy-start.4 = (bf16[4,3,4,16,128]{4,3,2,1,0:T(8,128)(2,1)S(1)}, bf16[4,3,4,16,128]{4,3,2,1,0:T(8,128)(2,1)}, u32[]{:S(2)}) copy-start(bf16[4,3,4,16,128]{4,3,2,1,0:T(8,128)(2,1)} %get-tuple-element.43.refs_0_) | copy-start | bytes 589828
  38.6 18.2 %collective-permute-start.10 = (bf16[4,3,4,16,128]{4,3,2,1,0:T(8,128)(2,1)}, bf16[4,3,4,16,128]{4,3,2,1,0:T(8,128)(2,1)S(1)}, u32[]{:S(2)}, u32[]{:S(2)}) collective-permute-start(bf16[4,3,4,16,128]{4,3,2,1,0:T(8,128)(2,1)} %get-tuple-element.62), channel_id=1, source_target_pairs={{0,5},{1,4},{2,7},{3,6},{4,1},{5,0},{6,3},{7,2},{8,13},{9,12},{10,... | collective-permute-start | bytes 589832 | tf_op jit(solution)/shard_map/ppermute | solution.py:522
  40.4 18.5 %collective-permute-start.11 = (bf16[4,3,4,16,128]{4,3,2,1,0:T(8,128)(2,1)}, bf16[4,3,4,16,128]{4,3,2,1,0:T(8,128)(2,1)S(1)}, u32[]{:S(2)}, u32[]{:S(2)}) collective-permute-start(bf16[4,3,4,16,128]{4,3,2,1,0:T(8,128)(2,1)} %get-tuple-element.63), channel_id=1, source_target_pairs={{0,6},{1,7},{2,4},{3,5},{4,2},{5,3},{6,0},{7,1},{8,14},{9,15},{10,... | collective-permute-start | bytes 589832 | tf_op jit(solution)/shard_map/ppermute | solution.py:522
  43.4 17.9 %collective-permute-start.13 = (bf16[4,3,4,16,128]{4,3,2,1,0:T(8,128)(2,1)S(1)}, bf16[4,3,4,16,128]{4,3,2,1,0:T(8,128)(2,1)S(1)}, u32[]{:S(2)}, u32[]{:S(2)}) collective-permute-start(bf16[4,3,4,16,128]{4,3,2,1,0:T(8,128)(2,1)S(1)} %get-tuple-element.69), channel_id=1, source_target_pairs={{0,2},{1,3},{2,0},{3,1},{4,6},{5,7},{6,4},{7,5},{8,10},{9,11},{10,... | collective-permute-start | bytes 589832 | tf_op jit(solution)/shard_map/ppermute | solution.py:522
  44.0 22.9 %collective-permute-start.14 = (bf16[4,3,4,16,128]{4,3,2,1,0:T(8,128)(2,1)S(1)}, bf16[4,3,4,16,128]{4,3,2,1,0:T(8,128)(2,1)S(1)}, u32[]{:S(2)}, u32[]{:S(2)}) collective-permute-start(bf16[4,3,4,16,128]{4,3,2,1,0:T(8,128)(2,1)S(1)} %get-tuple-element.70), channel_id=1, source_target_pairs={{0,3},{1,2},{2,1},{3,0},{4,7},{5,6},{6,5},{7,4},{8,11},{9,10},{10,... | collective-permute-start | bytes 589832 | tf_op jit(solution)/shard_map/ppermute | solution.py:522
  46.3 20.6 %collective-permute-start.15 = (bf16[4,3,4,16,128]{4,3,2,1,0:T(8,128)(2,1)S(1)}, bf16[4,3,4,16,128]{4,3,2,1,0:T(8,128)(2,1)S(1)}, u32[]{:S(2)}, u32[]{:S(2)}) collective-permute-start(bf16[4,3,4,16,128]{4,3,2,1,0:T(8,128)(2,1)S(1)} %get-tuple-element.72), channel_id=1, source_target_pairs={{0,1},{1,0},{2,3},{3,2},{4,5},{5,4},{6,7},{7,6},{8,9},{9,8},{10,11... | collective-permute-start | bytes 589832 | tf_op jit(solution)/shard_map/ppermute | solution.py:522
  56.8 17.4 %collective-permute-start.12 = (bf16[4,3,4,16,128]{4,3,2,1,0:T(8,128)(2,1)}, bf16[4,3,4,16,128]{4,3,2,1,0:T(8,128)(2,1)S(1)}, u32[]{:S(2)}, u32[]{:S(2)}) collective-permute-start(bf16[4,3,4,16,128]{4,3,2,1,0:T(8,128)(2,1)} %get-tuple-element.64), channel_id=1, source_target_pairs={{0,7},{1,6},{2,5},{3,4},{4,3},{5,2},{6,1},{7,0},{8,15},{9,14},{10,... | collective-permute-start | bytes 589832 | tf_op jit(solution)/shard_map/ppermute | solution.py:522
  58.9 17.1 %collective-permute-start.6 = (bf16[4,3,4,16,128]{4,3,2,1,0:T(8,128)(2,1)}, bf16[4,3,4,16,128]{4,3,2,1,0:T(8,128)(2,1)S(1)}, u32[]{:S(2)}, u32[]{:S(2)}) collective-permute-start(bf16[4,3,4,16,128]{4,3,2,1,0:T(8,128)(2,1)} %get-tuple-element.55), channel_id=1, source_target_pairs={{0,4},{1,5},{2,6},{3,7},{4,0},{5,1},{6,2},{7,3},{8,12},{9,13},{10,... | collective-permute-start | bytes 589832 | tf_op jit(solution)/shard_map/ppermute | solution.py:522
  61.3 14.7 %collective-permute-start.3 = (bf16[4,3,4,16,128]{4,3,2,1,0:T(8,128)(2,1)}, bf16[4,3,4,16,128]{4,3,2,1,0:T(8,128)(2,1)S(1)}, u32[]{:S(2)}, u32[]{:S(2)}) collective-permute-start(bf16[4,3,4,16,128]{4,3,2,1,0:T(8,128)(2,1)} %get-tuple-element.52), channel_id=1, source_target_pairs={{0,1},{1,0},{2,3},{3,2},{4,5},{5,4},{6,7},{7,6},{8,9},{9,8},{10,11... | collective-permute-start | bytes 589832 | tf_op jit(solution)/shard_map/ppermute | solution.py:522
  66.9 10.8 %collective-permute-start.4 = (bf16[4,3,4,16,128]{4,3,2,1,0:T(8,128)(2,1)}, bf16[4,3,4,16,128]{4,3,2,1,0:T(8,128)(2,1)S(1)}, u32[]{:S(2)}, u32[]{:S(2)}) collective-permute-start(bf16[4,3,4,16,128]{4,3,2,1,0:T(8,128)(2,1)} %get-tuple-element.53), channel_id=1, source_target_pairs={{0,2},{1,3},{2,0},{3,1},{4,6},{5,7},{6,4},{7,5},{8,10},{9,11},{10,... | collective-permute-start | bytes 589832 | tf_op jit(solution)/shard_map/ppermute | solution.py:522
  66.9 12.6 %collective-permute-start.5 = (bf16[4,3,4,16,128]{4,3,2,1,0:T(8,128)(2,1)}, bf16[4,3,4,16,128]{4,3,2,1,0:T(8,128)(2,1)S(1)}, u32[]{:S(2)}, u32[]{:S(2)}) collective-permute-start(bf16[4,3,4,16,128]{4,3,2,1,0:T(8,128)(2,1)} %get-tuple-element.54), channel_id=1, source_target_pairs={{0,3},{1,2},{2,1},{3,0},{4,7},{5,6},{6,5},{7,4},{8,11},{9,10},{10,... | collective-permute-start | bytes 589832 | tf_op jit(solution)/shard_map/ppermute | solution.py:522
  (2 other events, 2.9 us)

commit v6 on v5

--- a/solution.py
+++ b/solution.py
@@ -158,16 +158,7 @@
                     packed_ref.at[field], outs[0].at[:, field], sent.at[field, 0]
                 )
             ]
-        copies = [
-            pltpu.make_async_copy(
-                packed_ref.at[field, slot], outs[slot].at[field], sent.at[field, slot]
-            )
-            for slot in range(slots)
-        ]
-        copies.append(
-            pltpu.make_async_copy(raw_ref.at[field], outs[slots].at[field], sent.at[field, slots])
-        )
-        return copies
+        return [pltpu.make_async_copy(raw_ref.at[field], outs[0].at[field], sent.at[field, 0])]
 
     def keep_halo(array):
         for row in range(HALO):
@@ -223,7 +214,8 @@
         if by_turn:
             for tile in range(tiles):
                 raw_ref[field, tile] = kept_ref[tile].astype(raw_ref.dtype)
-        pack_rows(kept_ref, turned_starts(start_ref, by_turn, slots), blocks, store)
+        else:
+            pack_rows(kept_ref, turned_starts(start_ref, False, slots), blocks, store)
         for copy in halo_out(field) + field_out(field):
             copy.start()
         return carry
@@ -406,20 +398,19 @@
     return lambda field: sorted_ref[field]
 
 
+def turn_kernel(*refs):
+    count = len(refs) // 2
+    for source_ref, out_ref in zip(refs[:count], refs[count:]):
+        out_ref[...] = source_ref[...].T
+
+
 def half_kernel(rows, row_list, by_turn, groups_ref, counts_ref, *refs):
-    out_ref, first_out, second_out, third_out, sorted_ref = refs[-5:]
-    *refs, remap_ref, first_ref, second_ref, third_ref = refs[:-5]
-
-    @pl.when(pl.program_id(0) == 0)
-    def _():
-        first_out[...] = first_ref[...].T
-        second_out[...] = second_ref[...].T
-        third_out[...] = third_ref[...].T
-
+    out_ref, sorted_ref = refs[-2:]
+    *refs, remap_ref, first_ref, second_ref, third_ref = refs[:-2]
     columns = column_source(by_turn, refs, sorted_ref)
     fields = sorted_ref.shape[0]
     remapped, tendency = column_update(
-        columns, fields, remap_ref, first_out, second_out, third_out
+        columns, fields, remap_ref, first_ref, second_ref, third_ref
     )
     live = live_lanes(counts_ref, remapped.shape[0], pl.program_id(0))
     first_row = lax.axis_index("lat") * rows
@@ -492,7 +483,7 @@
     piece = jax.ShapeDtypeStruct(payload(blocks)[1:], jnp.bfloat16)
     whole_payload = jax.ShapeDtypeStruct(payload(blocks), jnp.bfloat16)
     raw = jax.ShapeDtypeStruct(raw_shape, jnp.bfloat16)
-    inner_shapes = [piece] * near + [raw] if by_turn else [whole_payload]
+    inner_shapes = [raw] if by_turn else [whole_payload]
     starts_scratch = pltpu.SMEM((owner_count,), jnp.int32)
     *inner, first, last = pl.pallas_call(
         functools.partial(inner_kernel, lat_rows, by_turn),
@@ -521,9 +512,20 @@
     def turned_exchange(x, turn):
         return lax.ppermute(x, "lev", [(i, i ^ turn) for i in range(owner_count)]) if turn else x
 
+    def pack_half(raw_rows):
+        return pl.pallas_call(
+            mirror_kernel,
+            in_specs=[smem, pl.BlockSpec(memory_space=pltpu.VMEM)],
+            out_shape=[piece] * near,
+            scratch_shapes=[scratch((), lat_rows)[2], starts_scratch],
+            compiler_params=light,
+            cost_estimate=pl.CostEstimate(flops=1, bytes_accessed=1, transcendentals=0),
+            name="half_slots",
+        )(lon_counts, raw_rows)
+
     if by_turn:
-        crossed = turned_exchange(inner[near], near + near // 2)
-        inner_parts = [turned_exchange(x, turn) for turn, x in enumerate(inner[:near])]
+        crossed = turned_exchange(inner[0], near + near // 2)
+        inner_parts = [turned_exchange(x, turn) for turn, x in enumerate(pack_half(inner[0]))]
     else:
         inner_parts = [exchange(inner[0])]
     before = lax.ppermute(last, "lat", up)
@@ -544,20 +546,23 @@
         name="edge_rows",
     )(lon_counts, flat_fields, flat_winds, before, after)
 
+    weights = (w_first, w_second, w_third)
+    weights, _ = lax.optimization_barrier((weights, edge[0]))
+    turned = pl.pallas_call(
+        turn_kernel,
+        in_specs=[pl.BlockSpec(memory_space=pltpu.VMEM)] * len(weights),
+        out_shape=[jax.ShapeDtypeStruct(w.shape[::-1], w.dtype) for w in weights],
+        compiler_params=light,
+        cost_estimate=pl.CostEstimate(flops=1, bytes_accessed=1, transcendentals=0),
+        name="turned_weights",
+    )(*weights)
     if by_turn:
         edge = list(edge)
-        mirrored = pl.pallas_call(
-            mirror_kernel,
-            in_specs=[smem, pl.BlockSpec(memory_space=pltpu.VMEM)],
-            out_shape=[piece] * near,
-            scratch_shapes=[scratch((), lat_rows)[2], starts_scratch],
-            compiler_params=light,
-            cost_estimate=pl.CostEstimate(flops=1, bytes_accessed=1, transcendentals=0),
-            name="mirror_rows",
-        )(lon_counts, crossed)
+        edge[near:], _ = lax.optimization_barrier((edge[near:], turned))
+        mirrored = pack_half(crossed)
         edge[1:near], mirrored = lax.optimization_barrier((edge[1:near], mirrored))
         near_parts = inner_parts[1:]
-        near_parts, edge[near + 1 :] = lax.optimization_barrier((near_parts, edge[near + 1 :]))
+        near_parts, edge[near :] = lax.optimization_barrier((near_parts, edge[near :]))
         inner_parts = inner_parts[:1] + near_parts
         edge_parts = [turned_exchange(x, turn) for turn, x in enumerate(edge)]
         mirrored = [turned_exchange(x, turn) for turn, x in enumerate(mirrored)]
@@ -572,9 +577,6 @@
             1, field_count, block.shape[2], half, all_levels, LANES
         )
 
-    def whole(shape):
-        return pl.BlockSpec(shape, lambda i: (0,) * len(shape))
-
     def block_spec(block):
         return pl.BlockSpec(
             block.shape[:2] + (1,) + block.shape[3:], lambda i: (0, 0, i, 0, 0, 0)
@@ -583,7 +585,6 @@
     def cost(count):
         return pl.CostEstimate(flops=1, bytes_accessed=1, transcendentals=0)
 
-    weights = (w_first, w_second, w_third)
     weight_specs = [pl.BlockSpec(memory_space=pltpu.VMEM)] * 4
     if by_turn:
         part_specs = [
@@ -595,18 +596,17 @@
         part_specs = [block_spec(edge_parts[0])]
     sorted_scratch = pltpu.VMEM((field_count, all_levels, half * LANES), jnp.bfloat16)
     done_spec = pl.BlockSpec((half, features, LANES), lambda i: (0, 0, i))
-    done, *turned = pl.pallas_call(
+    done = pl.pallas_call(
         functools.partial(half_kernel, lat_rows, inner_rows, by_turn),
         grid=(blocks,),
         in_specs=[smem, smem] + part_specs + weight_specs,
-        out_specs=[done_spec] + [whole(w.shape[::-1]) for w in weights],
-        out_shape=[jax.ShapeDtypeStruct((half, features, slot_width), jnp.bfloat16)]
-        + [jax.ShapeDtypeStruct(w.shape[::-1], w.dtype) for w in weights],
+        out_specs=done_spec,
+        out_shape=jax.ShapeDtypeStruct((half, features, slot_width), jnp.bfloat16),
         scratch_shapes=[sorted_scratch],
         compiler_params=light,
         cost_estimate=cost(blocks),
         name="inner_columns",
-    )(group_list, lon_counts, *inner_parts, remap_weight, *weights)
+    )(group_list, lon_counts, *inner_parts, remap_weight, *turned)
     out = pl.pallas_call(
         functools.partial(last_kernel, edge_rows, inner_rows, by_turn),
         grid=(blocks,),

time: 87.1 us -> 86.7 us (level); the launches traced: 86.9 us -> 85.3 us
  waiting for transfers between devices: 29.4 us -> 27.6 us
    ppermute x14, waiting for transfers between devices: 29.4 us -> 27.6 us  [turned_exchange(): lax.ppermute(x, 'lev', [(i, i ^ turn) for i in range(owner_count)])]
    pallas_call x1 -> x3, Pallas kernels: 1.19 us -> 2.83 us  [the longest x2 2.37 us: pack_half(): pl.pallas_call(mirror_kernel, in_specs=[smem, pl.BlockSpec(memory_space=p...]
  transfers between devices with their start and end apart: 16 -> 16, of which waited for: 7 -> 6; matrix products, arithmetic and copies ran while one was open for 0% -> 0% of each run, Pallas kernels for 19% -> 21%
where the time goes in v6:
time: 86.7 us; the launch traced here: 85.3 us
  Pallas kernels  32.3 us (37%)
  waiting for transfers between devices  27.6 us (32%)
  starting transfers between devices  24.2 us (28%)
  local copies, waits for them, and re-layouts  1.11 us (1%)
    ppermute x14, waiting for transfers between devices, turned_exchange(): lax.ppermute(x, 'lev', [(i, i ^ turn) for i in range(owner_count)])  27.6 us
    ppermute x14, starting transfers between devices, turned_exchange(): lax.ppermute(x, 'lev', [(i, i ^ turn) for i in range(owner_count)])  20.5 us
    pallas_call x1, Pallas kernels, shards(): pl.pallas_call(functools.partial(edge_kernel, lat_rows, by_turn), in_spec...  8.97 us
    pallas_call x1, Pallas kernels, shards(): pl.pallas_call(functools.partial(last_kernel, edge_rows, inner_rows, by_t...  7.45 us
    pallas_call x1, Pallas kernels, shards(): pl.pallas_call(functools.partial(inner_kernel, lat_rows, by_turn), in_spe...  7.24 us
    pallas_call x1, Pallas kernels, shards(): pl.pallas_call(functools.partial(half_kernel, lat_rows, inner_rows, by_tu...  5.77 us
    ppermute x1, starting transfers between devices, shards(): before = lax.ppermute(last, 'lat', up)  2.38 us
    pallas_call x2, Pallas kernels, pack_half(): pl.pallas_call(mirror_kernel, in_specs=[smem, pl.BlockSpec(memory_space=p...  2.37 us
  transfers between devices with their start and end apart: 16, of which 6 were waited for; matrix products, arithmetic and copies ran while one was open for 0% of the time, Pallas kernels for 21%

profile of v6, /device:TPU:0, one launch (start us, length us, event | category | flops | bytes accessed | tf_op | source)
XLA Modules:
  0.0 85.3 jit_solution(2798636750554364782)
XLA Ops:
  0.0 7.2 %inner_rows.1 = (bf16[4,9,4,16,128]{4,3,2,1,0:T(8,128)(2,1)}, bf16[6,2,16,1152]{3,2,1,0:T(8,128)(2,1)}, bf16[6,2,16,1152]{3,2,1,0:T(8,128)(2,1)}) custom-call(s32[1,8]{1,0:T(1,128)} %counts_ref.11, f32[4,128,1152]{2,1,0:T(8,128)} %bitcast.3, f32[2,128,1152]{2,1,0:T(8,128)} %bitcast.5), custom_call_target="tpu_custom_call" | custom-call | flops 1 | bytes 1 | tf_op jit(solution)/shard_map/inner_rows/pallas_call | solution.py:488
  7.3 2.4 %collective-permute-start = (bf16[6,2,16,1152]{3,2,1,0:T(8,128)(2,1)}, bf16[6,2,16,1152]{3,2,1,0:T(8,128)(2,1)S(1)}, u32[]{:S(2)}, u32[]{:S(2)}) collective-permute-start(bf16[6,2,16,1152]{3,2,1,0:T(8,128)(2,1)} %get-tuple-element.48), channel_id=1, source_target_pairs={{0,8},{8,16},{16,24},{1,9},{9,17},{17,25},{2,10},{10,18},{18,26},{... | collective-permute-start | bytes 1327112 | tf_op jit(solution)/shard_map/ppermute | solution.py:531
  9.6 4.5 %collective-permute-start.2 = (bf16[4,9,4,16,128]{4,3,2,1,0:T(8,128)(2,1)}, bf16[4,9,4,16,128]{4,3,2,1,0:T(8,128)(2,1)S(1)}, u32[]{:S(2)}, u32[]{:S(2)}) collective-permute-start(bf16[4,9,4,16,128]{4,3,2,1,0:T(8,128)(2,1)} %get-tuple-element.54.raw_ref), channel_id=1, source_target_pairs={{0,6},{1,7},{2,4},{3,5},{4,2},{5,3},{6,0},{7,1},{8,14},{9,15},{10,... | collective-permute-start | bytes 1769480 | tf_op jit(solution)/shard_map/ppermute | solution.py:513
  14.1 1.3 %collective-permute-start.1 = (bf16[6,2,16,1152]{3,2,1,0:T(8,128)(2,1)}, bf16[6,2,16,1152]{3,2,1,0:T(8,128)(2,1)}, u32[]{:S(2)}, u32[]{:S(2)}) collective-permute-start(bf16[6,2,16,1152]{3,2,1,0:T(8,128)(2,1)} %get-tuple-element.49), channel_id=1, source_target_pairs={{8,0},{16,8},{24,16},{9,1},{17,9},{25,17},{10,2},{18,10},{26,18},{... | collective-permute-start | bytes 1327112 | tf_op jit(solution)/shard_map/ppermute | solution.py:532
  15.4 1.1 %copy-done = bf16[4,9,4,16,128]{4,3,2,1,0:T(8,128)(2,1)S(1)} copy-done((bf16[4,9,4,16,128]{4,3,2,1,0:T(8,128)(2,1)S(1)}, bf16[4,9,4,16,128]{4,3,2,1,0:T(8,128)(2,1)}, u32[]{:S(2)}) %copy-start) | copy-done | bytes 589848
  16.5 1.2 %half_slots.3 = (bf16[4,3,4,16,128]{4,3,2,1,0:T(8,128)(2,1)S(1)}, bf16[4,3,4,16,128]{4,3,2,1,0:T(8,128)(2,1)S(1)}, bf16[4,3,4,16,128]{4,3,2,1,0:T(8,128)(2,1)S(1)}, bf16[4,3,4,16,128]{4,3,2,1,0:T(8,128)(2,1)S(1)}) custom-call(s32[1,8]{1,0:T(1,128)S(1)} %copy-done.6, bf16[4,9,4,16,128]{4,3,2,1,0:T(8,128)(2,1)S(1)} %copy-done), custom_call_target="tpu_custom_call" | custom-call | flops 1 | bytes 1 | tf_op jit(solution)/shard_map/half_slots/pallas_call | solution.py:516
  17.7 1.6 %collective-permute-start.6 = (bf16[4,3,4,16,128]{4,3,2,1,0:T(8,128)(2,1)S(1)}, bf16[4,3,4,16,128]{4,3,2,1,0:T(8,128)(2,1)S(1)}, u32[]{:S(2)}, u32[]{:S(2)}) collective-permute-start(bf16[4,3,4,16,128]{4,3,2,1,0:T(8,128)(2,1)S(1)} %get-tuple-element.62), channel_id=1, source_target_pairs={{0,1},{1,0},{2,3},{3,2},{4,5},{5,4},{6,7},{7,6},{8,9},{9,8},{10,11... | collective-permute-start | bytes 589832 | tf_op jit(solution)/shard_map/ppermute | solution.py:513
  19.3 2.0 %collective-permute-start.8 = (bf16[4,3,4,16,128]{4,3,2,1,0:T(8,128)(2,1)S(1)}, bf16[4,3,4,16,128]{4,3,2,1,0:T(8,128)(2,1)S(1)}, u32[]{:S(2)}, u32[]{:S(2)}) collective-permute-start(bf16[4,3,4,16,128]{4,3,2,1,0:T(8,128)(2,1)S(1)} %get-tuple-element.64), channel_id=1, source_target_pairs={{0,3},{1,2},{2,1},{3,0},{4,7},{5,6},{6,5},{7,4},{8,11},{9,10},{10,... | collective-permute-start | bytes 589832 | tf_op jit(solution)/shard_map/ppermute | solution.py:513
  21.4 9.0 %edge_rows.1 = (bf16[4,3,4,16,128]{4,3,2,1,0:T(8,128)(2,1)}, bf16[4,3,4,16,128]{4,3,2,1,0:T(8,128)(2,1)}, bf16[4,3,4,16,128]{4,3,2,1,0:T(8,128)(2,1)}, bf16[4,3,...) custom-call(s32[1,8]{1,0:T(1,128)} %counts_ref.11, ...), custom_call_target="tpu_custom_call" | custom-call | flops 1 | bytes 1 | tf_op jit(solution)/shard_map/edge_rows/pallas_call | solution.py:535
  30.9 1.9 %collective-permute-done.7.refs_2_ = bf16[4,3,4,16,128]{4,3,2,1,0:T(8,128)(2,1)S(1)} collective-permute-done((bf16[4,3,4,16,128]{4,3,2,1,0:T(8,128)(2,1)S(1)}, bf16[4,3,4,16,128]{4,3,2,1,0:T(8,128)(2,1)S(1)}, u32[]{:S(2)}, u32[]{:S(2)}) %collective-permute-start.7) | collective-permute-done | bytes 196640 | tf_op jit(solution)/shard_map/ppermute | solution.py:513
  32.8 5.4 %collective-permute-done.8.refs_3_ = bf16[4,3,4,16,128]{4,3,2,1,0:T(8,128)(2,1)S(1)} collective-permute-done((bf16[4,3,4,16,128]{4,3,2,1,0:T(8,128)(2,1)S(1)}, bf16[4,3,4,16,128]{4,3,2,1,0:T(8,128)(2,1)S(1)}, u32[]{:S(2)}, u32[]{:S(2)}) %collective-permute-start.8) | collective-permute-done | bytes 196640 | tf_op jit(solution)/shard_map/ppermute | solution.py:513
  38.9 1.9 %collective-permute-start.10 = (bf16[4,3,4,16,128]{4,3,2,1,0:T(8,128)(2,1)}, bf16[4,3,4,16,128]{4,3,2,1,0:T(8,128)(2,1)S(1)}, u32[]{:S(2)}, u32[]{:S(2)}) collective-permute-start(bf16[4,3,4,16,128]{4,3,2,1,0:T(8,128)(2,1)} %get-tuple-element.80), channel_id=1, source_target_pairs={{0,5},{1,4},{2,7},{3,6},{4,1},{5,0},{6,3},{7,2},{8,13},{9,12},{10,... | collective-permute-start | bytes 589832 | tf_op jit(solution)/shard_map/ppermute | solution.py:513
  40.8 1.2 %half_slots.2 = (bf16[4,3,4,16,128]{4,3,2,1,0:T(8,128)(2,1)S(1)}, bf16[4,3,4,16,128]{4,3,2,1,0:T(8,128)(2,1)S(1)}, bf16[4,3,4,16,128]{4,3,2,1,0:T(8,128)(2,1)S(1)}, bf16[4,3,4,16,128]{4,3,2,1,0:T(8,128)(2,1)S(1)}) custom-call(s32[1,8]{1,0:T(1,128)S(1)} %copy-done.7, bf16[4,9,4,16,128]{4,3,2,1,0:T(8,128)(2,1)S(1)} %collective-permute-done.2.raw_ref), custom_call_target="tpu_custom_call" | custom-call | flops 1 | bytes 1 | tf_op jit(solution)/shard_map/half_slots/pallas_call | solution.py:516
  42.0 1.5 %collective-permute-start.13 = (bf16[4,3,4,16,128]{4,3,2,1,0:T(8,128)(2,1)S(1)}, bf16[4,3,4,16,128]{4,3,2,1,0:T(8,128)(2,1)S(1)}, u32[]{:S(2)}, u32[]{:S(2)}) collective-permute-start(bf16[4,3,4,16,128]{4,3,2,1,0:T(8,128)(2,1)S(1)} %get-tuple-element.87), channel_id=1, source_target_pairs={{0,2},{1,3},{2,0},{3,1},{4,6},{5,7},{6,4},{7,5},{8,10},{9,11},{10,... | collective-permute-start | bytes 589832 | tf_op jit(solution)/shard_map/ppermute | solution.py:513
  43.5 1.7 %collective-permute-start.14 = (bf16[4,3,4,16,128]{4,3,2,1,0:T(8,128)(2,1)S(1)}, bf16[4,3,4,16,128]{4,3,2,1,0:T(8,128)(2,1)S(1)}, u32[]{:S(2)}, u32[]{:S(2)}) collective-permute-start(bf16[4,3,4,16,128]{4,3,2,1,0:T(8,128)(2,1)S(1)} %get-tuple-element.88), channel_id=1, source_target_pairs={{0,3},{1,2},{2,1},{3,0},{4,7},{5,6},{6,5},{7,4},{8,11},{9,10},{10,... | collective-permute-start | bytes 589832 | tf_op jit(solution)/shard_map/ppermute | solution.py:513
  45.6 10.0 %collective-permute-done.9.refs_4_ = bf16[4,3,4,16,128]{4,3,2,1,0:T(8,128)(2,1)S(1)} collective-permute-done((bf16[4,3,4,16,128]{4,3,2,1,0:T(8,128)(2,1)}, bf16[4,3,4,16,128]{4,3,2,1,0:T(8,128)(2,1)S(1)}, u32[]{:S(2)}, u32[]{:S(2)}) %collective-permute-start.9) | collective-permute-done | bytes 196640 | tf_op jit(solution)/shard_map/ppermute | solution.py:513
  55.5 1.1 %collective-permute-start.11 = (bf16[4,3,4,16,128]{4,3,2,1,0:T(8,128)(2,1)}, bf16[4,3,4,16,128]{4,3,2,1,0:T(8,128)(2,1)S(1)}, u32[]{:S(2)}, u32[]{:S(2)}) collective-permute-start(bf16[4,3,4,16,128]{4,3,2,1,0:T(8,128)(2,1)} %get-tuple-element.81), channel_id=1, source_target_pairs={{0,6},{1,7},{2,4},{3,5},{4,2},{5,3},{6,0},{7,1},{8,14},{9,15},{10,... | collective-permute-start | bytes 589832 | tf_op jit(solution)/shard_map/ppermute | solution.py:513
  56.6 2.8 %collective-permute-done.10.refs_5_ = bf16[4,3,4,16,128]{4,3,2,1,0:T(8,128)(2,1)S(1)} collective-permute-done((bf16[4,3,4,16,128]{4,3,2,1,0:T(8,128)(2,1)}, bf16[4,3,4,16,128]{4,3,2,1,0:T(8,128)(2,1)S(1)}, u32[]{:S(2)}, u32[]{:S(2)}) %collective-permute-start.10) | collective-permute-done | bytes 196640 | tf_op jit(solution)/shard_map/ppermute | solution.py:513
  59.4 2.2 %collective-permute-start.12 = (bf16[4,3,4,16,128]{4,3,2,1,0:T(8,128)(2,1)}, bf16[4,3,4,16,128]{4,3,2,1,0:T(8,128)(2,1)S(1)}, u32[]{:S(2)}, u32[]{:S(2)}) collective-permute-start(bf16[4,3,4,16,128]{4,3,2,1,0:T(8,128)(2,1)} %get-tuple-element.82), channel_id=1, source_target_pairs={{0,7},{1,6},{2,5},{3,4},{4,3},{5,2},{6,1},{7,0},{8,15},{9,14},{10,... | collective-permute-start | bytes 589832 | tf_op jit(solution)/shard_map/ppermute | solution.py:513
  61.6 1.5 %collective-permute-start.3 = (bf16[4,3,4,16,128]{4,3,2,1,0:T(8,128)(2,1)}, bf16[4,3,4,16,128]{4,3,2,1,0:T(8,128)(2,1)S(1)}, u32[]{:S(2)}, u32[]{:S(2)}) collective-permute-start(bf16[4,3,4,16,128]{4,3,2,1,0:T(8,128)(2,1)} %get-tuple-element.59), channel_id=1, source_target_pairs={{0,1},{1,0},{2,3},{3,2},{4,5},{5,4},{6,7},{7,6},{8,9},{9,8},{10,11... | collective-permute-start | bytes 589832 | tf_op jit(solution)/shard_map/ppermute | solution.py:513
  63.1 7.0 %collective-permute-done.14.refs_5_ = bf16[4,3,4,16,128]{4,3,2,1,0:T(8,128)(2,1)S(1)} collective-permute-done((bf16[4,3,4,16,128]{4,3,2,1,0:T(8,128)(2,1)S(1)}, bf16[4,3,4,16,128]{4,3,2,1,0:T(8,128)(2,1)S(1)}, u32[]{:S(2)}, u32[]{:S(2)}) %collective-permute-start.14) | collective-permute-done | bytes 196640 | tf_op jit(solution)/shard_map/ppermute | solution.py:513
  70.2 1.4 %collective-permute-start.5 = (bf16[4,3,4,16,128]{4,3,2,1,0:T(8,128)(2,1)}, bf16[4,3,4,16,128]{4,3,2,1,0:T(8,128)(2,1)S(1)}, u32[]{:S(2)}, u32[]{:S(2)}) collective-permute-start(bf16[4,3,4,16,128]{4,3,2,1,0:T(8,128)(2,1)} %get-tuple-element.61), channel_id=1, source_target_pairs={{0,3},{1,2},{2,1},{3,0},{4,7},{5,6},{6,5},{7,4},{8,11},{9,10},{10,... | collective-permute-start | bytes 589832 | tf_op jit(solution)/shard_map/ppermute | solution.py:513
  71.5 5.8 %inner_columns.1.refs_8_ = bf16[4,512,384]{2,1,0:T(8,128)(2,1)S(1)} custom-call(s32[4,6]{1,0:T(4,128)S(1)} %copy-done.8, s32[1,8]{1,0:T(1,128)S(1)} %copy-done.7, bf16[4,3,4,16,128]{4,3,2,1,0:T(8,128)(2,1)S(1)} %get-tuple-element.83.refs_0_, bf16[4,3,4,16,128]{4,3,2,1,0:T(8,128)(2,1)S(1)} %collective-permute-done.6.refs_1_, ...), custom_call_target="tpu_custom_call" | custom-call | flops 1 | bytes 1 | tf_op jit(solution)/shard_map/inner_columns/pallas_call | solution.py:599
  77.8 7.5 %edge_columns.1 = bf16[512,8,384]{2,1,0:T(8,128)(2,1)} custom-call(s32[4,6]{1,0:T(4,128)S(1)} %copy-done.8, s32[1,8]{1,0:T(1,128)S(1)} %copy-done.7, bf16[4,3,4,16,128]{4,3,2,1,0:T(8,128)(2,1)S(1)} %copy-done.4, bf16[4,3,4,16,128]{4,3,2,1,0:T(8,128)(2,1)S(1)} %collective-permute-done.3.refs_1_, ...), custom_call_target="tpu_custom_call" | custom-call | flops 1 | bytes 1 | tf_op jit(solution)/shard_map/edge_columns/pallas_call | solution.py:610
  (35 shorter events, 2.1 us)
Async XLA Ops:
  0.0 15.4 %copy-start.6 = (s32[1,8]{1,0:T(1,128)S(1)}, s32[1,8]{1,0:T(1,128)}, u32[]{:S(2)}) copy-start(s32[1,8]{1,0:T(1,128)} %counts_ref.11) | copy-start | bytes 100
  7.3 12.0 %collective-permute-start = (bf16[6,2,16,1152]{3,2,1,0:T(8,128)(2,1)}, bf16[6,2,16,1152]{3,2,1,0:T(8,128)(2,1)S(1)}, u32[]{:S(2)}, u32[]{:S(2)}) collective-permute-start(bf16[6,2,16,1152]{3,2,1,0:T(8,128)(2,1)} %get-tuple-element.48), channel_id=1, source_target_pairs={{0,8},{8,16},{16,24},{1,9},{9,17},{17,25},{2,10},{10,18},{18,26},{... | collective-permute-start | bytes 1327112 | tf_op jit(solution)/shard_map/ppermute | solution.py:531
  9.6 31.2 %collective-permute-start.2 = (bf16[4,9,4,16,128]{4,3,2,1,0:T(8,128)(2,1)}, bf16[4,9,4,16,128]{4,3,2,1,0:T(8,128)(2,1)S(1)}, u32[]{:S(2)}, u32[]{:S(2)}) collective-permute-start(bf16[4,9,4,16,128]{4,3,2,1,0:T(8,128)(2,1)} %get-tuple-element.54.raw_ref), channel_id=1, source_target_pairs={{0,6},{1,7},{2,4},{3,5},{4,2},{5,3},{6,0},{7,1},{8,14},{9,15},{10,... | collective-permute-start | bytes 1769480 | tf_op jit(solution)/shard_map/ppermute | solution.py:513
  14.1 7.2 %collective-permute-start.1 = (bf16[6,2,16,1152]{3,2,1,0:T(8,128)(2,1)}, bf16[6,2,16,1152]{3,2,1,0:T(8,128)(2,1)}, u32[]{:S(2)}, u32[]{:S(2)}) collective-permute-start(bf16[6,2,16,1152]{3,2,1,0:T(8,128)(2,1)} %get-tuple-element.49), channel_id=1, source_target_pairs={{8,0},{16,8},{24,16},{9,1},{17,9},{25,17},{10,2},{18,10},{26,18},{... | collective-permute-start | bytes 1327112 | tf_op jit(solution)/shard_map/ppermute | solution.py:532
  17.7 12.7 %copy-start.1 = (bf16[512,512]{1,0:T(8,128)(2,1)S(1)}, bf16[512,512]{1,0:T(8,128)(2,1)}, u32[]{:S(2)}) copy-start(bf16[512,512]{1,0:T(8,128)(2,1)} %refs_0_) | copy-start | bytes 1572868
  17.7 12.7 %copy-start.2 = (bf16[512,512]{1,0:T(8,128)(2,1)S(1)}, bf16[512,512]{1,0:T(8,128)(2,1)}, u32[]{:S(2)}) copy-start(bf16[512,512]{1,0:T(8,128)(2,1)} %refs_1_) | copy-start | bytes 1572868
  17.7 12.7 %copy-start.3 = (bf16[512,512]{1,0:T(8,128)(2,1)S(1)}, bf16[512,512]{1,0:T(8,128)(2,1)}, u32[]{:S(2)}) copy-start(bf16[512,512]{1,0:T(8,128)(2,1)} %refs_2_) | copy-start | bytes 1572868
  17.7 13.1 %collective-permute-start.6 = (bf16[4,3,4,16,128]{4,3,2,1,0:T(8,128)(2,1)S(1)}, bf16[4,3,4,16,128]{4,3,2,1,0:T(8,128)(2,1)S(1)}, u32[]{:S(2)}, u32[]{:S(2)}) collective-permute-start(bf16[4,3,4,16,128]{4,3,2,1,0:T(8,128)(2,1)S(1)} %get-tuple-element.62), channel_id=1, source_target_pairs={{0,1},{1,0},{2,3},{3,2},{4,5},{5,4},{6,7},{7,6},{8,9},{9,8},{10,11... | collective-permute-start | bytes 589832 | tf_op jit(solution)/shard_map/ppermute | solution.py:513
  19.3 13.5 %collective-permute-start.7 = (bf16[4,3,4,16,128]{4,3,2,1,0:T(8,128)(2,1)S(1)}, bf16[4,3,4,16,128]{4,3,2,1,0:T(8,128)(2,1)S(1)}, u32[]{:S(2)}, u32[]{:S(2)}) collective-permute-start(bf16[4,3,4,16,128]{4,3,2,1,0:T(8,128)(2,1)S(1)} %get-tuple-element.63), channel_id=1, source_target_pairs={{0,2},{1,3},{2,0},{3,1},{4,6},{5,7},{6,4},{7,5},{8,10},{9,11},{10,... | collective-permute-start | bytes 589832 | tf_op jit(solution)/shard_map/ppermute | solution.py:513
  19.3 21.5 %copy-start.7 = (s32[1,8]{1,0:T(1,128)S(1)}, s32[1,8]{1,0:T(1,128)}, u32[]{:S(2)}) copy-start(s32[1,8]{1,0:T(1,128)} %counts_ref.11) | copy-start | bytes 100
  19.3 52.2 %copy-start.5 = (bf16[128,128]{1,0:T(8,128)(2,1)S(1)}, bf16[128,128]{1,0:T(8,128)(2,1)}, u32[]{:S(2)}) copy-start(bf16[128,128]{1,0:T(8,128)(2,1)} %refs_9_.1) | copy-start | bytes 98308
  19.3 52.2 %copy-start.8 = (s32[4,6]{1,0:T(4,128)S(1)}, s32[4,6]{1,0:T(4,128)}, u32[]{:S(2)}) copy-start(s32[4,6]{1,0:T(4,128)} %groups_ref.3) | copy-start | bytes 292
  19.3 18.8 %collective-permute-start.8 = (bf16[4,3,4,16,128]{4,3,2,1,0:T(8,128)(2,1)S(1)}, bf16[4,3,4,16,128]{4,3,2,1,0:T(8,128)(2,1)S(1)}, u32[]{:S(2)}, u32[]{:S(2)}) collective-permute-start(bf16[4,3,4,16,128]{4,3,2,1,0:T(8,128)(2,1)S(1)} %get-tuple-element.64), channel_id=1, source_target_pairs={{0,3},{1,2},{2,1},{3,0},{4,7},{5,6},{6,5},{7,4},{8,11},{9,10},{10,... | collective-permute-start | bytes 589832 | tf_op jit(solution)/shard_map/ppermute | solution.py:513
  38.1 17.4 %collective-permute-start.9 = (bf16[4,3,4,16,128]{4,3,2,1,0:T(8,128)(2,1)}, bf16[4,3,4,16,128]{4,3,2,1,0:T(8,128)(2,1)S(1)}, u32[]{:S(2)}, u32[]{:S(2)}) collective-permute-start(bf16[4,3,4,16,128]{4,3,2,1,0:T(8,128)(2,1)} %get-tuple-element.79), channel_id=1, source_target_pairs={{0,4},{1,5},{2,6},{3,7},{4,0},{5,1},{6,2},{7,3},{8,12},{9,13},{10,... | collective-permute-start | bytes 589832 | tf_op jit(solution)/shard_map/ppermute | solution.py:513
  38.9 20.6 %collective-permute-start.10 = (bf16[4,3,4,16,128]{4,3,2,1,0:T(8,128)(2,1)}, bf16[4,3,4,16,128]{4,3,2,1,0:T(8,128)(2,1)S(1)}, u32[]{:S(2)}, u32[]{:S(2)}) collective-permute-start(bf16[4,3,4,16,128]{4,3,2,1,0:T(8,128)(2,1)} %get-tuple-element.80), channel_id=1, source_target_pairs={{0,5},{1,4},{2,7},{3,6},{4,1},{5,0},{6,3},{7,2},{8,13},{9,12},{10,... | collective-permute-start | bytes 589832 | tf_op jit(solution)/shard_map/ppermute | solution.py:513
  42.0 19.6 %collective-permute-start.13 = (bf16[4,3,4,16,128]{4,3,2,1,0:T(8,128)(2,1)S(1)}, bf16[4,3,4,16,128]{4,3,2,1,0:T(8,128)(2,1)S(1)}, u32[]{:S(2)}, u32[]{:S(2)}) collective-permute-start(bf16[4,3,4,16,128]{4,3,2,1,0:T(8,128)(2,1)S(1)} %get-tuple-element.87), channel_id=1, source_target_pairs={{0,2},{1,3},{2,0},{3,1},{4,6},{5,7},{6,4},{7,5},{8,10},{9,11},{10,... | collective-permute-start | bytes 589832 | tf_op jit(solution)/shard_map/ppermute | solution.py:513
  43.5 26.6 %collective-permute-start.14 = (bf16[4,3,4,16,128]{4,3,2,1,0:T(8,128)(2,1)S(1)}, bf16[4,3,4,16,128]{4,3,2,1,0:T(8,128)(2,1)S(1)}, u32[]{:S(2)}, u32[]{:S(2)}) collective-permute-start(bf16[4,3,4,16,128]{4,3,2,1,0:T(8,128)(2,1)S(1)} %get-tuple-element.88), channel_id=1, source_target_pairs={{0,3},{1,2},{2,1},{3,0},{4,7},{5,6},{6,5},{7,4},{8,11},{9,10},{10,... | collective-permute-start | bytes 589832 | tf_op jit(solution)/shard_map/ppermute | solution.py:513
  45.2 24.9 %collective-permute-start.15 = (bf16[4,3,4,16,128]{4,3,2,1,0:T(8,128)(2,1)S(1)}, bf16[4,3,4,16,128]{4,3,2,1,0:T(8,128)(2,1)S(1)}, u32[]{:S(2)}, u32[]{:S(2)}) collective-permute-start(bf16[4,3,4,16,128]{4,3,2,1,0:T(8,128)(2,1)S(1)} %get-tuple-element.90), channel_id=1, source_target_pairs={{0,1},{1,0},{2,3},{3,2},{4,5},{5,4},{6,7},{7,6},{8,9},{9,8},{10,11... | collective-permute-start | bytes 589832 | tf_op jit(solution)/shard_map/ppermute | solution.py:513
  55.5 21.8 %collective-permute-start.11 = (bf16[4,3,4,16,128]{4,3,2,1,0:T(8,128)(2,1)}, bf16[4,3,4,16,128]{4,3,2,1,0:T(8,128)(2,1)S(1)}, u32[]{:S(2)}, u32[]{:S(2)}) collective-permute-start(bf16[4,3,4,16,128]{4,3,2,1,0:T(8,128)(2,1)} %get-tuple-element.81), channel_id=1, source_target_pairs={{0,6},{1,7},{2,4},{3,5},{4,2},{5,3},{6,0},{7,1},{8,14},{9,15},{10,... | collective-permute-start | bytes 589832 | tf_op jit(solution)/shard_map/ppermute | solution.py:513
  59.4 17.9 %collective-permute-start.12 = (bf16[4,3,4,16,128]{4,3,2,1,0:T(8,128)(2,1)}, bf16[4,3,4,16,128]{4,3,2,1,0:T(8,128)(2,1)S(1)}, u32[]{:S(2)}, u32[]{:S(2)}) collective-permute-start(bf16[4,3,4,16,128]{4,3,2,1,0:T(8,128)(2,1)} %get-tuple-element.82), channel_id=1, source_target_pairs={{0,7},{1,6},{2,5},{3,4},{4,3},{5,2},{6,1},{7,0},{8,15},{9,14},{10,... | collective-permute-start | bytes 589832 | tf_op jit(solution)/shard_map/ppermute | solution.py:513
  61.6 15.7 %collective-permute-start.3 = (bf16[4,3,4,16,128]{4,3,2,1,0:T(8,128)(2,1)}, bf16[4,3,4,16,128]{4,3,2,1,0:T(8,128)(2,1)S(1)}, u32[]{:S(2)}, u32[]{:S(2)}) collective-permute-start(bf16[4,3,4,16,128]{4,3,2,1,0:T(8,128)(2,1)} %get-tuple-element.59), channel_id=1, source_target_pairs={{0,1},{1,0},{2,3},{3,2},{4,5},{5,4},{6,7},{7,6},{8,9},{9,8},{10,11... | collective-permute-start | bytes 589832 | tf_op jit(solution)/shard_map/ppermute | solution.py:513
  70.2 7.2 %collective-permute-start.4 = (bf16[4,3,4,16,128]{4,3,2,1,0:T(8,128)(2,1)}, bf16[4,3,4,16,128]{4,3,2,1,0:T(8,128)(2,1)S(1)}, u32[]{:S(2)}, u32[]{:S(2)}) collective-permute-start(bf16[4,3,4,16,128]{4,3,2,1,0:T(8,128)(2,1)} %get-tuple-element.60), channel_id=1, source_target_pairs={{0,2},{1,3},{2,0},{3,1},{4,6},{5,7},{6,4},{7,5},{8,10},{9,11},{10,... | collective-permute-start | bytes 589832 | tf_op jit(solution)/shard_map/ppermute | solution.py:513
  70.2 7.7 %collective-permute-start.5 = (bf16[4,3,4,16,128]{4,3,2,1,0:T(8,128)(2,1)}, bf16[4,3,4,16,128]{4,3,2,1,0:T(8,128)(2,1)S(1)}, u32[]{:S(2)}, u32[]{:S(2)}) collective-permute-start(bf16[4,3,4,16,128]{4,3,2,1,0:T(8,128)(2,1)} %get-tuple-element.61), channel_id=1, source_target_pairs={{0,3},{1,2},{2,1},{3,0},{4,7},{5,6},{6,5},{7,4},{8,11},{9,10},{10,... | collective-permute-start | bytes 589832 | tf_op jit(solution)/shard_map/ppermute | solution.py:513
  71.5 6.3 %copy-start.4 = (bf16[4,3,4,16,128]{4,3,2,1,0:T(8,128)(2,1)S(1)}, bf16[4,3,4,16,128]{4,3,2,1,0:T(8,128)(2,1)}, u32[]{:S(2)}) copy-start(bf16[4,3,4,16,128]{4,3,2,1,0:T(8,128)(2,1)} %get-tuple-element.50.refs_0_) | copy-start | bytes 589828
  (2 other events, 3.2 us)

commit v7 on v6

--- a/solution.py
+++ b/solution.py
@@ -560,7 +560,7 @@
         edge = list(edge)
         edge[near:], _ = lax.optimization_barrier((edge[near:], turned))
         mirrored = pack_half(crossed)
-        edge[1:near], mirrored = lax.optimization_barrier((edge[1:near], mirrored))
+        edge[2:near], mirrored = lax.optimization_barrier((edge[2:near], mirrored))
         near_parts = inner_parts[1:]
         near_parts, edge[near :] = lax.optimization_barrier((near_parts, edge[near :]))
         inner_parts = inner_parts[:1] + near_parts

time: 86.7 us -> 85.6 us (0.987)
  waiting for transfers between devices: 27.6 us -> 23.1 us
  starting transfers between devices: 24.2 us -> 27.7 us
    ppermute x14, waiting for transfers between devices: 27.6 us -> 23.1 us  [turned_exchange(): lax.ppermute(x, 'lev', [(i, i ^ turn) for i in range(owner_count)])]
    ppermute x14, starting transfers between devices: 20.5 us -> 24.1 us  [turned_exchange(): lax.ppermute(x, 'lev', [(i, i ^ turn) for i in range(owner_count)])]
  transfers between devices with their start and end apart: 16 -> 16, of which waited for: 6 -> 7; matrix products, arithmetic and copies ran while one was open for 0% -> 0% of each run, Pallas kernels for 21% -> 21%
where the time goes in v7:
time: 85.6 us; the launch traced here: 84.4 us
  Pallas kernels  32.2 us (38%)
  starting transfers between devices  27.7 us (32%)
  waiting for transfers between devices  23.1 us (27%)
  local copies, waits for them, and re-layouts  1.11 us (1%)
    ppermute x14, starting transfers between devices, turned_exchange(): lax.ppermute(x, 'lev', [(i, i ^ turn) for i in range(owner_count)])  24.1 us
    ppermute x14, waiting for transfers between devices, turned_exchange(): lax.ppermute(x, 'lev', [(i, i ^ turn) for i in range(owner_count)])  23.1 us
    pallas_call x1, Pallas kernels, shards(): pl.pallas_call(functools.partial(edge_kernel, lat_rows, by_turn), in_spec...  8.97 us
    pallas_call x1, Pallas kernels, shards(): pl.pallas_call(functools.partial(last_kernel, edge_rows, inner_rows, by_t...  7.46 us
    pallas_call x1, Pallas kernels, shards(): pl.pallas_call(functools.partial(inner_kernel, lat_rows, by_turn), in_spe...  7.24 us
    pallas_call x1, Pallas kernels, shards(): pl.pallas_call(functools.partial(half_kernel, lat_rows, inner_rows, by_tu...  5.76 us
    ppermute x1, starting transfers between devices, shards(): before = lax.ppermute(last, 'lat', up)  2.38 us
    pallas_call x2, Pallas kernels, pack_half(): pl.pallas_call(mirror_kernel, in_specs=[smem, pl.BlockSpec(memory_space=p...  2.37 us
  transfers between devices with their start and end apart: 16, of which 7 were waited for; matrix products, arithmetic and copies ran while one was open for 0% of the time, Pallas kernels for 21%

profile of v7, /device:TPU:0, one launch (start us, length us, event | category | flops | bytes accessed | tf_op | source)
XLA Modules:
  0.0 84.4 jit_solution(11974259390480279359)
XLA Ops:
  0.0 7.2 %inner_rows.1 = (bf16[4,9,4,16,128]{4,3,2,1,0:T(8,128)(2,1)}, bf16[6,2,16,1152]{3,2,1,0:T(8,128)(2,1)}, bf16[6,2,16,1152]{3,2,1,0:T(8,128)(2,1)}) custom-call(s32[1,8]{1,0:T(1,128)} %counts_ref.11, f32[4,128,1152]{2,1,0:T(8,128)} %bitcast.3, f32[2,128,1152]{2,1,0:T(8,128)} %bitcast.5), custom_call_target="tpu_custom_call" | custom-call | flops 1 | bytes 1 | tf_op jit(solution)/shard_map/inner_rows/pallas_call | solution.py:488
  7.3 2.4 %collective-permute-start = (bf16[6,2,16,1152]{3,2,1,0:T(8,128)(2,1)}, bf16[6,2,16,1152]{3,2,1,0:T(8,128)(2,1)S(1)}, u32[]{:S(2)}, u32[]{:S(2)}) collective-permute-start(bf16[6,2,16,1152]{3,2,1,0:T(8,128)(2,1)} %get-tuple-element.47), channel_id=1, source_target_pairs={{0,8},{8,16},{16,24},{1,9},{9,17},{17,25},{2,10},{10,18},{18,26},{... | collective-permute-start | bytes 1327112 | tf_op jit(solution)/shard_map/ppermute | solution.py:531
  9.6 4.5 %collective-permute-start.3 = (bf16[4,9,4,16,128]{4,3,2,1,0:T(8,128)(2,1)}, bf16[4,9,4,16,128]{4,3,2,1,0:T(8,128)(2,1)S(1)}, u32[]{:S(2)}, u32[]{:S(2)}) collective-permute-start(bf16[4,9,4,16,128]{4,3,2,1,0:T(8,128)(2,1)} %get-tuple-element.53.raw_ref), channel_id=1, source_target_pairs={{0,6},{1,7},{2,4},{3,5},{4,2},{5,3},{6,0},{7,1},{8,14},{9,15},{10,... | collective-permute-start | bytes 1769480 | tf_op jit(solution)/shard_map/ppermute | solution.py:513
  14.1 1.3 %collective-permute-start.1 = (bf16[6,2,16,1152]{3,2,1,0:T(8,128)(2,1)}, bf16[6,2,16,1152]{3,2,1,0:T(8,128)(2,1)}, u32[]{:S(2)}, u32[]{:S(2)}) collective-permute-start(bf16[6,2,16,1152]{3,2,1,0:T(8,128)(2,1)} %get-tuple-element.48), channel_id=1, source_target_pairs={{8,0},{16,8},{24,16},{9,1},{17,9},{25,17},{10,2},{18,10},{26,18},{... | collective-permute-start | bytes 1327112 | tf_op jit(solution)/shard_map/ppermute | solution.py:532
  15.4 1.1 %copy-done = bf16[4,9,4,16,128]{4,3,2,1,0:T(8,128)(2,1)S(1)} copy-done((bf16[4,9,4,16,128]{4,3,2,1,0:T(8,128)(2,1)S(1)}, bf16[4,9,4,16,128]{4,3,2,1,0:T(8,128)(2,1)}, u32[]{:S(2)}) %copy-start) | copy-done | bytes 589848
  16.5 1.2 %half_slots.3 = (bf16[4,3,4,16,128]{4,3,2,1,0:T(8,128)(2,1)S(1)}, bf16[4,3,4,16,128]{4,3,2,1,0:T(8,128)(2,1)S(1)}, bf16[4,3,4,16,128]{4,3,2,1,0:T(8,128)(2,1)S(1)}, bf16[4,3,4,16,128]{4,3,2,1,0:T(8,128)(2,1)S(1)}) custom-call(s32[1,8]{1,0:T(1,128)S(1)} %copy-done.6, bf16[4,9,4,16,128]{4,3,2,1,0:T(8,128)(2,1)S(1)} %copy-done), custom_call_target="tpu_custom_call" | custom-call | flops 1 | bytes 1 | tf_op jit(solution)/shard_map/half_slots/pallas_call | solution.py:516
  17.7 1.6 %collective-permute-start.6 = (bf16[4,3,4,16,128]{4,3,2,1,0:T(8,128)(2,1)S(1)}, bf16[4,3,4,16,128]{4,3,2,1,0:T(8,128)(2,1)S(1)}, u32[]{:S(2)}, u32[]{:S(2)}) collective-permute-start(bf16[4,3,4,16,128]{4,3,2,1,0:T(8,128)(2,1)S(1)} %get-tuple-element.60), channel_id=1, source_target_pairs={{0,1},{1,0},{2,3},{3,2},{4,5},{5,4},{6,7},{7,6},{8,9},{9,8},{10,11... | collective-permute-start | bytes 589832 | tf_op jit(solution)/shard_map/ppermute | solution.py:513
  19.3 2.0 %collective-permute-start.8 = (bf16[4,3,4,16,128]{4,3,2,1,0:T(8,128)(2,1)S(1)}, bf16[4,3,4,16,128]{4,3,2,1,0:T(8,128)(2,1)S(1)}, u32[]{:S(2)}, u32[]{:S(2)}) collective-permute-start(bf16[4,3,4,16,128]{4,3,2,1,0:T(8,128)(2,1)S(1)} %get-tuple-element.62), channel_id=1, source_target_pairs={{0,3},{1,2},{2,1},{3,0},{4,7},{5,6},{6,5},{7,4},{8,11},{9,10},{10,... | collective-permute-start | bytes 589832 | tf_op jit(solution)/shard_map/ppermute | solution.py:513
  21.4 9.0 %edge_rows.1 = (bf16[4,3,4,16,128]{4,3,2,1,0:T(8,128)(2,1)}, bf16[4,3,4,16,128]{4,3,2,1,0:T(8,128)(2,1)}, bf16[4,3,4,16,128]{4,3,2,1,0:T(8,128)(2,1)}, bf16[4,3,...) custom-call(s32[1,8]{1,0:T(1,128)} %counts_ref.11, ...), custom_call_target="tpu_custom_call" | custom-call | flops 1 | bytes 1 | tf_op jit(solution)/shard_map/edge_rows/pallas_call | solution.py:535
  30.4 1.6 %collective-permute-start.2 = (bf16[4,3,4,16,128]{4,3,2,1,0:T(8,128)(2,1)}, bf16[4,3,4,16,128]{4,3,2,1,0:T(8,128)(2,1)S(1)}, u32[]{:S(2)}, u32[]{:S(2)}) collective-permute-start(bf16[4,3,4,16,128]{4,3,2,1,0:T(8,128)(2,1)} %get-tuple-element.50), channel_id=1, source_target_pairs={{0,1},{1,0},{2,3},{3,2},{4,5},{5,4},{6,7},{7,6},{8,9},{9,8},{10,11... | collective-permute-start | bytes 589832 | tf_op jit(solution)/shard_map/ppermute | solution.py:513
  32.8 5.5 %collective-permute-done.8.refs_3_ = bf16[4,3,4,16,128]{4,3,2,1,0:T(8,128)(2,1)S(1)} collective-permute-done((bf16[4,3,4,16,128]{4,3,2,1,0:T(8,128)(2,1)S(1)}, bf16[4,3,4,16,128]{4,3,2,1,0:T(8,128)(2,1)S(1)}, u32[]{:S(2)}, u32[]{:S(2)}) %collective-permute-start.8) | collective-permute-done | bytes 196640 | tf_op jit(solution)/shard_map/ppermute | solution.py:513
  38.9 1.2 %half_slots.2 = (bf16[4,3,4,16,128]{4,3,2,1,0:T(8,128)(2,1)S(1)}, bf16[4,3,4,16,128]{4,3,2,1,0:T(8,128)(2,1)S(1)}, bf16[4,3,4,16,128]{4,3,2,1,0:T(8,128)(2,1)S(1)}, bf16[4,3,4,16,128]{4,3,2,1,0:T(8,128)(2,1)S(1)}) custom-call(s32[1,8]{1,0:T(1,128)S(1)} %copy-done.7, bf16[4,9,4,16,128]{4,3,2,1,0:T(8,128)(2,1)S(1)} %collective-permute-done.3.raw_ref), custom_call_target="tpu_custom_call" | custom-call | flops 1 | bytes 1 | tf_op jit(solution)/shard_map/half_slots/pallas_call | solution.py:516
  40.1 3.5 %collective-permute-start.13 = (bf16[4,3,4,16,128]{4,3,2,1,0:T(8,128)(2,1)S(1)}, bf16[4,3,4,16,128]{4,3,2,1,0:T(8,128)(2,1)S(1)}, u32[]{:S(2)}, u32[]{:S(2)}) collective-permute-start(bf16[4,3,4,16,128]{4,3,2,1,0:T(8,128)(2,1)S(1)} %get-tuple-element.85), channel_id=1, source_target_pairs={{0,2},{1,3},{2,0},{3,1},{4,6},{5,7},{6,4},{7,5},{8,10},{9,11},{10,... | collective-permute-start | bytes 589832 | tf_op jit(solution)/shard_map/ppermute | solution.py:513
  43.7 1.5 %collective-permute-start.15 = (bf16[4,3,4,16,128]{4,3,2,1,0:T(8,128)(2,1)S(1)}, bf16[4,3,4,16,128]{4,3,2,1,0:T(8,128)(2,1)S(1)}, u32[]{:S(2)}, u32[]{:S(2)}) collective-permute-start(bf16[4,3,4,16,128]{4,3,2,1,0:T(8,128)(2,1)S(1)} %get-tuple-element.88), channel_id=1, source_target_pairs={{0,1},{1,0},{2,3},{3,2},{4,5},{5,4},{6,7},{7,6},{8,9},{9,8},{10,11... | collective-permute-start | bytes 589832 | tf_op jit(solution)/shard_map/ppermute | solution.py:513
  45.2 1.9 %collective-permute-start.10 = (bf16[4,3,4,16,128]{4,3,2,1,0:T(8,128)(2,1)}, bf16[4,3,4,16,128]{4,3,2,1,0:T(8,128)(2,1)S(1)}, u32[]{:S(2)}, u32[]{:S(2)}) collective-permute-start(bf16[4,3,4,16,128]{4,3,2,1,0:T(8,128)(2,1)} %get-tuple-element.78), channel_id=1, source_target_pairs={{0,5},{1,4},{2,7},{3,6},{4,1},{5,0},{6,3},{7,2},{8,13},{9,12},{10,... | collective-permute-start | bytes 589832 | tf_op jit(solution)/shard_map/ppermute | solution.py:513
  47.1 4.3 %collective-permute-done.9.refs_4_ = bf16[4,3,4,16,128]{4,3,2,1,0:T(8,128)(2,1)S(1)} collective-permute-done((bf16[4,3,4,16,128]{4,3,2,1,0:T(8,128)(2,1)}, bf16[4,3,4,16,128]{4,3,2,1,0:T(8,128)(2,1)S(1)}, u32[]{:S(2)}, u32[]{:S(2)}) %collective-permute-start.9) | collective-permute-done | bytes 196640 | tf_op jit(solution)/shard_map/ppermute | solution.py:513
  51.4 1.0 %collective-permute-start.11 = (bf16[4,3,4,16,128]{4,3,2,1,0:T(8,128)(2,1)}, bf16[4,3,4,16,128]{4,3,2,1,0:T(8,128)(2,1)S(1)}, u32[]{:S(2)}, u32[]{:S(2)}) collective-permute-start(bf16[4,3,4,16,128]{4,3,2,1,0:T(8,128)(2,1)} %get-tuple-element.79), channel_id=1, source_target_pairs={{0,6},{1,7},{2,4},{3,5},{4,2},{5,3},{6,0},{7,1},{8,14},{9,15},{10,... | collective-permute-start | bytes 589832 | tf_op jit(solution)/shard_map/ppermute | solution.py:513
  52.4 4.2 %collective-permute-done.13.refs_4_ = bf16[4,3,4,16,128]{4,3,2,1,0:T(8,128)(2,1)S(1)} collective-permute-done((bf16[4,3,4,16,128]{4,3,2,1,0:T(8,128)(2,1)S(1)}, bf16[4,3,4,16,128]{4,3,2,1,0:T(8,128)(2,1)S(1)}, u32[]{:S(2)}, u32[]{:S(2)}) %collective-permute-start.13) | collective-permute-done | bytes 196640 | tf_op jit(solution)/shard_map/ppermute | solution.py:513
  56.6 2.5 %collective-permute-start.12 = (bf16[4,3,4,16,128]{4,3,2,1,0:T(8,128)(2,1)}, bf16[4,3,4,16,128]{4,3,2,1,0:T(8,128)(2,1)S(1)}, u32[]{:S(2)}, u32[]{:S(2)}) collective-permute-start(bf16[4,3,4,16,128]{4,3,2,1,0:T(8,128)(2,1)} %get-tuple-element.80), channel_id=1, source_target_pairs={{0,7},{1,6},{2,5},{3,4},{4,3},{5,2},{6,1},{7,0},{8,15},{9,14},{10,... | collective-permute-start | bytes 589832 | tf_op jit(solution)/shard_map/ppermute | solution.py:513
  59.9 3.2 %collective-permute-start.5 = (bf16[4,3,4,16,128]{4,3,2,1,0:T(8,128)(2,1)}, bf16[4,3,4,16,128]{4,3,2,1,0:T(8,128)(2,1)S(1)}, u32[]{:S(2)}, u32[]{:S(2)}) collective-permute-start(bf16[4,3,4,16,128]{4,3,2,1,0:T(8,128)(2,1)} %get-tuple-element.59), channel_id=1, source_target_pairs={{0,3},{1,2},{2,1},{3,0},{4,7},{5,6},{6,5},{7,4},{8,11},{9,10},{10,... | collective-permute-start | bytes 589832 | tf_op jit(solution)/shard_map/ppermute | solution.py:513
  63.1 5.8 %inner_columns.1.refs_8_ = bf16[4,512,384]{2,1,0:T(8,128)(2,1)S(1)} custom-call(s32[4,6]{1,0:T(4,128)S(1)} %copy-done.8, s32[1,8]{1,0:T(1,128)S(1)} %copy-done.7, bf16[4,3,4,16,128]{4,3,2,1,0:T(8,128)(2,1)S(1)} %get-tuple-element.81.refs_0_, bf16[4,3,4,16,128]{4,3,2,1,0:T(8,128)(2,1)S(1)} %collective-permute-done.6.refs_1_, ...), custom_call_target="tpu_custom_call" | custom-call | flops 1 | bytes 1 | tf_op jit(solution)/shard_map/inner_columns/pallas_call | solution.py:599
  68.9 3.9 %collective-permute-done.4.refs_2_ = bf16[4,3,4,16,128]{4,3,2,1,0:T(8,128)(2,1)S(1)} collective-permute-done((bf16[4,3,4,16,128]{4,3,2,1,0:T(8,128)(2,1)}, bf16[4,3,4,16,128]{4,3,2,1,0:T(8,128)(2,1)S(1)}, u32[]{:S(2)}, u32[]{:S(2)}) %collective-permute-start.4) | collective-permute-done | bytes 196640 | tf_op jit(solution)/shard_map/ppermute | solution.py:513
  72.9 4.1 %collective-permute-done.5.refs_3_ = bf16[4,3,4,16,128]{4,3,2,1,0:T(8,128)(2,1)S(1)} collective-permute-done((bf16[4,3,4,16,128]{4,3,2,1,0:T(8,128)(2,1)}, bf16[4,3,4,16,128]{4,3,2,1,0:T(8,128)(2,1)S(1)}, u32[]{:S(2)}, u32[]{:S(2)}) %collective-permute-start.5) | collective-permute-done | bytes 196640 | tf_op jit(solution)/shard_map/ppermute | solution.py:513
  76.9 7.5 %edge_columns.1 = bf16[512,8,384]{2,1,0:T(8,128)(2,1)} custom-call(s32[4,6]{1,0:T(4,128)S(1)} %copy-done.8, s32[1,8]{1,0:T(1,128)S(1)} %copy-done.7, bf16[4,3,4,16,128]{4,3,2,1,0:T(8,128)(2,1)S(1)} %copy-done.4, bf16[4,3,4,16,128]{4,3,2,1,0:T(8,128)(2,1)S(1)} %collective-permute-done.2.refs_1_, ...), custom_call_target="tpu_custom_call" | custom-call | flops 1 | bytes 1 | tf_op jit(solution)/shard_map/edge_columns/pallas_call | solution.py:610
  (35 shorter events, 2.4 us)
Async XLA Ops:
  0.0 15.4 %copy-start.6 = (s32[1,8]{1,0:T(1,128)S(1)}, s32[1,8]{1,0:T(1,128)}, u32[]{:S(2)}) copy-start(s32[1,8]{1,0:T(1,128)} %counts_ref.11) | copy-start | bytes 100
  7.3 12.0 %collective-permute-start = (bf16[6,2,16,1152]{3,2,1,0:T(8,128)(2,1)}, bf16[6,2,16,1152]{3,2,1,0:T(8,128)(2,1)S(1)}, u32[]{:S(2)}, u32[]{:S(2)}) collective-permute-start(bf16[6,2,16,1152]{3,2,1,0:T(8,128)(2,1)} %get-tuple-element.47), channel_id=1, source_target_pairs={{0,8},{8,16},{16,24},{1,9},{9,17},{17,25},{2,10},{10,18},{18,26},{... | collective-permute-start | bytes 1327112 | tf_op jit(solution)/shard_map/ppermute | solution.py:531
  9.6 29.3 %collective-permute-start.3 = (bf16[4,9,4,16,128]{4,3,2,1,0:T(8,128)(2,1)}, bf16[4,9,4,16,128]{4,3,2,1,0:T(8,128)(2,1)S(1)}, u32[]{:S(2)}, u32[]{:S(2)}) collective-permute-start(bf16[4,9,4,16,128]{4,3,2,1,0:T(8,128)(2,1)} %get-tuple-element.53.raw_ref), channel_id=1, source_target_pairs={{0,6},{1,7},{2,4},{3,5},{4,2},{5,3},{6,0},{7,1},{8,14},{9,15},{10,... | collective-permute-start | bytes 1769480 | tf_op jit(solution)/shard_map/ppermute | solution.py:513
  14.1 7.2 %collective-permute-start.1 = (bf16[6,2,16,1152]{3,2,1,0:T(8,128)(2,1)}, bf16[6,2,16,1152]{3,2,1,0:T(8,128)(2,1)}, u32[]{:S(2)}, u32[]{:S(2)}) collective-permute-start(bf16[6,2,16,1152]{3,2,1,0:T(8,128)(2,1)} %get-tuple-element.48), channel_id=1, source_target_pairs={{8,0},{16,8},{24,16},{9,1},{17,9},{25,17},{10,2},{18,10},{26,18},{... | collective-permute-start | bytes 1327112 | tf_op jit(solution)/shard_map/ppermute | solution.py:532
  17.7 14.2 %copy-start.1 = (bf16[512,512]{1,0:T(8,128)(2,1)S(1)}, bf16[512,512]{1,0:T(8,128)(2,1)}, u32[]{:S(2)}) copy-start(bf16[512,512]{1,0:T(8,128)(2,1)} %refs_0_) | copy-start | bytes 1572868
  17.7 14.2 %copy-start.2 = (bf16[512,512]{1,0:T(8,128)(2,1)S(1)}, bf16[512,512]{1,0:T(8,128)(2,1)}, u32[]{:S(2)}) copy-start(bf16[512,512]{1,0:T(8,128)(2,1)} %refs_1_) | copy-start | bytes 1572868
  17.7 14.2 %copy-start.3 = (bf16[512,512]{1,0:T(8,128)(2,1)S(1)}, bf16[512,512]{1,0:T(8,128)(2,1)}, u32[]{:S(2)}) copy-start(bf16[512,512]{1,0:T(8,128)(2,1)} %refs_2_) | copy-start | bytes 1572868
  17.7 14.7 %collective-permute-start.6 = (bf16[4,3,4,16,128]{4,3,2,1,0:T(8,128)(2,1)S(1)}, bf16[4,3,4,16,128]{4,3,2,1,0:T(8,128)(2,1)S(1)}, u32[]{:S(2)}, u32[]{:S(2)}) collective-permute-start(bf16[4,3,4,16,128]{4,3,2,1,0:T(8,128)(2,1)S(1)} %get-tuple-element.60), channel_id=1, source_target_pairs={{0,1},{1,0},{2,3},{3,2},{4,5},{5,4},{6,7},{7,6},{8,9},{9,8},{10,11... | collective-permute-start | bytes 589832 | tf_op jit(solution)/shard_map/ppermute | solution.py:513
  19.3 13.5 %collective-permute-start.7 = (bf16[4,3,4,16,128]{4,3,2,1,0:T(8,128)(2,1)S(1)}, bf16[4,3,4,16,128]{4,3,2,1,0:T(8,128)(2,1)S(1)}, u32[]{:S(2)}, u32[]{:S(2)}) collective-permute-start(bf16[4,3,4,16,128]{4,3,2,1,0:T(8,128)(2,1)S(1)} %get-tuple-element.61), channel_id=1, source_target_pairs={{0,2},{1,3},{2,0},{3,1},{4,6},{5,7},{6,4},{7,5},{8,10},{9,11},{10,... | collective-permute-start | bytes 589832 | tf_op jit(solution)/shard_map/ppermute | solution.py:513
  19.3 19.6 %copy-start.7 = (s32[1,8]{1,0:T(1,128)S(1)}, s32[1,8]{1,0:T(1,128)}, u32[]{:S(2)}) copy-start(s32[1,8]{1,0:T(1,128)} %counts_ref.11) | copy-start | bytes 100
  19.3 43.8 %copy-start.5 = (bf16[128,128]{1,0:T(8,128)(2,1)S(1)}, bf16[128,128]{1,0:T(8,128)(2,1)}, u32[]{:S(2)}) copy-start(bf16[128,128]{1,0:T(8,128)(2,1)} %refs_9_.1) | copy-start | bytes 98308
  19.3 43.8 %copy-start.8 = (s32[4,6]{1,0:T(4,128)S(1)}, s32[4,6]{1,0:T(4,128)}, u32[]{:S(2)}) copy-start(s32[4,6]{1,0:T(4,128)} %groups_ref.3) | copy-start | bytes 292
  19.3 18.9 %collective-permute-start.8 = (bf16[4,3,4,16,128]{4,3,2,1,0:T(8,128)(2,1)S(1)}, bf16[4,3,4,16,128]{4,3,2,1,0:T(8,128)(2,1)S(1)}, u32[]{:S(2)}, u32[]{:S(2)}) collective-permute-start(bf16[4,3,4,16,128]{4,3,2,1,0:T(8,128)(2,1)S(1)} %get-tuple-element.62), channel_id=1, source_target_pairs={{0,3},{1,2},{2,1},{3,0},{4,7},{5,6},{6,5},{7,4},{8,11},{9,10},{10,... | collective-permute-start | bytes 589832 | tf_op jit(solution)/shard_map/ppermute | solution.py:513
  30.4 14.8 %collective-permute-start.2 = (bf16[4,3,4,16,128]{4,3,2,1,0:T(8,128)(2,1)}, bf16[4,3,4,16,128]{4,3,2,1,0:T(8,128)(2,1)S(1)}, u32[]{:S(2)}, u32[]{:S(2)}) collective-permute-start(bf16[4,3,4,16,128]{4,3,2,1,0:T(8,128)(2,1)} %get-tuple-element.50), channel_id=1, source_target_pairs={{0,1},{1,0},{2,3},{3,2},{4,5},{5,4},{6,7},{7,6},{8,9},{9,8},{10,11... | collective-permute-start | bytes 589832 | tf_op jit(solution)/shard_map/ppermute | solution.py:513
  38.2 13.2 %collective-permute-start.9 = (bf16[4,3,4,16,128]{4,3,2,1,0:T(8,128)(2,1)}, bf16[4,3,4,16,128]{4,3,2,1,0:T(8,128)(2,1)S(1)}, u32[]{:S(2)}, u32[]{:S(2)}) collective-permute-start(bf16[4,3,4,16,128]{4,3,2,1,0:T(8,128)(2,1)} %get-tuple-element.77), channel_id=1, source_target_pairs={{0,4},{1,5},{2,6},{3,7},{4,0},{5,1},{6,2},{7,3},{8,12},{9,13},{10,... | collective-permute-start | bytes 589832 | tf_op jit(solution)/shard_map/ppermute | solution.py:513
  40.1 16.5 %collective-permute-start.13 = (bf16[4,3,4,16,128]{4,3,2,1,0:T(8,128)(2,1)S(1)}, bf16[4,3,4,16,128]{4,3,2,1,0:T(8,128)(2,1)S(1)}, u32[]{:S(2)}, u32[]{:S(2)}) collective-permute-start(bf16[4,3,4,16,128]{4,3,2,1,0:T(8,128)(2,1)S(1)} %get-tuple-element.85), channel_id=1, source_target_pairs={{0,2},{1,3},{2,0},{3,1},{4,6},{5,7},{6,4},{7,5},{8,10},{9,11},{10,... | collective-permute-start | bytes 589832 | tf_op jit(solution)/shard_map/ppermute | solution.py:513
  43.6 16.3 %collective-permute-start.14 = (bf16[4,3,4,16,128]{4,3,2,1,0:T(8,128)(2,1)S(1)}, bf16[4,3,4,16,128]{4,3,2,1,0:T(8,128)(2,1)S(1)}, u32[]{:S(2)}, u32[]{:S(2)}) collective-permute-start(bf16[4,3,4,16,128]{4,3,2,1,0:T(8,128)(2,1)S(1)} %get-tuple-element.86), channel_id=1, source_target_pairs={{0,3},{1,2},{2,1},{3,0},{4,7},{5,6},{6,5},{7,4},{8,11},{9,10},{10,... | collective-permute-start | bytes 589832 | tf_op jit(solution)/shard_map/ppermute | solution.py:513
  43.7 16.2 %collective-permute-start.15 = (bf16[4,3,4,16,128]{4,3,2,1,0:T(8,128)(2,1)S(1)}, bf16[4,3,4,16,128]{4,3,2,1,0:T(8,128)(2,1)S(1)}, u32[]{:S(2)}, u32[]{:S(2)}) collective-permute-start(bf16[4,3,4,16,128]{4,3,2,1,0:T(8,128)(2,1)S(1)} %get-tuple-element.88), channel_id=1, source_target_pairs={{0,1},{1,0},{2,3},{3,2},{4,5},{5,4},{6,7},{7,6},{8,9},{9,8},{10,11... | collective-permute-start | bytes 589832 | tf_op jit(solution)/shard_map/ppermute | solution.py:513
  45.2 23.7 %collective-permute-start.10 = (bf16[4,3,4,16,128]{4,3,2,1,0:T(8,128)(2,1)}, bf16[4,3,4,16,128]{4,3,2,1,0:T(8,128)(2,1)S(1)}, u32[]{:S(2)}, u32[]{:S(2)}) collective-permute-start(bf16[4,3,4,16,128]{4,3,2,1,0:T(8,128)(2,1)} %get-tuple-element.78), channel_id=1, source_target_pairs={{0,5},{1,4},{2,7},{3,6},{4,1},{5,0},{6,3},{7,2},{8,13},{9,12},{10,... | collective-permute-start | bytes 589832 | tf_op jit(solution)/shard_map/ppermute | solution.py:513
  51.4 17.5 %collective-permute-start.11 = (bf16[4,3,4,16,128]{4,3,2,1,0:T(8,128)(2,1)}, bf16[4,3,4,16,128]{4,3,2,1,0:T(8,128)(2,1)S(1)}, u32[]{:S(2)}, u32[]{:S(2)}) collective-permute-start(bf16[4,3,4,16,128]{4,3,2,1,0:T(8,128)(2,1)} %get-tuple-element.79), channel_id=1, source_target_pairs={{0,6},{1,7},{2,4},{3,5},{4,2},{5,3},{6,0},{7,1},{8,14},{9,15},{10,... | collective-permute-start | bytes 589832 | tf_op jit(solution)/shard_map/ppermute | solution.py:513
  56.6 12.3 %collective-permute-start.12 = (bf16[4,3,4,16,128]{4,3,2,1,0:T(8,128)(2,1)}, bf16[4,3,4,16,128]{4,3,2,1,0:T(8,128)(2,1)S(1)}, u32[]{:S(2)}, u32[]{:S(2)}) collective-permute-start(bf16[4,3,4,16,128]{4,3,2,1,0:T(8,128)(2,1)} %get-tuple-element.80), channel_id=1, source_target_pairs={{0,7},{1,6},{2,5},{3,4},{4,3},{5,2},{6,1},{7,0},{8,15},{9,14},{10,... | collective-permute-start | bytes 589832 | tf_op jit(solution)/shard_map/ppermute | solution.py:513
  59.9 12.9 %collective-permute-start.4 = (bf16[4,3,4,16,128]{4,3,2,1,0:T(8,128)(2,1)}, bf16[4,3,4,16,128]{4,3,2,1,0:T(8,128)(2,1)S(1)}, u32[]{:S(2)}, u32[]{:S(2)}) collective-permute-start(bf16[4,3,4,16,128]{4,3,2,1,0:T(8,128)(2,1)} %get-tuple-element.58), channel_id=1, source_target_pairs={{0,2},{1,3},{2,0},{3,1},{4,6},{5,7},{6,4},{7,5},{8,10},{9,11},{10,... | collective-permute-start | bytes 589832 | tf_op jit(solution)/shard_map/ppermute | solution.py:513
  59.9 17.0 %collective-permute-start.5 = (bf16[4,3,4,16,128]{4,3,2,1,0:T(8,128)(2,1)}, bf16[4,3,4,16,128]{4,3,2,1,0:T(8,128)(2,1)S(1)}, u32[]{:S(2)}, u32[]{:S(2)}) collective-permute-start(bf16[4,3,4,16,128]{4,3,2,1,0:T(8,128)(2,1)} %get-tuple-element.59), channel_id=1, source_target_pairs={{0,3},{1,2},{2,1},{3,0},{4,7},{5,6},{6,5},{7,4},{8,11},{9,10},{10,... | collective-permute-start | bytes 589832 | tf_op jit(solution)/shard_map/ppermute | solution.py:513
  63.1 13.8 %copy-start.4 = (bf16[4,3,4,16,128]{4,3,2,1,0:T(8,128)(2,1)S(1)}, bf16[4,3,4,16,128]{4,3,2,1,0:T(8,128)(2,1)}, u32[]{:S(2)}) copy-start(bf16[4,3,4,16,128]{4,3,2,1,0:T(8,128)(2,1)} %get-tuple-element.49.refs_0_) | copy-start | bytes 589828
  (2 other events, 3.2 us)

commit v8 on v7

--- a/solution.py
+++ b/solution.py
@@ -562,7 +562,9 @@
         mirrored = pack_half(crossed)
         edge[2:near], mirrored = lax.optimization_barrier((edge[2:near], mirrored))
         near_parts = inner_parts[1:]
-        near_parts, edge[near :] = lax.optimization_barrier((near_parts, edge[near :]))
+        near_parts, edge[near + 1 :] = lax.optimization_barrier(
+            (near_parts, edge[near + 1 :])
+        )
         inner_parts = inner_parts[:1] + near_parts
         edge_parts = [turned_exchange(x, turn) for turn, x in enumerate(edge)]
         mirrored = [turned_exchange(x, turn) for turn, x in enumerate(mirrored)]

time: 85.6 us -> 85.5 us (level); the launches traced: 84.4 us -> 85.3 us
  waiting for transfers between devices: 23.1 us -> 28.8 us
  starting transfers between devices: 27.7 us -> 23 us
    ppermute x14, waiting for transfers between devices: 23.1 us -> 28.8 us  [turned_exchange(): lax.ppermute(x, 'lev', [(i, i ^ turn) for i in range(owner_count)])]
    ppermute x14, starting transfers between devices: 24.1 us -> 19.3 us  [turned_exchange(): lax.ppermute(x, 'lev', [(i, i ^ turn) for i in range(owner_count)])]
  transfers between devices with their start and end apart: 16 -> 16, of which waited for: 7 -> 8; matrix products, arithmetic and copies ran while one was open for 0% -> 0% of each run, Pallas kernels for 21% -> 21%
where the time goes in v8:
time: 85.5 us; the launch traced here: 85.3 us
  Pallas kernels  32.2 us (38%)
  waiting for transfers between devices  28.8 us (34%)
  starting transfers between devices  23 us (27%)
  local copies, waits for them, and re-layouts  1.11 us (1%)
    ppermute x14, waiting for transfers between devices, turned_exchange(): lax.ppermute(x, 'lev', [(i, i ^ turn) for i in range(owner_count)])  28.8 us
    ppermute x14, starting transfers between devices, turned_exchange(): lax.ppermute(x, 'lev', [(i, i ^ turn) for i in range(owner_count)])  19.3 us
    pallas_call x1, Pallas kernels, shards(): pl.pallas_call(functools.partial(edge_kernel, lat_rows, by_turn), in_spec...  8.97 us
    pallas_call x1, Pallas kernels, shards(): pl.pallas_call(functools.partial(last_kernel, edge_rows, inner_rows, by_t...  7.45 us
    pallas_call x1, Pallas kernels, shards(): pl.pallas_call(functools.partial(inner_kernel, lat_rows, by_turn), in_spe...  7.24 us
    pallas_call x1, Pallas kernels, shards(): pl.pallas_call(functools.partial(half_kernel, lat_rows, inner_rows, by_tu...  5.76 us
    ppermute x1, starting transfers between devices, shards(): before = lax.ppermute(last, 'lat', up)  2.38 us
    pallas_call x2, Pallas kernels, pack_half(): pl.pallas_call(mirror_kernel, in_specs=[smem, pl.BlockSpec(memory_space=p...  2.37 us
  transfers between devices with their start and end apart: 16, of which 8 were waited for; matrix products, arithmetic and copies ran while one was open for 0% of the time, Pallas kernels for 21%

profile of v8, /device:TPU:0, one launch (start us, length us, event | category | flops | bytes accessed | tf_op | source)
XLA Modules:
  0.0 85.3 jit_solution(14137592909744364575)
XLA Ops:
  0.0 7.2 %inner_rows.1 = (bf16[4,9,4,16,128]{4,3,2,1,0:T(8,128)(2,1)}, bf16[6,2,16,1152]{3,2,1,0:T(8,128)(2,1)}, bf16[6,2,16,1152]{3,2,1,0:T(8,128)(2,1)}) custom-call(s32[1,8]{1,0:T(1,128)} %counts_ref.11, f32[4,128,1152]{2,1,0:T(8,128)} %bitcast.3, f32[2,128,1152]{2,1,0:T(8,128)} %bitcast.5), custom_call_target="tpu_custom_call" | custom-call | flops 1 | bytes 1 | tf_op jit(solution)/shard_map/inner_rows/pallas_call | solution.py:488
  7.3 2.4 %collective-permute-start = (bf16[6,2,16,1152]{3,2,1,0:T(8,128)(2,1)}, bf16[6,2,16,1152]{3,2,1,0:T(8,128)(2,1)S(1)}, u32[]{:S(2)}, u32[]{:S(2)}) collective-permute-start(bf16[6,2,16,1152]{3,2,1,0:T(8,128)(2,1)} %get-tuple-element.46), channel_id=1, source_target_pairs={{0,8},{8,16},{16,24},{1,9},{9,17},{17,25},{2,10},{10,18},{18,26},{... | collective-permute-start | bytes 1327112 | tf_op jit(solution)/shard_map/ppermute | solution.py:531
  9.6 4.5 %collective-permute-start.3 = (bf16[4,9,4,16,128]{4,3,2,1,0:T(8,128)(2,1)}, bf16[4,9,4,16,128]{4,3,2,1,0:T(8,128)(2,1)S(1)}, u32[]{:S(2)}, u32[]{:S(2)}) collective-permute-start(bf16[4,9,4,16,128]{4,3,2,1,0:T(8,128)(2,1)} %get-tuple-element.52.raw_ref), channel_id=1, source_target_pairs={{0,6},{1,7},{2,4},{3,5},{4,2},{5,3},{6,0},{7,1},{8,14},{9,15},{10,... | collective-permute-start | bytes 1769480 | tf_op jit(solution)/shard_map/ppermute | solution.py:513
  14.1 1.3 %collective-permute-start.1 = (bf16[6,2,16,1152]{3,2,1,0:T(8,128)(2,1)}, bf16[6,2,16,1152]{3,2,1,0:T(8,128)(2,1)}, u32[]{:S(2)}, u32[]{:S(2)}) collective-permute-start(bf16[6,2,16,1152]{3,2,1,0:T(8,128)(2,1)} %get-tuple-element.47), channel_id=1, source_target_pairs={{8,0},{16,8},{24,16},{9,1},{17,9},{25,17},{10,2},{18,10},{26,18},{... | collective-permute-start | bytes 1327112 | tf_op jit(solution)/shard_map/ppermute | solution.py:532
  15.4 1.1 %copy-done = bf16[4,9,4,16,128]{4,3,2,1,0:T(8,128)(2,1)S(1)} copy-done((bf16[4,9,4,16,128]{4,3,2,1,0:T(8,128)(2,1)S(1)}, bf16[4,9,4,16,128]{4,3,2,1,0:T(8,128)(2,1)}, u32[]{:S(2)}) %copy-start) | copy-done | bytes 589848
  16.5 1.2 %half_slots.3 = (bf16[4,3,4,16,128]{4,3,2,1,0:T(8,128)(2,1)S(1)}, bf16[4,3,4,16,128]{4,3,2,1,0:T(8,128)(2,1)S(1)}, bf16[4,3,4,16,128]{4,3,2,1,0:T(8,128)(2,1)S(1)}, bf16[4,3,4,16,128]{4,3,2,1,0:T(8,128)(2,1)S(1)}) custom-call(s32[1,8]{1,0:T(1,128)S(1)} %copy-done.6, bf16[4,9,4,16,128]{4,3,2,1,0:T(8,128)(2,1)S(1)} %copy-done), custom_call_target="tpu_custom_call" | custom-call | flops 1 | bytes 1 | tf_op jit(solution)/shard_map/half_slots/pallas_call | solution.py:516
  17.7 1.6 %collective-permute-start.7 = (bf16[4,3,4,16,128]{4,3,2,1,0:T(8,128)(2,1)S(1)}, bf16[4,3,4,16,128]{4,3,2,1,0:T(8,128)(2,1)S(1)}, u32[]{:S(2)}, u32[]{:S(2)}) collective-permute-start(bf16[4,3,4,16,128]{4,3,2,1,0:T(8,128)(2,1)S(1)} %get-tuple-element.70), channel_id=1, source_target_pairs={{0,1},{1,0},{2,3},{3,2},{4,5},{5,4},{6,7},{7,6},{8,9},{9,8},{10,11... | collective-permute-start | bytes 589832 | tf_op jit(solution)/shard_map/ppermute | solution.py:513
  19.3 2.0 %collective-permute-start.9 = (bf16[4,3,4,16,128]{4,3,2,1,0:T(8,128)(2,1)S(1)}, bf16[4,3,4,16,128]{4,3,2,1,0:T(8,128)(2,1)S(1)}, u32[]{:S(2)}, u32[]{:S(2)}) collective-permute-start(bf16[4,3,4,16,128]{4,3,2,1,0:T(8,128)(2,1)S(1)} %get-tuple-element.72), channel_id=1, source_target_pairs={{0,3},{1,2},{2,1},{3,0},{4,7},{5,6},{6,5},{7,4},{8,11},{9,10},{10,... | collective-permute-start | bytes 589832 | tf_op jit(solution)/shard_map/ppermute | solution.py:513
  21.4 9.0 %edge_rows.1 = (bf16[4,3,4,16,128]{4,3,2,1,0:T(8,128)(2,1)}, bf16[4,3,4,16,128]{4,3,2,1,0:T(8,128)(2,1)}, bf16[4,3,4,16,128]{4,3,2,1,0:T(8,128)(2,1)}, bf16[4,3,...) custom-call(s32[1,8]{1,0:T(1,128)} %counts_ref.11, ...), custom_call_target="tpu_custom_call" | custom-call | flops 1 | bytes 1 | tf_op jit(solution)/shard_map/edge_rows/pallas_call | solution.py:535
  30.4 1.6 %collective-permute-start.2 = (bf16[4,3,4,16,128]{4,3,2,1,0:T(8,128)(2,1)}, bf16[4,3,4,16,128]{4,3,2,1,0:T(8,128)(2,1)S(1)}, u32[]{:S(2)}, u32[]{:S(2)}) collective-permute-start(bf16[4,3,4,16,128]{4,3,2,1,0:T(8,128)(2,1)} %get-tuple-element.49), channel_id=1, source_target_pairs={{0,1},{1,0},{2,3},{3,2},{4,5},{5,4},{6,7},{7,6},{8,9},{9,8},{10,11... | collective-permute-start | bytes 589832 | tf_op jit(solution)/shard_map/ppermute | solution.py:513
  32.8 5.5 %collective-permute-done.9.refs_3_ = bf16[4,3,4,16,128]{4,3,2,1,0:T(8,128)(2,1)S(1)} collective-permute-done((bf16[4,3,4,16,128]{4,3,2,1,0:T(8,128)(2,1)S(1)}, bf16[4,3,4,16,128]{4,3,2,1,0:T(8,128)(2,1)S(1)}, u32[]{:S(2)}, u32[]{:S(2)}) %collective-permute-start.9) | collective-permute-done | bytes 196640 | tf_op jit(solution)/shard_map/ppermute | solution.py:513
  38.2 1.6 %collective-permute-start.10 = (bf16[4,3,4,16,128]{4,3,2,1,0:T(8,128)(2,1)}, bf16[4,3,4,16,128]{4,3,2,1,0:T(8,128)(2,1)S(1)}, u32[]{:S(2)}, u32[]{:S(2)}) collective-permute-start(bf16[4,3,4,16,128]{4,3,2,1,0:T(8,128)(2,1)} %get-tuple-element.76), channel_id=1, source_target_pairs={{0,5},{1,4},{2,7},{3,6},{4,1},{5,0},{6,3},{7,2},{8,13},{9,12},{10,... | collective-permute-start | bytes 589832 | tf_op jit(solution)/shard_map/ppermute | solution.py:513
  39.8 1.2 %half_slots.2 = (bf16[4,3,4,16,128]{4,3,2,1,0:T(8,128)(2,1)S(1)}, bf16[4,3,4,16,128]{4,3,2,1,0:T(8,128)(2,1)S(1)}, bf16[4,3,4,16,128]{4,3,2,1,0:T(8,128)(2,1)S(1)}, bf16[4,3,4,16,128]{4,3,2,1,0:T(8,128)(2,1)S(1)}) custom-call(s32[1,8]{1,0:T(1,128)S(1)} %copy-done.7, bf16[4,9,4,16,128]{4,3,2,1,0:T(8,128)(2,1)S(1)} %collective-permute-done.3.raw_ref), custom_call_target="tpu_custom_call" | custom-call | flops 1 | bytes 1 | tf_op jit(solution)/shard_map/half_slots/pallas_call | solution.py:516
  41.0 2.6 %collective-permute-start.13 = (bf16[4,3,4,16,128]{4,3,2,1,0:T(8,128)(2,1)S(1)}, bf16[4,3,4,16,128]{4,3,2,1,0:T(8,128)(2,1)S(1)}, u32[]{:S(2)}, u32[]{:S(2)}) collective-permute-start(bf16[4,3,4,16,128]{4,3,2,1,0:T(8,128)(2,1)S(1)} %get-tuple-element.83), channel_id=1, source_target_pairs={{0,2},{1,3},{2,0},{3,1},{4,6},{5,7},{6,4},{7,5},{8,10},{9,11},{10,... | collective-permute-start | bytes 589832 | tf_op jit(solution)/shard_map/ppermute | solution.py:513
  45.2 1.4 %collective-permute-start.11 = (bf16[4,3,4,16,128]{4,3,2,1,0:T(8,128)(2,1)}, bf16[4,3,4,16,128]{4,3,2,1,0:T(8,128)(2,1)S(1)}, u32[]{:S(2)}, u32[]{:S(2)}) collective-permute-start(bf16[4,3,4,16,128]{4,3,2,1,0:T(8,128)(2,1)} %get-tuple-element.77), channel_id=1, source_target_pairs={{0,6},{1,7},{2,4},{3,5},{4,2},{5,3},{6,0},{7,1},{8,14},{9,15},{10,... | collective-permute-start | bytes 589832 | tf_op jit(solution)/shard_map/ppermute | solution.py:513
  46.6 5.7 %collective-permute-done.10.refs_5_ = bf16[4,3,4,16,128]{4,3,2,1,0:T(8,128)(2,1)S(1)} collective-permute-done((bf16[4,3,4,16,128]{4,3,2,1,0:T(8,128)(2,1)}, bf16[4,3,4,16,128]{4,3,2,1,0:T(8,128)(2,1)S(1)}, u32[]{:S(2)}, u32[]{:S(2)}) %collective-permute-start.10) | collective-permute-done | bytes 196640 | tf_op jit(solution)/shard_map/ppermute | solution.py:513
  52.2 2.0 %collective-permute-start.12 = (bf16[4,3,4,16,128]{4,3,2,1,0:T(8,128)(2,1)}, bf16[4,3,4,16,128]{4,3,2,1,0:T(8,128)(2,1)S(1)}, u32[]{:S(2)}, u32[]{:S(2)}) collective-permute-start(bf16[4,3,4,16,128]{4,3,2,1,0:T(8,128)(2,1)} %get-tuple-element.78), channel_id=1, source_target_pairs={{0,7},{1,6},{2,5},{3,4},{4,3},{5,2},{6,1},{7,0},{8,15},{9,14},{10,... | collective-permute-start | bytes 589832 | tf_op jit(solution)/shard_map/ppermute | solution.py:513
  54.2 2.6 %collective-permute-done.14.refs_5_ = bf16[4,3,4,16,128]{4,3,2,1,0:T(8,128)(2,1)S(1)} collective-permute-done((bf16[4,3,4,16,128]{4,3,2,1,0:T(8,128)(2,1)S(1)}, bf16[4,3,4,16,128]{4,3,2,1,0:T(8,128)(2,1)S(1)}, u32[]{:S(2)}, u32[]{:S(2)}) %collective-permute-start.14) | collective-permute-done | bytes 196640 | tf_op jit(solution)/shard_map/ppermute | solution.py:513
  56.9 1.3 %collective-permute-done.15.refs_7_ = bf16[4,3,4,16,128]{4,3,2,1,0:T(8,128)(2,1)S(1)} collective-permute-done((bf16[4,3,4,16,128]{4,3,2,1,0:T(8,128)(2,1)S(1)}, bf16[4,3,4,16,128]{4,3,2,1,0:T(8,128)(2,1)S(1)}, u32[]{:S(2)}, u32[]{:S(2)}) %collective-permute-start.15) | collective-permute-done | bytes 196640 | tf_op jit(solution)/shard_map/ppermute | solution.py:513
  58.7 5.8 %inner_columns.1.refs_8_ = bf16[4,512,384]{2,1,0:T(8,128)(2,1)S(1)} custom-call(s32[4,6]{1,0:T(4,128)S(1)} %copy-done.8, s32[1,8]{1,0:T(1,128)S(1)} %copy-done.7, bf16[4,3,4,16,128]{4,3,2,1,0:T(8,128)(2,1)S(1)} %get-tuple-element.79.refs_0_, bf16[4,3,4,16,128]{4,3,2,1,0:T(8,128)(2,1)S(1)} %collective-permute-done.7.refs_1_, ...), custom_call_target="tpu_custom_call" | custom-call | flops 1 | bytes 1 | tf_op jit(solution)/shard_map/inner_columns/pallas_call | solution.py:601
  64.5 1.0 %collective-permute-done.12.refs_7_ = bf16[4,3,4,16,128]{4,3,2,1,0:T(8,128)(2,1)S(1)} collective-permute-done((bf16[4,3,4,16,128]{4,3,2,1,0:T(8,128)(2,1)}, bf16[4,3,4,16,128]{4,3,2,1,0:T(8,128)(2,1)S(1)}, u32[]{:S(2)}, u32[]{:S(2)}) %collective-permute-start.12) | collective-permute-done | bytes 196640 | tf_op jit(solution)/shard_map/ppermute | solution.py:513
  65.5 10.1 %collective-permute-done.6.refs_4_ = bf16[4,3,4,16,128]{4,3,2,1,0:T(8,128)(2,1)S(1)} collective-permute-done((bf16[4,3,4,16,128]{4,3,2,1,0:T(8,128)(2,1)}, bf16[4,3,4,16,128]{4,3,2,1,0:T(8,128)(2,1)S(1)}, u32[]{:S(2)}, u32[]{:S(2)}) %collective-permute-start.6) | collective-permute-done | bytes 196640 | tf_op jit(solution)/shard_map/ppermute | solution.py:513
  75.6 2.2 %collective-permute-done.5.refs_3_ = bf16[4,3,4,16,128]{4,3,2,1,0:T(8,128)(2,1)S(1)} collective-permute-done((bf16[4,3,4,16,128]{4,3,2,1,0:T(8,128)(2,1)}, bf16[4,3,4,16,128]{4,3,2,1,0:T(8,128)(2,1)S(1)}, u32[]{:S(2)}, u32[]{:S(2)}) %collective-permute-start.5) | collective-permute-done | bytes 196640 | tf_op jit(solution)/shard_map/ppermute | solution.py:513
  77.8 7.5 %edge_columns.1 = bf16[512,8,384]{2,1,0:T(8,128)(2,1)} custom-call(s32[4,6]{1,0:T(4,128)S(1)} %copy-done.8, s32[1,8]{1,0:T(1,128)S(1)} %copy-done.7, bf16[4,3,4,16,128]{4,3,2,1,0:T(8,128)(2,1)S(1)} %copy-done.4, bf16[4,3,4,16,128]{4,3,2,1,0:T(8,128)(2,1)S(1)} %collective-permute-done.2.refs_1_, ...), custom_call_target="tpu_custom_call" | custom-call | flops 1 | bytes 1 | tf_op jit(solution)/shard_map/edge_columns/pallas_call | solution.py:612
  (35 shorter events, 3.0 us)
Async XLA Ops:
  0.0 15.4 %copy-start.6 = (s32[1,8]{1,0:T(1,128)S(1)}, s32[1,8]{1,0:T(1,128)}, u32[]{:S(2)}) copy-start(s32[1,8]{1,0:T(1,128)} %counts_ref.11) | copy-start | bytes 100
  7.3 12.0 %collective-permute-start = (bf16[6,2,16,1152]{3,2,1,0:T(8,128)(2,1)}, bf16[6,2,16,1152]{3,2,1,0:T(8,128)(2,1)S(1)}, u32[]{:S(2)}, u32[]{:S(2)}) collective-permute-start(bf16[6,2,16,1152]{3,2,1,0:T(8,128)(2,1)} %get-tuple-element.46), channel_id=1, source_target_pairs={{0,8},{8,16},{16,24},{1,9},{9,17},{17,25},{2,10},{10,18},{18,26},{... | collective-permute-start | bytes 1327112 | tf_op jit(solution)/shard_map/ppermute | solution.py:531
  9.6 30.2 %collective-permute-start.3 = (bf16[4,9,4,16,128]{4,3,2,1,0:T(8,128)(2,1)}, bf16[4,9,4,16,128]{4,3,2,1,0:T(8,128)(2,1)S(1)}, u32[]{:S(2)}, u32[]{:S(2)}) collective-permute-start(bf16[4,9,4,16,128]{4,3,2,1,0:T(8,128)(2,1)} %get-tuple-element.52.raw_ref), channel_id=1, source_target_pairs={{0,6},{1,7},{2,4},{3,5},{4,2},{5,3},{6,0},{7,1},{8,14},{9,15},{10,... | collective-permute-start | bytes 1769480 | tf_op jit(solution)/shard_map/ppermute | solution.py:513
  14.1 7.2 %collective-permute-start.1 = (bf16[6,2,16,1152]{3,2,1,0:T(8,128)(2,1)}, bf16[6,2,16,1152]{3,2,1,0:T(8,128)(2,1)}, u32[]{:S(2)}, u32[]{:S(2)}) collective-permute-start(bf16[6,2,16,1152]{3,2,1,0:T(8,128)(2,1)} %get-tuple-element.47), channel_id=1, source_target_pairs={{8,0},{16,8},{24,16},{9,1},{17,9},{25,17},{10,2},{18,10},{26,18},{... | collective-permute-start | bytes 1327112 | tf_op jit(solution)/shard_map/ppermute | solution.py:532
  17.7 14.2 %copy-start.1 = (bf16[512,512]{1,0:T(8,128)(2,1)S(1)}, bf16[512,512]{1,0:T(8,128)(2,1)}, u32[]{:S(2)}) copy-start(bf16[512,512]{1,0:T(8,128)(2,1)} %refs_0_) | copy-start | bytes 1572868
  17.7 14.2 %copy-start.2 = (bf16[512,512]{1,0:T(8,128)(2,1)S(1)}, bf16[512,512]{1,0:T(8,128)(2,1)}, u32[]{:S(2)}) copy-start(bf16[512,512]{1,0:T(8,128)(2,1)} %refs_1_) | copy-start | bytes 1572868
  17.7 14.2 %copy-start.3 = (bf16[512,512]{1,0:T(8,128)(2,1)S(1)}, bf16[512,512]{1,0:T(8,128)(2,1)}, u32[]{:S(2)}) copy-start(bf16[512,512]{1,0:T(8,128)(2,1)} %refs_2_) | copy-start | bytes 1572868
  17.7 14.7 %collective-permute-start.7 = (bf16[4,3,4,16,128]{4,3,2,1,0:T(8,128)(2,1)S(1)}, bf16[4,3,4,16,128]{4,3,2,1,0:T(8,128)(2,1)S(1)}, u32[]{:S(2)}, u32[]{:S(2)}) collective-permute-start(bf16[4,3,4,16,128]{4,3,2,1,0:T(8,128)(2,1)S(1)} %get-tuple-element.70), channel_id=1, source_target_pairs={{0,1},{1,0},{2,3},{3,2},{4,5},{5,4},{6,7},{7,6},{8,9},{9,8},{10,11... | collective-permute-start | bytes 589832 | tf_op jit(solution)/shard_map/ppermute | solution.py:513
  19.3 13.5 %collective-permute-start.8 = (bf16[4,3,4,16,128]{4,3,2,1,0:T(8,128)(2,1)S(1)}, bf16[4,3,4,16,128]{4,3,2,1,0:T(8,128)(2,1)S(1)}, u32[]{:S(2)}, u32[]{:S(2)}) collective-permute-start(bf16[4,3,4,16,128]{4,3,2,1,0:T(8,128)(2,1)S(1)} %get-tuple-element.71), channel_id=1, source_target_pairs={{0,2},{1,3},{2,0},{3,1},{4,6},{5,7},{6,4},{7,5},{8,10},{9,11},{10,... | collective-permute-start | bytes 589832 | tf_op jit(solution)/shard_map/ppermute | solution.py:513
  19.3 20.5 %copy-start.7 = (s32[1,8]{1,0:T(1,128)S(1)}, s32[1,8]{1,0:T(1,128)}, u32[]{:S(2)}) copy-start(s32[1,8]{1,0:T(1,128)} %counts_ref.11) | copy-start | bytes 100
  19.3 39.4 %copy-start.5 = (bf16[128,128]{1,0:T(8,128)(2,1)S(1)}, bf16[128,128]{1,0:T(8,128)(2,1)}, u32[]{:S(2)}) copy-start(bf16[128,128]{1,0:T(8,128)(2,1)} %refs_9_.1) | copy-start | bytes 98308
  19.3 39.4 %copy-start.8 = (s32[4,6]{1,0:T(4,128)S(1)}, s32[4,6]{1,0:T(4,128)}, u32[]{:S(2)}) copy-start(s32[4,6]{1,0:T(4,128)} %groups_ref.3) | copy-start | bytes 292
  19.3 18.9 %collective-permute-start.9 = (bf16[4,3,4,16,128]{4,3,2,1,0:T(8,128)(2,1)S(1)}, bf16[4,3,4,16,128]{4,3,2,1,0:T(8,128)(2,1)S(1)}, u32[]{:S(2)}, u32[]{:S(2)}) collective-permute-start(bf16[4,3,4,16,128]{4,3,2,1,0:T(8,128)(2,1)S(1)} %get-tuple-element.72), channel_id=1, source_target_pairs={{0,3},{1,2},{2,1},{3,0},{4,7},{5,6},{6,5},{7,4},{8,11},{9,10},{10,... | collective-permute-start | bytes 589832 | tf_op jit(solution)/shard_map/ppermute | solution.py:513
  30.4 14.8 %collective-permute-start.2 = (bf16[4,3,4,16,128]{4,3,2,1,0:T(8,128)(2,1)}, bf16[4,3,4,16,128]{4,3,2,1,0:T(8,128)(2,1)S(1)}, u32[]{:S(2)}, u32[]{:S(2)}) collective-permute-start(bf16[4,3,4,16,128]{4,3,2,1,0:T(8,128)(2,1)} %get-tuple-element.49), channel_id=1, source_target_pairs={{0,1},{1,0},{2,3},{3,2},{4,5},{5,4},{6,7},{7,6},{8,9},{9,8},{10,11... | collective-permute-start | bytes 589832 | tf_op jit(solution)/shard_map/ppermute | solution.py:513
  38.2 14.0 %collective-permute-start.10 = (bf16[4,3,4,16,128]{4,3,2,1,0:T(8,128)(2,1)}, bf16[4,3,4,16,128]{4,3,2,1,0:T(8,128)(2,1)S(1)}, u32[]{:S(2)}, u32[]{:S(2)}) collective-permute-start(bf16[4,3,4,16,128]{4,3,2,1,0:T(8,128)(2,1)} %get-tuple-element.76), channel_id=1, source_target_pairs={{0,5},{1,4},{2,7},{3,6},{4,1},{5,0},{6,3},{7,2},{8,13},{9,12},{10,... | collective-permute-start | bytes 589832 | tf_op jit(solution)/shard_map/ppermute | solution.py:513
  41.0 13.2 %collective-permute-start.13 = (bf16[4,3,4,16,128]{4,3,2,1,0:T(8,128)(2,1)S(1)}, bf16[4,3,4,16,128]{4,3,2,1,0:T(8,128)(2,1)S(1)}, u32[]{:S(2)}, u32[]{:S(2)}) collective-permute-start(bf16[4,3,4,16,128]{4,3,2,1,0:T(8,128)(2,1)S(1)} %get-tuple-element.83), channel_id=1, source_target_pairs={{0,2},{1,3},{2,0},{3,1},{4,6},{5,7},{6,4},{7,5},{8,10},{9,11},{10,... | collective-permute-start | bytes 589832 | tf_op jit(solution)/shard_map/ppermute | solution.py:513
  43.6 13.3 %collective-permute-start.14 = (bf16[4,3,4,16,128]{4,3,2,1,0:T(8,128)(2,1)S(1)}, bf16[4,3,4,16,128]{4,3,2,1,0:T(8,128)(2,1)S(1)}, u32[]{:S(2)}, u32[]{:S(2)}) collective-permute-start(bf16[4,3,4,16,128]{4,3,2,1,0:T(8,128)(2,1)S(1)} %get-tuple-element.84), channel_id=1, source_target_pairs={{0,3},{1,2},{2,1},{3,0},{4,7},{5,6},{6,5},{7,4},{8,11},{9,10},{10,... | collective-permute-start | bytes 589832 | tf_op jit(solution)/shard_map/ppermute | solution.py:513
  44.6 13.6 %collective-permute-start.15 = (bf16[4,3,4,16,128]{4,3,2,1,0:T(8,128)(2,1)S(1)}, bf16[4,3,4,16,128]{4,3,2,1,0:T(8,128)(2,1)S(1)}, u32[]{:S(2)}, u32[]{:S(2)}) collective-permute-start(bf16[4,3,4,16,128]{4,3,2,1,0:T(8,128)(2,1)S(1)} %get-tuple-element.86), channel_id=1, source_target_pairs={{0,1},{1,0},{2,3},{3,2},{4,5},{5,4},{6,7},{7,6},{8,9},{9,8},{10,11... | collective-permute-start | bytes 589832 | tf_op jit(solution)/shard_map/ppermute | solution.py:513
  45.2 19.3 %collective-permute-start.11 = (bf16[4,3,4,16,128]{4,3,2,1,0:T(8,128)(2,1)}, bf16[4,3,4,16,128]{4,3,2,1,0:T(8,128)(2,1)S(1)}, u32[]{:S(2)}, u32[]{:S(2)}) collective-permute-start(bf16[4,3,4,16,128]{4,3,2,1,0:T(8,128)(2,1)} %get-tuple-element.77), channel_id=1, source_target_pairs={{0,6},{1,7},{2,4},{3,5},{4,2},{5,3},{6,0},{7,1},{8,14},{9,15},{10,... | collective-permute-start | bytes 589832 | tf_op jit(solution)/shard_map/ppermute | solution.py:513
  52.2 13.2 %collective-permute-start.12 = (bf16[4,3,4,16,128]{4,3,2,1,0:T(8,128)(2,1)}, bf16[4,3,4,16,128]{4,3,2,1,0:T(8,128)(2,1)S(1)}, u32[]{:S(2)}, u32[]{:S(2)}) collective-permute-start(bf16[4,3,4,16,128]{4,3,2,1,0:T(8,128)(2,1)} %get-tuple-element.78), channel_id=1, source_target_pairs={{0,7},{1,6},{2,5},{3,4},{4,3},{5,2},{6,1},{7,0},{8,15},{9,14},{10,... | collective-permute-start | bytes 589832 | tf_op jit(solution)/shard_map/ppermute | solution.py:513
  54.2 21.4 %collective-permute-start.6 = (bf16[4,3,4,16,128]{4,3,2,1,0:T(8,128)(2,1)}, bf16[4,3,4,16,128]{4,3,2,1,0:T(8,128)(2,1)S(1)}, u32[]{:S(2)}, u32[]{:S(2)}) collective-permute-start(bf16[4,3,4,16,128]{4,3,2,1,0:T(8,128)(2,1)} %get-tuple-element.69), channel_id=1, source_target_pairs={{0,4},{1,5},{2,6},{3,7},{4,0},{5,1},{6,2},{7,3},{8,12},{9,13},{10,... | collective-permute-start | bytes 589832 | tf_op jit(solution)/shard_map/ppermute | solution.py:513
  56.9 18.7 %collective-permute-start.4 = (bf16[4,3,4,16,128]{4,3,2,1,0:T(8,128)(2,1)}, bf16[4,3,4,16,128]{4,3,2,1,0:T(8,128)(2,1)S(1)}, u32[]{:S(2)}, u32[]{:S(2)}) collective-permute-start(bf16[4,3,4,16,128]{4,3,2,1,0:T(8,128)(2,1)} %get-tuple-element.57), channel_id=1, source_target_pairs={{0,2},{1,3},{2,0},{3,1},{4,6},{5,7},{6,4},{7,5},{8,10},{9,11},{10,... | collective-permute-start | bytes 589832 | tf_op jit(solution)/shard_map/ppermute | solution.py:513
  58.2 19.6 %collective-permute-start.5 = (bf16[4,3,4,16,128]{4,3,2,1,0:T(8,128)(2,1)}, bf16[4,3,4,16,128]{4,3,2,1,0:T(8,128)(2,1)S(1)}, u32[]{:S(2)}, u32[]{:S(2)}) collective-permute-start(bf16[4,3,4,16,128]{4,3,2,1,0:T(8,128)(2,1)} %get-tuple-element.58), channel_id=1, source_target_pairs={{0,3},{1,2},{2,1},{3,0},{4,7},{5,6},{6,5},{7,4},{8,11},{9,10},{10,... | collective-permute-start | bytes 589832 | tf_op jit(solution)/shard_map/ppermute | solution.py:513
  58.7 19.1 %copy-start.4 = (bf16[4,3,4,16,128]{4,3,2,1,0:T(8,128)(2,1)S(1)}, bf16[4,3,4,16,128]{4,3,2,1,0:T(8,128)(2,1)}, u32[]{:S(2)}) copy-start(bf16[4,3,4,16,128]{4,3,2,1,0:T(8,128)(2,1)} %get-tuple-element.48.refs_0_) | copy-start | bytes 589828
  (2 other events, 3.2 us)

commit v9 on v8

--- a/solution.py
+++ b/solution.py
@@ -193,7 +193,6 @@
 
     def one_field(field, carry):
         wait(field)
-        keep_halo(field)
 
         def one_group(group, carry):
             place = pl.ds(group * size, size)
@@ -216,11 +215,15 @@
                 raw_ref[field, tile] = kept_ref[tile].astype(raw_ref.dtype)
         else:
             pack_rows(kept_ref, turned_starts(start_ref, False, slots), blocks, store)
-        for copy in halo_out(field) + field_out(field):
+        for copy in field_out(field):
             copy.start()
         return carry
 
     lax.fori_loop(0, fields, one_field, 0)
+    for field in range(fields):
+        keep_halo(field)
+        for copy in halo_out(field):
+            copy.start()
     for field in range(fields):
         for copy in field_out(field):
             copy.wait()

time: 85.5 us -> 85.5 us (level)
  no operation moved by 1% of the time
where the time goes in v9:
time: 85.5 us; the launch traced here: 85.3 us
  Pallas kernels  32.2 us (38%)
  waiting for transfers between devices  28.8 us (34%)
  starting transfers between devices  23 us (27%)
  local copies, waits for them, and re-layouts  1.11 us (1%)
    ppermute x14, waiting for transfers between devices, turned_exchange(): lax.ppermute(x, 'lev', [(i, i ^ turn) for i in range(owner_count)])  28.8 us
    ppermute x14, starting transfers between devices, turned_exchange(): lax.ppermute(x, 'lev', [(i, i ^ turn) for i in range(owner_count)])  19.3 us
    pallas_call x1, Pallas kernels, shards(): pl.pallas_call(functools.partial(edge_kernel, lat_rows, by_turn), in_spec...  8.97 us
    pallas_call x1, Pallas kernels, shards(): pl.pallas_call(functools.partial(last_kernel, edge_rows, inner_rows, by_t...  7.46 us
    pallas_call x1, Pallas kernels, shards(): pl.pallas_call(functools.partial(inner_kernel, lat_rows, by_turn), in_spe...  7.22 us
    pallas_call x1, Pallas kernels, shards(): pl.pallas_call(functools.partial(half_kernel, lat_rows, inner_rows, by_tu...  5.76 us
    ppermute x1, starting transfers between devices, shards(): before = lax.ppermute(last, 'lat', up)  2.38 us
    pallas_call x2, Pallas kernels, pack_half(): pl.pallas_call(mirror_kernel, in_specs=[smem, pl.BlockSpec(memory_space=p...  2.37 us
  transfers between devices with their start and end apart: 16, of which 8 were waited for; matrix products, arithmetic and copies ran while one was open for 0% of the time, Pallas kernels for 21%

profile of v9, /device:TPU:0, one launch (start us, length us, event | category | flops | bytes accessed | tf_op | source)
XLA Modules:
  0.0 85.3 jit_solution(17984948509449044778)
XLA Ops:
  0.0 7.2 %inner_rows.1 = (bf16[4,9,4,16,128]{4,3,2,1,0:T(8,128)(2,1)}, bf16[6,2,16,1152]{3,2,1,0:T(8,128)(2,1)}, bf16[6,2,16,1152]{3,2,1,0:T(8,128)(2,1)}) custom-call(s32[1,8]{1,0:T(1,128)} %counts_ref.11, f32[4,128,1152]{2,1,0:T(8,128)} %bitcast.3, f32[2,128,1152]{2,1,0:T(8,128)} %bitcast.5), custom_call_target="tpu_custom_call" | custom-call | flops 1 | bytes 1 | tf_op jit(solution)/shard_map/inner_rows/pallas_call | solution.py:491
  7.2 2.4 %collective-permute-start = (bf16[6,2,16,1152]{3,2,1,0:T(8,128)(2,1)}, bf16[6,2,16,1152]{3,2,1,0:T(8,128)(2,1)S(1)}, u32[]{:S(2)}, u32[]{:S(2)}) collective-permute-start(bf16[6,2,16,1152]{3,2,1,0:T(8,128)(2,1)} %get-tuple-element.46), channel_id=1, source_target_pairs={{0,8},{8,16},{16,24},{1,9},{9,17},{17,25},{2,10},{10,18},{18,26},{... | collective-permute-start | bytes 1327112 | tf_op jit(solution)/shard_map/ppermute | solution.py:534
  9.6 4.5 %collective-permute-start.3 = (bf16[4,9,4,16,128]{4,3,2,1,0:T(8,128)(2,1)}, bf16[4,9,4,16,128]{4,3,2,1,0:T(8,128)(2,1)S(1)}, u32[]{:S(2)}, u32[]{:S(2)}) collective-permute-start(bf16[4,9,4,16,128]{4,3,2,1,0:T(8,128)(2,1)} %get-tuple-element.52.raw_ref), channel_id=1, source_target_pairs={{0,6},{1,7},{2,4},{3,5},{4,2},{5,3},{6,0},{7,1},{8,14},{9,15},{10,... | collective-permute-start | bytes 1769480 | tf_op jit(solution)/shard_map/ppermute | solution.py:516
  14.1 1.3 %collective-permute-start.1 = (bf16[6,2,16,1152]{3,2,1,0:T(8,128)(2,1)}, bf16[6,2,16,1152]{3,2,1,0:T(8,128)(2,1)}, u32[]{:S(2)}, u32[]{:S(2)}) collective-permute-start(bf16[6,2,16,1152]{3,2,1,0:T(8,128)(2,1)} %get-tuple-element.47), channel_id=1, source_target_pairs={{8,0},{16,8},{24,16},{9,1},{17,9},{25,17},{10,2},{18,10},{26,18},{... | collective-permute-start | bytes 1327112 | tf_op jit(solution)/shard_map/ppermute | solution.py:535
  15.4 1.1 %copy-done = bf16[4,9,4,16,128]{4,3,2,1,0:T(8,128)(2,1)S(1)} copy-done((bf16[4,9,4,16,128]{4,3,2,1,0:T(8,128)(2,1)S(1)}, bf16[4,9,4,16,128]{4,3,2,1,0:T(8,128)(2,1)}, u32[]{:S(2)}) %copy-start) | copy-done | bytes 589848
  16.5 1.2 %half_slots.3 = (bf16[4,3,4,16,128]{4,3,2,1,0:T(8,128)(2,1)S(1)}, bf16[4,3,4,16,128]{4,3,2,1,0:T(8,128)(2,1)S(1)}, bf16[4,3,4,16,128]{4,3,2,1,0:T(8,128)(2,1)S(1)}, bf16[4,3,4,16,128]{4,3,2,1,0:T(8,128)(2,1)S(1)}) custom-call(s32[1,8]{1,0:T(1,128)S(1)} %copy-done.6, bf16[4,9,4,16,128]{4,3,2,1,0:T(8,128)(2,1)S(1)} %copy-done), custom_call_target="tpu_custom_call" | custom-call | flops 1 | bytes 1 | tf_op jit(solution)/shard_map/half_slots/pallas_call | solution.py:519
  17.7 1.6 %collective-permute-start.7 = (bf16[4,3,4,16,128]{4,3,2,1,0:T(8,128)(2,1)S(1)}, bf16[4,3,4,16,128]{4,3,2,1,0:T(8,128)(2,1)S(1)}, u32[]{:S(2)}, u32[]{:S(2)}) collective-permute-start(bf16[4,3,4,16,128]{4,3,2,1,0:T(8,128)(2,1)S(1)} %get-tuple-element.70), channel_id=1, source_target_pairs={{0,1},{1,0},{2,3},{3,2},{4,5},{5,4},{6,7},{7,6},{8,9},{9,8},{10,11... | collective-permute-start | bytes 589832 | tf_op jit(solution)/shard_map/ppermute | solution.py:516
  19.3 2.0 %collective-permute-start.9 = (bf16[4,3,4,16,128]{4,3,2,1,0:T(8,128)(2,1)S(1)}, bf16[4,3,4,16,128]{4,3,2,1,0:T(8,128)(2,1)S(1)}, u32[]{:S(2)}, u32[]{:S(2)}) collective-permute-start(bf16[4,3,4,16,128]{4,3,2,1,0:T(8,128)(2,1)S(1)} %get-tuple-element.72), channel_id=1, source_target_pairs={{0,3},{1,2},{2,1},{3,0},{4,7},{5,6},{6,5},{7,4},{8,11},{9,10},{10,... | collective-permute-start | bytes 589832 | tf_op jit(solution)/shard_map/ppermute | solution.py:516
  21.4 9.0 %edge_rows.1 = (bf16[4,3,4,16,128]{4,3,2,1,0:T(8,128)(2,1)}, bf16[4,3,4,16,128]{4,3,2,1,0:T(8,128)(2,1)}, bf16[4,3,4,16,128]{4,3,2,1,0:T(8,128)(2,1)}, bf16[4,3,...) custom-call(s32[1,8]{1,0:T(1,128)} %counts_ref.11, ...), custom_call_target="tpu_custom_call" | custom-call | flops 1 | bytes 1 | tf_op jit(solution)/shard_map/edge_rows/pallas_call | solution.py:538
  30.3 1.6 %collective-permute-start.2 = (bf16[4,3,4,16,128]{4,3,2,1,0:T(8,128)(2,1)}, bf16[4,3,4,16,128]{4,3,2,1,0:T(8,128)(2,1)S(1)}, u32[]{:S(2)}, u32[]{:S(2)}) collective-permute-start(bf16[4,3,4,16,128]{4,3,2,1,0:T(8,128)(2,1)} %get-tuple-element.49), channel_id=1, source_target_pairs={{0,1},{1,0},{2,3},{3,2},{4,5},{5,4},{6,7},{7,6},{8,9},{9,8},{10,11... | collective-permute-start | bytes 589832 | tf_op jit(solution)/shard_map/ppermute | solution.py:516
  32.7 5.5 %collective-permute-done.9.refs_3_ = bf16[4,3,4,16,128]{4,3,2,1,0:T(8,128)(2,1)S(1)} collective-permute-done((bf16[4,3,4,16,128]{4,3,2,1,0:T(8,128)(2,1)S(1)}, bf16[4,3,4,16,128]{4,3,2,1,0:T(8,128)(2,1)S(1)}, u32[]{:S(2)}, u32[]{:S(2)}) %collective-permute-start.9) | collective-permute-done | bytes 196640 | tf_op jit(solution)/shard_map/ppermute | solution.py:516
  38.2 1.6 %collective-permute-start.10 = (bf16[4,3,4,16,128]{4,3,2,1,0:T(8,128)(2,1)}, bf16[4,3,4,16,128]{4,3,2,1,0:T(8,128)(2,1)S(1)}, u32[]{:S(2)}, u32[]{:S(2)}) collective-permute-start(bf16[4,3,4,16,128]{4,3,2,1,0:T(8,128)(2,1)} %get-tuple-element.76), channel_id=1, source_target_pairs={{0,5},{1,4},{2,7},{3,6},{4,1},{5,0},{6,3},{7,2},{8,13},{9,12},{10,... | collective-permute-start | bytes 589832 | tf_op jit(solution)/shard_map/ppermute | solution.py:516
  39.8 1.2 %half_slots.2 = (bf16[4,3,4,16,128]{4,3,2,1,0:T(8,128)(2,1)S(1)}, bf16[4,3,4,16,128]{4,3,2,1,0:T(8,128)(2,1)S(1)}, bf16[4,3,4,16,128]{4,3,2,1,0:T(8,128)(2,1)S(1)}, bf16[4,3,4,16,128]{4,3,2,1,0:T(8,128)(2,1)S(1)}) custom-call(s32[1,8]{1,0:T(1,128)S(1)} %copy-done.7, bf16[4,9,4,16,128]{4,3,2,1,0:T(8,128)(2,1)S(1)} %collective-permute-done.3.raw_ref), custom_call_target="tpu_custom_call" | custom-call | flops 1 | bytes 1 | tf_op jit(solution)/shard_map/half_slots/pallas_call | solution.py:519
  41.0 2.6 %collective-permute-start.13 = (bf16[4,3,4,16,128]{4,3,2,1,0:T(8,128)(2,1)S(1)}, bf16[4,3,4,16,128]{4,3,2,1,0:T(8,128)(2,1)S(1)}, u32[]{:S(2)}, u32[]{:S(2)}) collective-permute-start(bf16[4,3,4,16,128]{4,3,2,1,0:T(8,128)(2,1)S(1)} %get-tuple-element.83), channel_id=1, source_target_pairs={{0,2},{1,3},{2,0},{3,1},{4,6},{5,7},{6,4},{7,5},{8,10},{9,11},{10,... | collective-permute-start | bytes 589832 | tf_op jit(solution)/shard_map/ppermute | solution.py:516
  45.1 1.4 %collective-permute-start.11 = (bf16[4,3,4,16,128]{4,3,2,1,0:T(8,128)(2,1)}, bf16[4,3,4,16,128]{4,3,2,1,0:T(8,128)(2,1)S(1)}, u32[]{:S(2)}, u32[]{:S(2)}) collective-permute-start(bf16[4,3,4,16,128]{4,3,2,1,0:T(8,128)(2,1)} %get-tuple-element.77), channel_id=1, source_target_pairs={{0,6},{1,7},{2,4},{3,5},{4,2},{5,3},{6,0},{7,1},{8,14},{9,15},{10,... | collective-permute-start | bytes 589832 | tf_op jit(solution)/shard_map/ppermute | solution.py:516
  46.6 5.7 %collective-permute-done.10.refs_5_ = bf16[4,3,4,16,128]{4,3,2,1,0:T(8,128)(2,1)S(1)} collective-permute-done((bf16[4,3,4,16,128]{4,3,2,1,0:T(8,128)(2,1)}, bf16[4,3,4,16,128]{4,3,2,1,0:T(8,128)(2,1)S(1)}, u32[]{:S(2)}, u32[]{:S(2)}) %collective-permute-start.10) | collective-permute-done | bytes 196640 | tf_op jit(solution)/shard_map/ppermute | solution.py:516
  52.2 2.0 %collective-permute-start.12 = (bf16[4,3,4,16,128]{4,3,2,1,0:T(8,128)(2,1)}, bf16[4,3,4,16,128]{4,3,2,1,0:T(8,128)(2,1)S(1)}, u32[]{:S(2)}, u32[]{:S(2)}) collective-permute-start(bf16[4,3,4,16,128]{4,3,2,1,0:T(8,128)(2,1)} %get-tuple-element.78), channel_id=1, source_target_pairs={{0,7},{1,6},{2,5},{3,4},{4,3},{5,2},{6,1},{7,0},{8,15},{9,14},{10,... | collective-permute-start | bytes 589832 | tf_op jit(solution)/shard_map/ppermute | solution.py:516
  54.2 2.6 %collective-permute-done.14.refs_5_ = bf16[4,3,4,16,128]{4,3,2,1,0:T(8,128)(2,1)S(1)} collective-permute-done((bf16[4,3,4,16,128]{4,3,2,1,0:T(8,128)(2,1)S(1)}, bf16[4,3,4,16,128]{4,3,2,1,0:T(8,128)(2,1)S(1)}, u32[]{:S(2)}, u32[]{:S(2)}) %collective-permute-start.14) | collective-permute-done | bytes 196640 | tf_op jit(solution)/shard_map/ppermute | solution.py:516
  56.9 1.3 %collective-permute-done.15.refs_7_ = bf16[4,3,4,16,128]{4,3,2,1,0:T(8,128)(2,1)S(1)} collective-permute-done((bf16[4,3,4,16,128]{4,3,2,1,0:T(8,128)(2,1)S(1)}, bf16[4,3,4,16,128]{4,3,2,1,0:T(8,128)(2,1)S(1)}, u32[]{:S(2)}, u32[]{:S(2)}) %collective-permute-start.15) | collective-permute-done | bytes 196640 | tf_op jit(solution)/shard_map/ppermute | solution.py:516
  58.7 5.8 %inner_columns.1.refs_8_ = bf16[4,512,384]{2,1,0:T(8,128)(2,1)S(1)} custom-call(s32[4,6]{1,0:T(4,128)S(1)} %copy-done.8, s32[1,8]{1,0:T(1,128)S(1)} %copy-done.7, bf16[4,3,4,16,128]{4,3,2,1,0:T(8,128)(2,1)S(1)} %get-tuple-element.79.refs_0_, bf16[4,3,4,16,128]{4,3,2,1,0:T(8,128)(2,1)S(1)} %collective-permute-done.7.refs_1_, ...), custom_call_target="tpu_custom_call" | custom-call | flops 1 | bytes 1 | tf_op jit(solution)/shard_map/inner_columns/pallas_call | solution.py:604
  64.5 1.0 %collective-permute-done.12.refs_7_ = bf16[4,3,4,16,128]{4,3,2,1,0:T(8,128)(2,1)S(1)} collective-permute-done((bf16[4,3,4,16,128]{4,3,2,1,0:T(8,128)(2,1)}, bf16[4,3,4,16,128]{4,3,2,1,0:T(8,128)(2,1)S(1)}, u32[]{:S(2)}, u32[]{:S(2)}) %collective-permute-start.12) | collective-permute-done | bytes 196640 | tf_op jit(solution)/shard_map/ppermute | solution.py:516
  65.5 10.1 %collective-permute-done.6.refs_4_ = bf16[4,3,4,16,128]{4,3,2,1,0:T(8,128)(2,1)S(1)} collective-permute-done((bf16[4,3,4,16,128]{4,3,2,1,0:T(8,128)(2,1)}, bf16[4,3,4,16,128]{4,3,2,1,0:T(8,128)(2,1)S(1)}, u32[]{:S(2)}, u32[]{:S(2)}) %collective-permute-start.6) | collective-permute-done | bytes 196640 | tf_op jit(solution)/shard_map/ppermute | solution.py:516
  75.6 2.2 %collective-permute-done.5.refs_3_ = bf16[4,3,4,16,128]{4,3,2,1,0:T(8,128)(2,1)S(1)} collective-permute-done((bf16[4,3,4,16,128]{4,3,2,1,0:T(8,128)(2,1)}, bf16[4,3,4,16,128]{4,3,2,1,0:T(8,128)(2,1)S(1)}, u32[]{:S(2)}, u32[]{:S(2)}) %collective-permute-start.5) | collective-permute-done | bytes 196640 | tf_op jit(solution)/shard_map/ppermute | solution.py:516
  77.8 7.5 %edge_columns.1 = bf16[512,8,384]{2,1,0:T(8,128)(2,1)} custom-call(s32[4,6]{1,0:T(4,128)S(1)} %copy-done.8, s32[1,8]{1,0:T(1,128)S(1)} %copy-done.7, bf16[4,3,4,16,128]{4,3,2,1,0:T(8,128)(2,1)S(1)} %copy-done.4, bf16[4,3,4,16,128]{4,3,2,1,0:T(8,128)(2,1)S(1)} %collective-permute-done.2.refs_1_, ...), custom_call_target="tpu_custom_call" | custom-call | flops 1 | bytes 1 | tf_op jit(solution)/shard_map/edge_columns/pallas_call | solution.py:615
  (35 shorter events, 3.0 us)
Async XLA Ops:
  0.0 15.4 %copy-start.6 = (s32[1,8]{1,0:T(1,128)S(1)}, s32[1,8]{1,0:T(1,128)}, u32[]{:S(2)}) copy-start(s32[1,8]{1,0:T(1,128)} %counts_ref.11) | copy-start | bytes 100
  7.2 12.0 %collective-permute-start = (bf16[6,2,16,1152]{3,2,1,0:T(8,128)(2,1)}, bf16[6,2,16,1152]{3,2,1,0:T(8,128)(2,1)S(1)}, u32[]{:S(2)}, u32[]{:S(2)}) collective-permute-start(bf16[6,2,16,1152]{3,2,1,0:T(8,128)(2,1)} %get-tuple-element.46), channel_id=1, source_target_pairs={{0,8},{8,16},{16,24},{1,9},{9,17},{17,25},{2,10},{10,18},{18,26},{... | collective-permute-start | bytes 1327112 | tf_op jit(solution)/shard_map/ppermute | solution.py:534
  9.6 30.2 %collective-permute-start.3 = (bf16[4,9,4,16,128]{4,3,2,1,0:T(8,128)(2,1)}, bf16[4,9,4,16,128]{4,3,2,1,0:T(8,128)(2,1)S(1)}, u32[]{:S(2)}, u32[]{:S(2)}) collective-permute-start(bf16[4,9,4,16,128]{4,3,2,1,0:T(8,128)(2,1)} %get-tuple-element.52.raw_ref), channel_id=1, source_target_pairs={{0,6},{1,7},{2,4},{3,5},{4,2},{5,3},{6,0},{7,1},{8,14},{9,15},{10,... | collective-permute-start | bytes 1769480 | tf_op jit(solution)/shard_map/ppermute | solution.py:516
  14.1 7.2 %collective-permute-start.1 = (bf16[6,2,16,1152]{3,2,1,0:T(8,128)(2,1)}, bf16[6,2,16,1152]{3,2,1,0:T(8,128)(2,1)}, u32[]{:S(2)}, u32[]{:S(2)}) collective-permute-start(bf16[6,2,16,1152]{3,2,1,0:T(8,128)(2,1)} %get-tuple-element.47), channel_id=1, source_target_pairs={{8,0},{16,8},{24,16},{9,1},{17,9},{25,17},{10,2},{18,10},{26,18},{... | collective-permute-start | bytes 1327112 | tf_op jit(solution)/shard_map/ppermute | solution.py:535
  17.7 14.2 %copy-start.1 = (bf16[512,512]{1,0:T(8,128)(2,1)S(1)}, bf16[512,512]{1,0:T(8,128)(2,1)}, u32[]{:S(2)}) copy-start(bf16[512,512]{1,0:T(8,128)(2,1)} %refs_0_) | copy-start | bytes 1572868
  17.7 14.2 %copy-start.2 = (bf16[512,512]{1,0:T(8,128)(2,1)S(1)}, bf16[512,512]{1,0:T(8,128)(2,1)}, u32[]{:S(2)}) copy-start(bf16[512,512]{1,0:T(8,128)(2,1)} %refs_1_) | copy-start | bytes 1572868
  17.7 14.2 %copy-start.3 = (bf16[512,512]{1,0:T(8,128)(2,1)S(1)}, bf16[512,512]{1,0:T(8,128)(2,1)}, u32[]{:S(2)}) copy-start(bf16[512,512]{1,0:T(8,128)(2,1)} %refs_2_) | copy-start | bytes 1572868
  17.7 14.7 %collective-permute-start.7 = (bf16[4,3,4,16,128]{4,3,2,1,0:T(8,128)(2,1)S(1)}, bf16[4,3,4,16,128]{4,3,2,1,0:T(8,128)(2,1)S(1)}, u32[]{:S(2)}, u32[]{:S(2)}) collective-permute-start(bf16[4,3,4,16,128]{4,3,2,1,0:T(8,128)(2,1)S(1)} %get-tuple-element.70), channel_id=1, source_target_pairs={{0,1},{1,0},{2,3},{3,2},{4,5},{5,4},{6,7},{7,6},{8,9},{9,8},{10,11... | collective-permute-start | bytes 589832 | tf_op jit(solution)/shard_map/ppermute | solution.py:516
  19.3 13.5 %collective-permute-start.8 = (bf16[4,3,4,16,128]{4,3,2,1,0:T(8,128)(2,1)S(1)}, bf16[4,3,4,16,128]{4,3,2,1,0:T(8,128)(2,1)S(1)}, u32[]{:S(2)}, u32[]{:S(2)}) collective-permute-start(bf16[4,3,4,16,128]{4,3,2,1,0:T(8,128)(2,1)S(1)} %get-tuple-element.71), channel_id=1, source_target_pairs={{0,2},{1,3},{2,0},{3,1},{4,6},{5,7},{6,4},{7,5},{8,10},{9,11},{10,... | collective-permute-start | bytes 589832 | tf_op jit(solution)/shard_map/ppermute | solution.py:516
  19.3 20.5 %copy-start.7 = (s32[1,8]{1,0:T(1,128)S(1)}, s32[1,8]{1,0:T(1,128)}, u32[]{:S(2)}) copy-start(s32[1,8]{1,0:T(1,128)} %counts_ref.11) | copy-start | bytes 100
  19.3 39.4 %copy-start.5 = (bf16[128,128]{1,0:T(8,128)(2,1)S(1)}, bf16[128,128]{1,0:T(8,128)(2,1)}, u32[]{:S(2)}) copy-start(bf16[128,128]{1,0:T(8,128)(2,1)} %refs_9_.1) | copy-start | bytes 98308
  19.3 39.4 %copy-start.8 = (s32[4,6]{1,0:T(4,128)S(1)}, s32[4,6]{1,0:T(4,128)}, u32[]{:S(2)}) copy-start(s32[4,6]{1,0:T(4,128)} %groups_ref.3) | copy-start | bytes 292
  19.3 18.9 %collective-permute-start.9 = (bf16[4,3,4,16,128]{4,3,2,1,0:T(8,128)(2,1)S(1)}, bf16[4,3,4,16,128]{4,3,2,1,0:T(8,128)(2,1)S(1)}, u32[]{:S(2)}, u32[]{:S(2)}) collective-permute-start(bf16[4,3,4,16,128]{4,3,2,1,0:T(8,128)(2,1)S(1)} %get-tuple-element.72), channel_id=1, source_target_pairs={{0,3},{1,2},{2,1},{3,0},{4,7},{5,6},{6,5},{7,4},{8,11},{9,10},{10,... | collective-permute-start | bytes 589832 | tf_op jit(solution)/shard_map/ppermute | solution.py:516
  30.3 14.8 %collective-permute-start.2 = (bf16[4,3,4,16,128]{4,3,2,1,0:T(8,128)(2,1)}, bf16[4,3,4,16,128]{4,3,2,1,0:T(8,128)(2,1)S(1)}, u32[]{:S(2)}, u32[]{:S(2)}) collective-permute-start(bf16[4,3,4,16,128]{4,3,2,1,0:T(8,128)(2,1)} %get-tuple-element.49), channel_id=1, source_target_pairs={{0,1},{1,0},{2,3},{3,2},{4,5},{5,4},{6,7},{7,6},{8,9},{9,8},{10,11... | collective-permute-start | bytes 589832 | tf_op jit(solution)/shard_map/ppermute | solution.py:516
  38.2 14.0 %collective-permute-start.10 = (bf16[4,3,4,16,128]{4,3,2,1,0:T(8,128)(2,1)}, bf16[4,3,4,16,128]{4,3,2,1,0:T(8,128)(2,1)S(1)}, u32[]{:S(2)}, u32[]{:S(2)}) collective-permute-start(bf16[4,3,4,16,128]{4,3,2,1,0:T(8,128)(2,1)} %get-tuple-element.76), channel_id=1, source_target_pairs={{0,5},{1,4},{2,7},{3,6},{4,1},{5,0},{6,3},{7,2},{8,13},{9,12},{10,... | collective-permute-start | bytes 589832 | tf_op jit(solution)/shard_map/ppermute | solution.py:516
  41.0 13.2 %collective-permute-start.13 = (bf16[4,3,4,16,128]{4,3,2,1,0:T(8,128)(2,1)S(1)}, bf16[4,3,4,16,128]{4,3,2,1,0:T(8,128)(2,1)S(1)}, u32[]{:S(2)}, u32[]{:S(2)}) collective-permute-start(bf16[4,3,4,16,128]{4,3,2,1,0:T(8,128)(2,1)S(1)} %get-tuple-element.83), channel_id=1, source_target_pairs={{0,2},{1,3},{2,0},{3,1},{4,6},{5,7},{6,4},{7,5},{8,10},{9,11},{10,... | collective-permute-start | bytes 589832 | tf_op jit(solution)/shard_map/ppermute | solution.py:516
  43.6 13.3 %collective-permute-start.14 = (bf16[4,3,4,16,128]{4,3,2,1,0:T(8,128)(2,1)S(1)}, bf16[4,3,4,16,128]{4,3,2,1,0:T(8,128)(2,1)S(1)}, u32[]{:S(2)}, u32[]{:S(2)}) collective-permute-start(bf16[4,3,4,16,128]{4,3,2,1,0:T(8,128)(2,1)S(1)} %get-tuple-element.84), channel_id=1, source_target_pairs={{0,3},{1,2},{2,1},{3,0},{4,7},{5,6},{6,5},{7,4},{8,11},{9,10},{10,... | collective-permute-start | bytes 589832 | tf_op jit(solution)/shard_map/ppermute | solution.py:516
  44.6 13.6 %collective-permute-start.15 = (bf16[4,3,4,16,128]{4,3,2,1,0:T(8,128)(2,1)S(1)}, bf16[4,3,4,16,128]{4,3,2,1,0:T(8,128)(2,1)S(1)}, u32[]{:S(2)}, u32[]{:S(2)}) collective-permute-start(bf16[4,3,4,16,128]{4,3,2,1,0:T(8,128)(2,1)S(1)} %get-tuple-element.86), channel_id=1, source_target_pairs={{0,1},{1,0},{2,3},{3,2},{4,5},{5,4},{6,7},{7,6},{8,9},{9,8},{10,11... | collective-permute-start | bytes 589832 | tf_op jit(solution)/shard_map/ppermute | solution.py:516
  45.1 19.3 %collective-permute-start.11 = (bf16[4,3,4,16,128]{4,3,2,1,0:T(8,128)(2,1)}, bf16[4,3,4,16,128]{4,3,2,1,0:T(8,128)(2,1)S(1)}, u32[]{:S(2)}, u32[]{:S(2)}) collective-permute-start(bf16[4,3,4,16,128]{4,3,2,1,0:T(8,128)(2,1)} %get-tuple-element.77), channel_id=1, source_target_pairs={{0,6},{1,7},{2,4},{3,5},{4,2},{5,3},{6,0},{7,1},{8,14},{9,15},{10,... | collective-permute-start | bytes 589832 | tf_op jit(solution)/shard_map/ppermute | solution.py:516
  52.2 13.2 %collective-permute-start.12 = (bf16[4,3,4,16,128]{4,3,2,1,0:T(8,128)(2,1)}, bf16[4,3,4,16,128]{4,3,2,1,0:T(8,128)(2,1)S(1)}, u32[]{:S(2)}, u32[]{:S(2)}) collective-permute-start(bf16[4,3,4,16,128]{4,3,2,1,0:T(8,128)(2,1)} %get-tuple-element.78), channel_id=1, source_target_pairs={{0,7},{1,6},{2,5},{3,4},{4,3},{5,2},{6,1},{7,0},{8,15},{9,14},{10,... | collective-permute-start | bytes 589832 | tf_op jit(solution)/shard_map/ppermute | solution.py:516
  54.2 21.3 %collective-permute-start.6 = (bf16[4,3,4,16,128]{4,3,2,1,0:T(8,128)(2,1)}, bf16[4,3,4,16,128]{4,3,2,1,0:T(8,128)(2,1)S(1)}, u32[]{:S(2)}, u32[]{:S(2)}) collective-permute-start(bf16[4,3,4,16,128]{4,3,2,1,0:T(8,128)(2,1)} %get-tuple-element.69), channel_id=1, source_target_pairs={{0,4},{1,5},{2,6},{3,7},{4,0},{5,1},{6,2},{7,3},{8,12},{9,13},{10,... | collective-permute-start | bytes 589832 | tf_op jit(solution)/shard_map/ppermute | solution.py:516
  56.9 18.7 %collective-permute-start.4 = (bf16[4,3,4,16,128]{4,3,2,1,0:T(8,128)(2,1)}, bf16[4,3,4,16,128]{4,3,2,1,0:T(8,128)(2,1)S(1)}, u32[]{:S(2)}, u32[]{:S(2)}) collective-permute-start(bf16[4,3,4,16,128]{4,3,2,1,0:T(8,128)(2,1)} %get-tuple-element.57), channel_id=1, source_target_pairs={{0,2},{1,3},{2,0},{3,1},{4,6},{5,7},{6,4},{7,5},{8,10},{9,11},{10,... | collective-permute-start | bytes 589832 | tf_op jit(solution)/shard_map/ppermute | solution.py:516
  58.1 19.6 %collective-permute-start.5 = (bf16[4,3,4,16,128]{4,3,2,1,0:T(8,128)(2,1)}, bf16[4,3,4,16,128]{4,3,2,1,0:T(8,128)(2,1)S(1)}, u32[]{:S(2)}, u32[]{:S(2)}) collective-permute-start(bf16[4,3,4,16,128]{4,3,2,1,0:T(8,128)(2,1)} %get-tuple-element.58), channel_id=1, source_target_pairs={{0,3},{1,2},{2,1},{3,0},{4,7},{5,6},{6,5},{7,4},{8,11},{9,10},{10,... | collective-permute-start | bytes 589832 | tf_op jit(solution)/shard_map/ppermute | solution.py:516
  58.7 19.1 %copy-start.4 = (bf16[4,3,4,16,128]{4,3,2,1,0:T(8,128)(2,1)S(1)}, bf16[4,3,4,16,128]{4,3,2,1,0:T(8,128)(2,1)}, u32[]{:S(2)}) copy-start(bf16[4,3,4,16,128]{4,3,2,1,0:T(8,128)(2,1)} %get-tuple-element.48.refs_0_) | copy-start | bytes 589828
  (2 other events, 3.2 us)
